TPU v7x, 32 devices: a whole 2x2x4 slice. The times are simulated.
32 devices in a mesh: section: 4 (over z), expert: 8 (over y, x, core).
Axes of the slice: x: 2, y: 2, z: 4, core: 2. Of those that a mesh axis runs over, the one named last changes fastest.
Arguments:
- tokens: bfloat16 [10240, 768], P(('section', 'expert')), may hold values from -6 to 6
- gate_prob: float32 [10240], P(('section', 'expert')), may hold values from 0.1 to 1
- routing: int32 [10240, 1], P(('section', 'expert')), may hold values from 0 to 7; in each aligned block of 320 rows (0 to 319, 320 to 639, ...) at most 80 rows name the same one
- up_weight: bfloat16 [32, 768, 512], P(('section', 'expert')), may hold values from -0.21875 to 0.21875
- down_weight: bfloat16 [32, 512, 768], P(('section', 'expert')), may hold values from -0.1875 to 0.1875
- cotangent: bfloat16 [10240, 768], P(('section', 'expert')), may hold values from -6 to 6
Outputs:
- mixed: bfloat16 [10240, 768], P(('section', 'expert'))
- token_grad: bfloat16 [10240, 768], P(('section', 'expert'))
- grad_up: bfloat16 [32, 768, 512], P(('section', 'expert'))
- grad_down: bfloat16 [32, 512, 768], P(('section', 'expert'))
Inputs may be any that keep to these rules, and one draw needn't show every extreme that they name: `routing`: at most 80 of one device's 320 tokens name the same expert, and in every draw some device's tokens name one expert exactly 80 times.
All inputs are finite; a program needn't handle non-finite values.
Results may differ from a plain program's by a relative error of at most 0.0065.
Values may be sent and summed in bfloat16 or wider, within the bound.
No kernel may reach another device: no remote copies, remote signals or barrier semaphores. Data moves between devices by JAX's collectives and lax.ppermute only.
A program may use at most 64 MiB of HBM per device.

v0:
```python
import jax
import jax.numpy as jnp
from jax import lax
from jax.sharding import PartitionSpec as P


def swapped(array, axis, bit):
    return lax.ppermute(array, axis, [(i, i ^ 1 << bit) for i in range(lax.axis_size(axis))])


def gelu_value(preact):
    inner = 0.7978845608 * (preact + 0.044715 * preact * preact * preact)
    return 0.5 * preact * (1.0 + jnp.tanh(inner))


def gelu_slope(preact):
    inner = 0.7978845608 * (preact + 0.044715 * preact * preact * preact)
    tangent = jnp.tanh(inner)
    return 0.5 * (1.0 + tangent) + 0.5 * preact * (1.0 - tangent * tangent) * 0.7978845608 * (
        1.0 + 0.134145 * preact * preact
    )


def slot_table(routing, experts, capacity):
    choose = (routing == jnp.arange(experts, dtype=jnp.int32)[None, :]).astype(jnp.int32)
    running = jnp.cumsum(choose, axis=0)
    ranking = jnp.sum(running * choose, axis=1) - 1
    position = routing[:, 0] * capacity + ranking
    return (position[None, :] == jnp.arange(experts * capacity, dtype=jnp.int32)[:, None]).astype(
        jnp.bfloat16
    )


def shards(tokens, gate_prob, routing, up_weight, down_weight, cotangent):
    experts = lax.axis_size("expert")
    sections = lax.axis_size("section")
    local_tokens = tokens.shape[0]
    capacity = 2 * local_tokens // experts
    half_ff = up_weight.shape[2]
    top_bit = sections.bit_length() - 2
    upper_half = lax.axis_index("section") >= sections // 2
    placing = slot_table(routing, experts, capacity)
    scaled = (gate_prob[:, None] * cotangent.astype(jnp.float32)).astype(jnp.bfloat16)
    send_tokens = jnp.dot(placing, tokens, preferred_element_type=jnp.float32).astype(jnp.bfloat16)
    send_grads = jnp.dot(placing, scaled, preferred_element_type=jnp.float32).astype(jnp.bfloat16)
    token_rows, grad_rows = (
        lax.all_to_all(send_tokens, "expert", split_axis=0, concat_axis=0, tiled=True),
        lax.all_to_all(send_grads, "expert", split_axis=0, concat_axis=0, tiled=True),
    )
    own_up = up_weight[0]
    own_down = down_weight[0]
    other_up, other_down = swapped((own_up, own_down), "section", top_bit)
    w_up = jnp.where(
        upper_half,
        jnp.concatenate([other_up, own_up], axis=1),
        jnp.concatenate([own_up, other_up], axis=1),
    )
    w_down = jnp.where(
        upper_half,
        jnp.concatenate([other_down, own_down], axis=0),
        jnp.concatenate([own_down, other_down], axis=0),
    )
    preact = jnp.dot(token_rows, w_up, preferred_element_type=jnp.float32)
    hidden = gelu_value(preact).astype(jnp.bfloat16)
    output_rows = jnp.dot(hidden, w_down, preferred_element_type=jnp.float32).astype(jnp.bfloat16)
    through = jnp.dot(grad_rows, w_down.T, preferred_element_type=jnp.float32)
    hidden_grad = (through * gelu_slope(preact)).astype(jnp.bfloat16)
    input_grad = jnp.dot(hidden_grad, w_up.T, preferred_element_type=jnp.float32).astype(
        jnp.bfloat16
    )
    part_up = jnp.dot(token_rows.T, hidden_grad, preferred_element_type=jnp.float32)
    part_down = jnp.dot(hidden.T, grad_rows, preferred_element_type=jnp.float32)
    mine_start = jnp.where(upper_half, half_ff, 0)
    their_start = half_ff - mine_start
    keep_up = lax.dynamic_slice_in_dim(part_up, mine_start, half_ff, 1)
    give_up = lax.dynamic_slice_in_dim(part_up, their_start, half_ff, 1)
    keep_down = lax.dynamic_slice_in_dim(part_down, mine_start, half_ff, 0)
    give_down = lax.dynamic_slice_in_dim(part_down, their_start, half_ff, 0)
    peer_up, peer_down = (
        swapped(give_up.astype(jnp.bfloat16), "section", top_bit).astype(give_up.dtype),
        swapped(give_down.astype(jnp.bfloat16), "section", top_bit).astype(give_down.dtype),
    )
    grad_up = (keep_up + peer_up).astype(jnp.bfloat16)
    grad_down = (keep_down + peer_down).astype(jnp.bfloat16)
    back_out, back_grad = (
        lax.all_to_all(output_rows, "expert", split_axis=0, concat_axis=0, tiled=True),
        lax.all_to_all(input_grad, "expert", split_axis=0, concat_axis=0, tiled=True),
    )
    picked = jnp.dot(placing.T, back_out, preferred_element_type=jnp.float32)
    mixed = (gate_prob[:, None] * picked).astype(jnp.bfloat16)
    token_grad = jnp.dot(placing.T, back_grad, preferred_element_type=jnp.float32).astype(
        jnp.bfloat16
    )
    return (mixed, token_grad, grad_up[None], grad_down[None])


def solution(mesh):
    in_specs = (
        P(("section", "expert"), None),
        P(("section", "expert")),
        P(("section", "expert"), None),
        P(("section", "expert"), None, None),
        P(("section", "expert"), None, None),
        P(("section", "expert"), None),
    )
    out_specs = (
        P(("section", "expert"), None),
        P(("section", "expert"), None),
        P(("section", "expert"), None, None),
        P(("section", "expert"), None, None),
    )
    return jax.shard_map(shards, mesh=mesh, in_specs=in_specs, out_specs=out_specs, check_vma=False)
```

profile of v0, /device:TPU:0, one launch (start us, length us, event | category | flops | bytes accessed | tf_op | source)
XLA Modules:
  0.0 175.4 jit_solution(14335980273915898616)
XLA Ops:
  0.6 0.0 copy-start
  0.6 0.0 copy-start.4
  0.7 0.0 copy-start.6
  0.7 0.0 copy-start.5
  0.7 0.8 reduce
  1.5 0.9 reduce-window.6
  2.4 0.2 slice_reduce_fusion
  2.6 0.1 add_bitcast_fusion
  2.8 0.0 copy-done
  2.8 1.6 convolution_convert_fusion.3
  4.4 5.2 %all-to-all-start = ((bf16[8,80,768]{2,1,0:T(8,128)(2,1)}), bf16[8,80,768]{2,1,0:T(8,128)(2,1)S(1)}, u32[]{:S(2)}, u32[]{:S(2)}) async-start(bf16[8,80,768]{2,1,0:T(8,128)(2,1)} %bitcast.3), calls=%async_computation | async-start | bytes 1966080 | tf_op jit(solution)/shard_map/all_to_all | solution.py:47
  9.6 2.6 %collective-permute-start = (bf16[768,512]{1,0:T(8,128)(2,1)}, bf16[768,512]{1,0:T(8,128)(2,1)}, u32[]{:S(2)}, u32[]{:S(2)}) collective-permute-start(bf16[768,512]{1,0:T(8,128)(2,1)} %bitcast.5), channel_id=1, source_target_pairs={{0,16},{8,24},{16,0},{24,8},{1,17},{9,25},{17,1},{25,9},{2,18},{10... | collective-permute-start | bytes 2359304 | tf_op jit(solution)/shard_map/ppermute | solution.py:8
  12.2 0.0 copy-done.4
  12.2 0.3 collective-permute-start.1
  12.5 0.0 copy-done.6
  12.5 0.0 copy-done.5
  12.5 1.8 %convolution_convert_fusion.1 = bf16[640,768]{1,0:T(8,128)(2,1)} fusion(bf16[320,768]{1,0:T(8,128)(2,1)S(1)} %copy-done.5, s32[320]{0:T(512)S(1)} %add_add_fusion, f32[320]{0:T(512)S(1)} %copy-done.6), kind=kOutput, calls=%fused_computation.17 | convolution fusion | flops 316006400 | bytes 1477120 | tf_op jit(solution)/shard_map/dot_general | solution.py:45
  14.3 10.0 %all-to-all-done = bf16[8,80,768]{2,1,0:T(8,128)(2,1)S(1)} async-done(((bf16[8,80,768]{2,1,0:T(8,128)(2,1)}), bf16[8,80,768]{2,1,0:T(8,128)(2,1)S(1)}, u32[]{:S(2)}, u32[]{:S(2)}) %all-to-all-start) | async-done | bytes 983072 | tf_op jit(solution)/shard_map/all_to_all | solution.py:47
  24.3 3.6 %all-to-all-start.2 = ((bf16[8,80,768]{2,1,0:T(8,128)(2,1)}), bf16[8,80,768]{2,1,0:T(8,128)(2,1)S(1)}, u32[]{:S(2)}, u32[]{:S(2)}) async-start(bf16[8,80,768]{2,1,0:T(8,128)(2,1)} %bitcast.9), calls=%async_computation.2 | async-start | bytes 1966080 | tf_op jit(solution)/shard_map/all_to_all | solution.py:48
  27.8 37.0 %collective-permute-done = bf16[768,512]{1,0:T(8,128)(2,1)} collective-permute-done((bf16[768,512]{1,0:T(8,128)(2,1)}, bf16[768,512]{1,0:T(8,128)(2,1)}, u32[]{:S(2)}, u32[]{:S(2)}) %collective-permute-start) | collective-permute-done | bytes 786464 | tf_op jit(solution)/shard_map/ppermute | solution.py:8
  64.8 4.7 %fusion.15 = f32[640,1024]{1,0:T(8,128)} fusion(bf16[640,768]{1,0:T(8,128)(2,1)S(1)} %bitcast.30, bf16[768,512]{1,0:T(8,128)(2,1)} %bitcast.5, bf16[768,512]{1,0:T(8,128)(2,1)} %collective-permute-done, pred[]{:T(512)S(6)} %ge.3), kind=kOutput, calls=%fused_computation.32 | convolution fusion | flops 1013710848 | bytes 5177345 | tf_op jit(solution)/shard_map/dot_general | solution.py:63
  69.5 11.8 %collective-permute-done.1 = bf16[512,768]{1,0:T(8,128)(2,1)} collective-permute-done((bf16[512,768]{1,0:T(8,128)(2,1)S(1)}, bf16[512,768]{1,0:T(8,128)(2,1)}, u32[]{:S(2)}, u32[]{:S(2)}) %collective-permute-start.1) | collective-permute-done | bytes 786464 | tf_op jit(solution)/shard_map/ppermute | solution.py:8
  81.3 5.0 %convolution_convert_fusion.2 = bf16[640,768]{1,0:T(8,128)(2,1)} fusion(bf16[512,768]{1,0:T(8,128)(2,1)S(1)} %bitcast.40, bf16[512,768]{1,0:T(8,128)(2,1)} %collective-permute-done.1, pred[]{:T(512)S(6)} %ge.3, f32[640,1024]{1,0:T(8,128)} %fusion.15), kind=kOutput, calls=%fused_computation.18 | convolution fusion | flops 1020100608 | bytes 5177345 | tf_op jit(solution)/shard_map/dot_general | solution.py:65
  86.3 0.0 all-to-all-done.2
  86.3 3.8 %all-to-all-start.1 = ((bf16[8,80,768]{2,1,0:T(8,128)(2,1)}), bf16[8,80,768]{2,1,0:T(8,128)(2,1)S(1)}, u32[]{:S(2)}, u32[]{:S(2)}) async-start(bf16[8,80,768]{2,1,0:T(8,128)(2,1)} %bitcast.35), calls=%async_computation.1 | async-start | bytes 1966080 | tf_op jit(solution)/shard_map/all_to_all | solution.py:86
  90.1 5.2 %fusion.6 = bf16[640,1024]{1,0:T(8,128)(2,1)S(1)} fusion(f32[640,1024]{1,0:T(8,128)} %fusion.15, bf16[640,768]{1,0:T(8,128)(2,1)S(1)} %bitcast.33, bf16[512,768]{1,0:T(8,128)(2,1)} %bitcast.38, bf16[512,768]{1,0:T(8,128)(2,1)} %collective-permute-done.1, pred[]{:T(512)S(6)} %ge.3), kind=kOutput, calls=%fused_computation.8 | convolution fusion | flops 1026162688 | bytes 6488065 | tf_op jit(solution)/shard_map/dot_general | solution.py:66
  95.3 1.4 fusion.22
  96.8 0.0 copy-start.3
  96.8 1.2 dynamic-slice_convert_fusion.1
  98.0 0.7 copy-done.3
  98.7 0.0 collective-permute-start.2
  98.7 3.6 %fusion.21 = f32[1024,768]{1,0:T(8,128)S(1)} fusion(bf16[640,768]{1,0:T(8,128)(2,1)S(1)} %bitcast.34, f32[640,1024]{1,0:T(8,128)} %fusion.15), kind=kOutput, calls=%fused_computation.45 | convolution fusion | flops 1012531200 | bytes 6750208 | tf_op jit(solution)/shard_map/dot_general | solution.py:72
  102.2 0.0 copy-start.1
  102.2 1.7 copy-done.1
  103.9 0.1 dynamic-slice_convert_fusion
  104.0 3.0 %collective-permute-start.3 = (bf16[512,768]{1,0:T(8,128)(2,1)S(1)}, bf16[512,768]{1,0:T(8,128)(2,1)}, u32[]{:S(2)}, u32[]{:S(2)}) collective-permute-start(bf16[512,768]{1,0:T(8,128)(2,1)S(1)} %dynamic-slice_convert_fusion), channel_id=1, source_target_pairs={{0,16},{8,24},{16,0},{24,8},{1,17},{9,25},{17,1},{25,9},{2,18},{10... | collective-permute-start | bytes 2359304 | tf_op jit(solution)/shard_map/ppermute | solution.py:8
  107.0 4.1 %convolution_convert_fusion = bf16[640,768]{1,0:T(8,128)(2,1)} fusion(bf16[640,1024]{1,0:T(8,128)(2,1)S(1)} %fusion.6, bf16[768,512]{1,0:T(8,128)(2,1)} %bitcast.5, bf16[768,512]{1,0:T(8,128)(2,1)} %collective-permute-done, pred[]{:T(512)S(6)} %ge.3), kind=kOutput, calls=%fused_computation.16 | convolution fusion | flops 1014202368 | bytes 3866625 | tf_op jit(solution)/shard_map/dot_general | solution.py:68
  111.1 0.0 all-to-all-done.1
  111.1 4.2 %all-to-all-start.3 = ((bf16[8,80,768]{2,1,0:T(8,128)(2,1)}), bf16[8,80,768]{2,1,0:T(8,128)(2,1)S(1)}, u32[]{:S(2)}, u32[]{:S(2)}) async-start(bf16[8,80,768]{2,1,0:T(8,128)(2,1)} %bitcast.11), calls=%async_computation.3 | async-start | bytes 1966080 | tf_op jit(solution)/shard_map/all_to_all | solution.py:87
  115.3 0.0 copy-start.2
  115.3 38.6 %collective-permute-done.2 = bf16[768,512]{1,0:T(8,128)(2,1)} collective-permute-done((bf16[768,512]{1,0:T(8,128)(2,1)}, bf16[768,512]{1,0:T(8,128)(2,1)}, u32[]{:S(2)}, u32[]{:S(2)}) %collective-permute-start.2) | collective-permute-done | bytes 786464 | tf_op jit(solution)/shard_map/ppermute | solution.py:8
  153.9 2.8 %fusion.8 = bf16[1,768,512]{2,1,0:T(8,128)(2,1)} fusion(bf16[768,512]{1,0:T(8,128)(2,1)} %collective-permute-done.2, f32[768,1024]{1,0:T(8,128)} %copy-done.3, s32[]{:T(128)S(6)} %select_n.30), kind=kLoop, calls=%fused_computation.25 | loop fusion | flops 1179648 | bytes 3145732 | tf_op jit(solution)/shard_map/broadcast_in_dim | solution.py:94
  156.7 13.7 %collective-permute-done.3 = bf16[512,768]{1,0:T(8,128)(2,1)} collective-permute-done((bf16[512,768]{1,0:T(8,128)(2,1)S(1)}, bf16[512,768]{1,0:T(8,128)(2,1)}, u32[]{:S(2)}, u32[]{:S(2)}) %collective-permute-start.3) | collective-permute-done | bytes 786464 | tf_op jit(solution)/shard_map/ppermute | solution.py:8
  170.4 0.0 copy-done.2
  170.4 2.2 %fusion.9 = bf16[1,512,768]{2,1,0:T(8,128)(2,1)} fusion(bf16[512,768]{1,0:T(8,128)(2,1)} %collective-permute-done.3, f32[1024,768]{1,0:T(8,128)S(1)} %copy-done.2, s32[]{:T(128)S(6)} %select_n.30), kind=kLoop, calls=%fused_computation.26 | loop fusion | flops 1179648 | bytes 3145732 | tf_op jit(solution)/shard_map/broadcast_in_dim | solution.py:94
  172.6 1.4 fusion.7
  174.0 0.0 all-to-all-done.3
  174.0 1.4 convolution_convert_fusion.4
  (5 shorter events, 0.1 us)
Async XLA Ops:
  0.6 2.1 %copy-start = (bf16[320,768]{1,0:T(8,128)(2,1)S(1)}, bf16[320,768]{1,0:T(8,128)(2,1)}, u32[]{:S(2)}) copy-start(bf16[320,768]{1,0:T(8,128)(2,1)} %param.6) | copy-start | bytes 1474564
  0.6 11.5 %copy-start.4 = (bf16[1,512,768]{2,1,0:T(8,128)(2,1)S(1)}, bf16[1,512,768]{2,1,0:T(8,128)(2,1)}, u32[]{:S(2)}) copy-start(bf16[1,512,768]{2,1,0:T(8,128)(2,1)} %param.10) | copy-start | bytes 2359300
  0.7 11.8 %copy-start.6 = (f32[320]{0:T(512)S(1)}, f32[320]{0:T(512)}, u32[]{:S(2)}) copy-start(f32[320]{0:T(512)} %param.7) | copy-start | bytes 3844
  0.7 11.8 %copy-start.5 = (bf16[320,768]{1,0:T(8,128)(2,1)S(1)}, bf16[320,768]{1,0:T(8,128)(2,1)}, u32[]{:S(2)}) copy-start(bf16[320,768]{1,0:T(8,128)(2,1)} %param.11) | copy-start | bytes 1474564
  4.4 19.9 %all-to-all-start = ((bf16[8,80,768]{2,1,0:T(8,128)(2,1)}), bf16[8,80,768]{2,1,0:T(8,128)(2,1)S(1)}, u32[]{:S(2)}, u32[]{:S(2)}) async-start(bf16[8,80,768]{2,1,0:T(8,128)(2,1)} %bitcast.3), calls=%async_computation | async-start | bytes 1966080 | tf_op jit(solution)/shard_map/all_to_all | solution.py:47
  9.6 55.3 %collective-permute-start = (bf16[768,512]{1,0:T(8,128)(2,1)}, bf16[768,512]{1,0:T(8,128)(2,1)}, u32[]{:S(2)}, u32[]{:S(2)}) collective-permute-start(bf16[768,512]{1,0:T(8,128)(2,1)} %bitcast.5), channel_id=1, source_target_pairs={{0,16},{8,24},{16,0},{24,8},{1,17},{9,25},{17,1},{25,9},{2,18},{10... | collective-permute-start | bytes 2359304 | tf_op jit(solution)/shard_map/ppermute | solution.py:8
  12.2 69.1 %collective-permute-start.1 = (bf16[512,768]{1,0:T(8,128)(2,1)S(1)}, bf16[512,768]{1,0:T(8,128)(2,1)}, u32[]{:S(2)}, u32[]{:S(2)}) collective-permute-start(bf16[512,768]{1,0:T(8,128)(2,1)S(1)} %bitcast.39), channel_id=1, source_target_pairs={{0,16},{8,24},{16,0},{24,8},{1,17},{9,25},{17,1},{25,9},{2,18},{10... | collective-permute-start | bytes 2359304 | tf_op jit(solution)/shard_map/ppermute | solution.py:8
  24.3 62.0 %all-to-all-start.2 = ((bf16[8,80,768]{2,1,0:T(8,128)(2,1)}), bf16[8,80,768]{2,1,0:T(8,128)(2,1)S(1)}, u32[]{:S(2)}, u32[]{:S(2)}) async-start(bf16[8,80,768]{2,1,0:T(8,128)(2,1)} %bitcast.9), calls=%async_computation.2 | async-start | bytes 1966080 | tf_op jit(solution)/shard_map/all_to_all | solution.py:48
  86.3 24.8 %all-to-all-start.1 = ((bf16[8,80,768]{2,1,0:T(8,128)(2,1)}), bf16[8,80,768]{2,1,0:T(8,128)(2,1)S(1)}, u32[]{:S(2)}, u32[]{:S(2)}) async-start(bf16[8,80,768]{2,1,0:T(8,128)(2,1)} %bitcast.35), calls=%async_computation.1 | async-start | bytes 1966080 | tf_op jit(solution)/shard_map/all_to_all | solution.py:86
  96.8 1.9 %copy-start.3 = (f32[768,1024]{1,0:T(8,128)}, f32[768,1024]{1,0:T(8,128)S(1)}, u32[]{:S(2)}) copy-start(f32[768,1024]{1,0:T(8,128)S(1)} %fusion.22) | copy-start | bytes 9437188
  98.7 55.3 %collective-permute-start.2 = (bf16[768,512]{1,0:T(8,128)(2,1)}, bf16[768,512]{1,0:T(8,128)(2,1)}, u32[]{:S(2)}, u32[]{:S(2)}) collective-permute-start(bf16[768,512]{1,0:T(8,128)(2,1)} %dynamic-slice_convert_fusion.1), channel_id=1, source_target_pairs={{0,16},{8,24},{16,0},{24,8},{1,17},{9,25},{17,1},{25,9},{2,18},{10... | collective-permute-start | bytes 2359304 | tf_op jit(solution)/shard_map/ppermute | solution.py:8
  102.2 1.7 copy-start.1
  104.0 66.4 %collective-permute-start.3 = (bf16[512,768]{1,0:T(8,128)(2,1)S(1)}, bf16[512,768]{1,0:T(8,128)(2,1)}, u32[]{:S(2)}, u32[]{:S(2)}) collective-permute-start(bf16[512,768]{1,0:T(8,128)(2,1)S(1)} %dynamic-slice_convert_fusion), channel_id=1, source_target_pairs={{0,16},{8,24},{16,0},{24,8},{1,17},{9,25},{17,1},{25,9},{2,18},{10... | collective-permute-start | bytes 2359304 | tf_op jit(solution)/shard_map/ppermute | solution.py:8
  111.1 62.9 %all-to-all-start.3 = ((bf16[8,80,768]{2,1,0:T(8,128)(2,1)}), bf16[8,80,768]{2,1,0:T(8,128)(2,1)S(1)}, u32[]{:S(2)}, u32[]{:S(2)}) async-start(bf16[8,80,768]{2,1,0:T(8,128)(2,1)} %bitcast.11), calls=%async_computation.3 | async-start | bytes 1966080 | tf_op jit(solution)/shard_map/all_to_all | solution.py:87
  115.3 55.1 %copy-start.2 = (f32[1024,768]{1,0:T(8,128)S(1)}, f32[1024,768]{1,0:T(8,128)}, u32[]{:S(2)}) copy-start(f32[1024,768]{1,0:T(8,128)} %copy-done.1) | copy-start | bytes 9437188
where the time goes:
time: 176 us; the launch traced here: 175 us
  waiting for transfers between devices  111 us (63%)
  matrix products  30.2 us (17%)
  starting transfers between devices  22.7 us (13%)
  other arithmetic  6.81 us (4%)
  local copies, waits for them, and re-layouts  3.86 us (2%)
    ppermute x4, waiting for transfers between devices, swapped(): lax.ppermute(array, axis, [(i, i ^ 1 << bit) for i in range(lax.axis_size...  101 us
    all_to_all x1, waiting for transfers between devices, shards(): lax.all_to_all(send_tokens, 'expert', split_axis=0, concat_axis=0, tiled=...  10 us
    ppermute x4, starting transfers between devices, swapped(): lax.ppermute(array, axis, [(i, i ^ 1 << bit) for i in range(lax.axis_size...  5.91 us
    dot_general x1, matrix products, shards(): through = jnp.dot(grad_rows, w_down.T, preferred_element_type=jnp.float32)  5.22 us
    all_to_all x1, starting transfers between devices, shards(): lax.all_to_all(send_tokens, 'expert', split_axis=0, concat_axis=0, tiled=...  5.17 us
    dot_general x1, matrix products, shards(): jnp.dot(hidden, w_down, preferred_element_type=jnp.float32)  4.96 us
    broadcast_in_dim x2, other arithmetic, shards(): return (mixed, token_grad, grad_up[None], grad_down[None])  4.96 us
    dot_general x1, matrix products, shards(): preact = jnp.dot(token_rows, w_up, preferred_element_type=jnp.float32)  4.69 us
  transfers between devices with their start and end apart: 8, of which 5 were waited for; matrix products, arithmetic and copies ran while one was open for 19% of the time, Pallas kernels for 0%

commit v1 on v0

v1 whole, which is shorter than its diff:
```python
import jax
import jax.numpy as jnp
from jax import lax
from jax.experimental import pallas as pl
from jax.experimental.pallas import tpu as pltpu
from jax.sharding import PartitionSpec as P

F32 = jnp.float32
BF16 = jnp.bfloat16
VMEM_LIMIT = 48 * 1024 * 1024


def exchange(array, axis, flip):
    return lax.ppermute(array, axis, [(i, i ^ flip) for i in range(lax.axis_size(axis))])


def dot(a, b, contract):
    return lax.dot_general(a, b, (contract, ((), ())), preferred_element_type=F32)


def call(body, out_shape, *args):
    return pl.pallas_call(
        body,
        out_shape=out_shape,
        compiler_params=pltpu.CompilerParams(vmem_limit_bytes=VMEM_LIMIT),
    )(*args)


def shape(rows, columns, dtype=BF16):
    return jax.ShapeDtypeStruct((rows, columns), dtype)


def slot_positions(route_row, device, experts, capacity):
    local = route_row.shape[1]

    def body(device_ref, route_ref, slot_ref):
        route = route_ref[...]
        expert = lax.broadcasted_iota(jnp.int32, (experts, local), 0)
        choose = jnp.where(expert == route, 1.0, 0.0)
        earlier = lax.broadcasted_iota(jnp.int32, (local, local), 0)
        later = lax.broadcasted_iota(jnp.int32, (local, local), 1)
        upto = jnp.where(earlier <= later, 1.0, 0.0).astype(BF16)
        running = dot(choose.astype(BF16), upto, ((1,), (0,)))
        rank = jnp.sum(running * choose, axis=0, keepdims=True) - 1.0
        slot_ref[...] = (route ^ device_ref[0]) * capacity + rank.astype(jnp.int32)

    return pl.pallas_call(
        body,
        out_shape=shape(1, local, jnp.int32),
        in_specs=[
            pl.BlockSpec(memory_space=pltpu.SMEM),
            pl.BlockSpec(memory_space=pltpu.VMEM),
        ],
    )(device, route_row)


def dispatch(slots, values, blocks, rows):
    local, width = values.shape

    def body(slot_ref, value_ref, *outs):
        number = lax.broadcasted_iota(jnp.int32, (blocks * rows, local), 0)
        placing = jnp.where(number == slot_ref[...], 1.0, 0.0).astype(BF16)
        placed = dot(placing, value_ref[...], ((1,), (0,))).astype(BF16)
        for block, out in enumerate(outs):
            out[...] = placed[block * rows : (block + 1) * rows]

    return call(body, [shape(rows, width)] * blocks, slots, values)


def collect(slots, parts):
    blocks = len(parts)
    rows, width = parts[0].shape
    local = slots.shape[1]

    def body(slot_ref, *refs):
        out = refs[-1]
        row = lax.broadcasted_iota(jnp.int32, (local, local), 0)
        column = lax.broadcasted_iota(jnp.int32, (local, local), 1)
        wanted = jnp.where(row == column, slot_ref[...].astype(F32), 0.0)
        wanted = jnp.sum(wanted, axis=1, keepdims=True).astype(jnp.int32)
        number = lax.broadcasted_iota(jnp.int32, (local, blocks * rows), 1)
        picking = jnp.where(number == wanted, 1.0, 0.0).astype(BF16)
        every = jnp.concatenate([ref[...] for ref in refs[:-1]], axis=0)
        out[...] = dot(picking, every, ((1,), (0,))).astype(BF16)

    return call(body, shape(local, width), slots, *parts)


def rows_of(refs, which, capacity):
    return jnp.concatenate(
        [ref[which * capacity : (which + 1) * capacity, :] for ref in refs], axis=0
    )


def forward(parts, ups, downs, capacity):
    blocks = len(parts)
    width, half = ups[0].shape
    count = blocks * capacity

    def body(*refs):
        tokens, refs = refs[:blocks], refs[blocks:]
        up, down, refs = refs[:2], refs[2:4], refs[4:]
        outs, hiddens, slopes = refs[:blocks], refs[blocks : blocks + 2], refs[blocks + 2 :]
        for which in range(2):
            preact = dot(rows_of(tokens, which, capacity), up[which][...], ((1,), (0,)))
            square = preact * preact
            tangent = jnp.tanh(0.7978845608 * (preact + 0.044715 * preact * square))
            hidden = (0.5 * preact * (1.0 + tangent)).astype(BF16)
            slope = 0.5 * (1.0 + tangent) + 0.5 * preact * (1.0 - tangent * tangent) * (
                0.7978845608 * (1.0 + 0.134145 * square)
            )
            hiddens[which][...] = hidden
            slopes[which][...] = slope.astype(BF16)
            result = dot(hidden, down[which][...], ((1,), (0,))).astype(BF16)
            for block, out in enumerate(outs):
                out[which * capacity : (which + 1) * capacity, :] = result[
                    block * capacity : (block + 1) * capacity
                ]

    results = call(
        body,
        [shape(2 * capacity, width)] * blocks + [shape(count, half)] * 4,
        *parts,
        *ups,
        *downs,
    )
    return results[:blocks], results[blocks : blocks + 2], results[blocks + 2 :]


def backward(parts, slopes, ups, downs, capacity):
    blocks = len(parts)
    width, half = ups[0].shape
    count = blocks * capacity

    def body(*refs):
        grads, refs = refs[:blocks], refs[blocks:]
        slope, up, down, refs = refs[:2], refs[2:4], refs[4:6], refs[6:]
        outs, hidden_grads = refs[:blocks], refs[blocks:]
        for which in range(2):
            through = dot(rows_of(grads, which, capacity), down[which][...], ((1,), (1,)))
            hidden_grad = (through * slope[which][...].astype(F32)).astype(BF16)
            hidden_grads[which][...] = hidden_grad
            result = dot(hidden_grad, up[which][...], ((1,), (1,))).astype(BF16)
            for block, out in enumerate(outs):
                out[which * capacity : (which + 1) * capacity, :] = result[
                    block * capacity : (block + 1) * capacity
                ]

    results = call(
        body,
        [shape(2 * capacity, width)] * blocks + [shape(count, half)] * 2,
        *parts,
        *slopes,
        *ups,
        *downs,
    )
    return results[:blocks], results[blocks:]


def weight_gradients(which, token_parts, grad_parts, hiddens, hidden_grads, capacity, dtype):
    blocks = len(token_parts)
    width = token_parts[0].shape[1]
    half = hiddens[0].shape[1]

    def body(*refs):
        tokens, refs = refs[:blocks], refs[blocks:]
        grads, refs = refs[:blocks], refs[blocks:]
        hidden, hidden_grad, refs = refs[:2], refs[2:4], refs[4:]
        up_out, down_out = refs
        rows = rows_of(tokens, which, capacity)
        both = jnp.concatenate([ref[...] for ref in hidden_grad], axis=0)
        up_out[...] = dot(rows, both, ((0,), (0,))).astype(dtype)
        rows = rows_of(grads, which, capacity)
        both = jnp.concatenate([ref[...] for ref in hidden], axis=0)
        down_out[...] = dot(both, rows, ((0,), (0,))).astype(dtype)

    return call(
        body,
        [shape(width, half, dtype), shape(half, width, dtype)],
        *token_parts,
        *grad_parts,
        *hiddens,
        *hidden_grads,
    )


def spread(parts):
    return [parts[0]] + [exchange(part, "expert", 2 * m) for m, part in enumerate(parts) if m]


def shards(tokens, gate_prob, routing, up_weight, down_weight, cotangent):
    experts = lax.axis_size("expert")
    opposite = lax.axis_size("section") // 2
    local = tokens.shape[0]
    capacity = -(-2 * local // experts // 16) * 16
    blocks = experts // 2
    device = lax.axis_index("expert").astype(jnp.int32).reshape(1)

    def across(array):
        return exchange(array, "section", opposite)

    pair_tokens = across(tokens)
    slots = slot_positions(routing.reshape(1, local), device, experts, capacity)
    pair_slots = across(slots)
    ups = (up_weight[0], exchange(up_weight[0], "expert", 1))
    downs = (down_weight[0], exchange(down_weight[0], "expert", 1))
    scaled = (gate_prob[:, None] * cotangent.astype(F32)).astype(BF16)
    own_x = spread(dispatch(slots, tokens, blocks, 2 * capacity))
    own_c = spread(dispatch(slots, scaled, blocks, 2 * capacity))
    later_scaled, _ = lax.optimization_barrier((scaled, pair_tokens))
    pair_scaled = across(later_scaled)

    pair_x = spread(dispatch(pair_slots, pair_tokens, blocks, 2 * capacity))
    pair_out, pair_hidden, pair_slope = forward(pair_x, ups, downs, capacity)
    pair_out = across(collect(pair_slots, spread(pair_out)))
    own_out, own_hidden, own_slope = forward(own_x, ups, downs, capacity)
    own_out = collect(slots, spread(own_out))

    pair_c = spread(dispatch(pair_slots, pair_scaled, blocks, 2 * capacity))
    pair_back, pair_hidden_grad = backward(pair_c, pair_slope, ups, downs, capacity)
    pair_back = across(collect(pair_slots, spread(pair_back)))
    own_back, own_hidden_grad = backward(own_c, own_slope, ups, downs, capacity)
    own_back = collect(slots, spread(own_back))

    def gradients(which, dtype):
        return weight_gradients(
            which,
            own_x + pair_x,
            own_c + pair_c,
            (own_hidden[which], pair_hidden[which]),
            (own_hidden_grad[which], pair_hidden_grad[which]),
            capacity,
            dtype,
        )

    give_up, give_down = gradients(1, BF16)
    peer_up, peer_down = exchange(give_up, "expert", 1), exchange(give_down, "expert", 1)
    keep_up, keep_down = gradients(0, F32)
    grad_up = (keep_up + peer_up.astype(F32)).astype(BF16)
    grad_down = (keep_down + peer_down.astype(F32)).astype(BF16)
    out = (own_out.astype(F32) + pair_out.astype(F32)).astype(BF16)
    mixed = (gate_prob[:, None] * out.astype(F32)).astype(BF16)
    token_grad = (own_back.astype(F32) + pair_back.astype(F32)).astype(BF16)
    return (mixed, token_grad, grad_up[None], grad_down[None])


def solution(mesh):
    in_specs = (
        P(("section", "expert"), None),
        P(("section", "expert")),
        P(("section", "expert"), None),
        P(("section", "expert"), None, None),
        P(("section", "expert"), None, None),
        P(("section", "expert"), None),
    )
    out_specs = (
        P(("section", "expert"), None),
        P(("section", "expert"), None),
        P(("section", "expert"), None, None),
        P(("section", "expert"), None, None),
    )
    return jax.shard_map(shards, mesh=mesh, in_specs=in_specs, out_specs=out_specs, check_vma=False)
```

time: 176 us -> 168 us (0.955)
  matrix products: 30.2 us -> 0 us
  Pallas kernels: 0 us -> 22.6 us
  starting transfers between devices: 22.7 us -> 32.6 us
  waiting for transfers between devices: 111 us -> 103 us
    dot_general x10 -> x0, matrix products: 30.2 us -> none  [the longest x1 5.22 us: shards(): through = jnp.dot(grad_rows, w_down.T, preferred_element_type=jnp.float32)]
    ppermute x4 -> x33, starting transfers between devices: 5.91 us -> 32.6 us  [exchange(): lax.ppermute(array, axis, [(i, i ^ flip) for i in range(lax.axis_size(axi...]
    pallas_call x0 -> x15, Pallas kernels: none -> 22.6 us  [the longest x14 21.2 us: call(): pl.pallas_call(body, out_shape=out_shape, compiler_params=pltpu.CompilerP...]
    all_to_all x4 -> x0, starting transfers between devices: 16.8 us -> none  [the longest x1 5.17 us: shards(): lax.all_to_all(send_tokens, 'expert', split_axis=0, concat_axis=0, tiled=...]
    all_to_all x4 -> x0, waiting for transfers between devices: 10 us -> none  [the longest x1 10 us: shards(): lax.all_to_all(send_tokens, 'expert', split_axis=0, concat_axis=0, tiled=...]
    convert_element_type x0 -> x2, other arithmetic: none -> 1.92 us  [the longest x1 1.03 us: shards(): scaled = (gate_prob[:, None] * cotangent.astype(F32)).astype(BF16)]
    ppermute x4 -> x33, waiting for transfers between devices: 101 us -> 103 us  [exchange(): lax.ppermute(array, axis, [(i, i ^ flip) for i in range(lax.axis_size(axi...]
  transfers between devices with their start and end apart: 8 -> 33, of which waited for: 5 -> 17; matrix products, arithmetic and copies ran while one was open for 19% -> 2% of each run, Pallas kernels for 0% -> 11%
where the time goes in v1:
time: 168 us; the launch traced here: 167 us
  waiting for transfers between devices  103 us (61%)
  starting transfers between devices  32.6 us (19%)
  Pallas kernels  22.6 us (13%)
  other arithmetic  5.68 us (3%)
  local copies, waits for them, and re-layouts  3.18 us (2%)
    ppermute x33, waiting for transfers between devices, exchange(): lax.ppermute(array, axis, [(i, i ^ flip) for i in range(lax.axis_size(axi...  103 us
    ppermute x33, starting transfers between devices, exchange(): lax.ppermute(array, axis, [(i, i ^ flip) for i in range(lax.axis_size(axi...  32.6 us
    pallas_call x14, Pallas kernels, call(): pl.pallas_call(body, out_shape=out_shape, compiler_params=pltpu.CompilerP...  21.2 us
    broadcast_in_dim x2, other arithmetic, shards(): return (mixed, token_grad, grad_up[None], grad_down[None])  3.76 us
  transfers between devices with their start and end apart: 33, of which 17 were waited for; matrix products, arithmetic and copies ran while one was open for 2% of the time, Pallas kernels for 11%

profile of v1, /device:TPU:0, one launch (start us, length us, event | category | flops | bytes accessed | tf_op | source)
XLA Modules:
  0.0 167.4 jit_solution(795435734192663627)
XLA Ops:
  0.6 0.5 collective-permute-start.3
  1.2 4.0 %collective-permute-start.9 = (bf16[320,768]{1,0:T(8,128)(2,1)}, bf16[320,768]{1,0:T(8,128)(2,1)S(1)}, u32[]{:S(2)}, u32[]{:S(2)}) collective-permute-start(bf16[320,768]{1,0:T(8,128)(2,1)} %value_ref.1), channel_id=1, source_target_pairs={{0,16},{8,24},{16,0},{24,8},{1,17},{9,25},{17,1},{25,9},{2,18},{10... | collective-permute-start | bytes 1474568 | tf_op jit(solution)/shard_map/ppermute | solution.py:14
  5.2 1.4 shard_map.93.slot_ref
  6.7 20.9 %collective-permute-done.8.slot_ref = s32[1,320]{1,0:T(1,128)S(1)} collective-permute-done((s32[1,320]{1,0:T(1,128)}, s32[1,320]{1,0:T(1,128)S(1)}, u32[]{:S(2)}, u32[]{:S(2)}) %collective-permute-start.8) | collective-permute-done | bytes 1312 | tf_op jit(solution)/shard_map/ppermute | solution.py:14
  27.5 0.7 shard_map.97
  28.2 1.6 collective-permute-start.10
  29.8 1.5 collective-permute-start.11
  31.3 0.4 collective-permute-start.12
  31.8 5.4 %collective-permute-done.10.refs_1_.refs_5_ = bf16[160,768]{1,0:T(8,128)(2,1)S(1)} collective-permute-done((bf16[160,768]{1,0:T(8,128)(2,1)S(1)}, bf16[160,768]{1,0:T(8,128)(2,1)S(1)}, u32[]{:S(2)}, u32[]{:S(2)}) %collective-permute-start.10) | collective-permute-done | bytes 245792 | tf_op jit(solution)/shard_map/ppermute | solution.py:14
  37.2 4.7 %collective-permute-done.11.refs_2_.refs_6_ = bf16[160,768]{1,0:T(8,128)(2,1)S(1)} collective-permute-done((bf16[160,768]{1,0:T(8,128)(2,1)S(1)}, bf16[160,768]{1,0:T(8,128)(2,1)S(1)}, u32[]{:S(2)}, u32[]{:S(2)}) %collective-permute-start.11) | collective-permute-done | bytes 245792 | tf_op jit(solution)/shard_map/ppermute | solution.py:14
  41.9 0.9 copy-done.6
  42.8 1.1 copy-done
  43.9 1.1 copy-done.2
  45.1 3.0 %shard_map.98 = (bf16[160,768]{1,0:T(8,128)(2,1)S(1)}, bf16[160,768]{1,0:T(8,128)(2,1)S(1)}, bf16[160,768]{1,0:T(8,128)(2,1)S(1)}, bf16[160,768]{1,0:T(8,128)(2,...) custom-call(bf16[160,768]{1,0:T(8,128)(2,1)S(1)} %get-tuple-element., ...), custom_call_target="tpu_custom_call" | custom-call | tf_op jit(solution)/shard_map/pallas_call | solution.py:22
  48.1 1.3 collective-permute-start.13
  49.4 0.8 collective-permute-start.14
  50.2 1.4 collective-permute-start.15
  51.6 0.7 shard_map.94
  52.3 1.3 collective-permute-start
  53.6 0.8 collective-permute-start.1
  54.4 2.6 %collective-permute-done.13.refs_1_ = bf16[160,768]{1,0:T(8,128)(2,1)S(1)} collective-permute-done((bf16[160,768]{1,0:T(8,128)(2,1)S(1)}, bf16[160,768]{1,0:T(8,128)(2,1)S(1)}, u32[]{:S(2)}, u32[]{:S(2)}) %collective-permute-start.13) | collective-permute-done | bytes 245792 | tf_op jit(solution)/shard_map/ppermute | solution.py:14
  57.0 1.5 collective-permute-start.2
  58.5 5.0 %collective-permute-done.14.refs_2_ = bf16[160,768]{1,0:T(8,128)(2,1)S(1)} collective-permute-done((bf16[160,768]{1,0:T(8,128)(2,1)S(1)}, bf16[160,768]{1,0:T(8,128)(2,1)S(1)}, u32[]{:S(2)}, u32[]{:S(2)}) %collective-permute-start.14) | collective-permute-done | bytes 245792 | tf_op jit(solution)/shard_map/ppermute | solution.py:14
  63.6 0.6 shard_map.99
  64.3 3.0 %collective-permute-done.refs_1_ = bf16[160,768]{1,0:T(8,128)(2,1)S(1)} collective-permute-done((bf16[160,768]{1,0:T(8,128)(2,1)S(1)}, bf16[160,768]{1,0:T(8,128)(2,1)S(1)}, u32[]{:S(2)}, u32[]{:S(2)}) %collective-permute-start) | collective-permute-done | bytes 245792 | tf_op jit(solution)/shard_map/ppermute | solution.py:14
  67.2 3.8 %collective-permute-done.1.refs_2_ = bf16[160,768]{1,0:T(8,128)(2,1)S(1)} collective-permute-done((bf16[160,768]{1,0:T(8,128)(2,1)S(1)}, bf16[160,768]{1,0:T(8,128)(2,1)S(1)}, u32[]{:S(2)}, u32[]{:S(2)}) %collective-permute-start.1) | collective-permute-done | bytes 245792 | tf_op jit(solution)/shard_map/ppermute | solution.py:14
  71.1 2.9 %shard_map.95 = (bf16[160,768]{1,0:T(8,128)(2,1)S(1)}, bf16[160,768]{1,0:T(8,128)(2,1)S(1)}, bf16[160,768]{1,0:T(8,128)(2,1)S(1)}, bf16[160,768]{1,0:T(8,128)(2,...) custom-call(bf16[160,768]{1,0:T(8,128)(2,1)S(1)} %get-tuple-element., ...), custom_call_target="tpu_custom_call" | custom-call | tf_op jit(solution)/shard_map/pallas_call | solution.py:22
  74.0 0.6 collective-permute-start.5
  74.7 1.5 collective-permute-start.6
  76.1 1.5 collective-permute-start.7
  77.6 2.9 %collective-permute-done.5.refs_1_ = bf16[160,768]{1,0:T(8,128)(2,1)S(1)} collective-permute-done((bf16[160,768]{1,0:T(8,128)(2,1)S(1)}, bf16[160,768]{1,0:T(8,128)(2,1)S(1)}, u32[]{:S(2)}, u32[]{:S(2)}) %collective-permute-start.5) | collective-permute-done | bytes 245792 | tf_op jit(solution)/shard_map/ppermute | solution.py:14
  80.5 3.6 %collective-permute-done.6.refs_2_ = bf16[160,768]{1,0:T(8,128)(2,1)S(1)} collective-permute-done((bf16[160,768]{1,0:T(8,128)(2,1)S(1)}, bf16[160,768]{1,0:T(8,128)(2,1)S(1)}, u32[]{:S(2)}, u32[]{:S(2)}) %collective-permute-start.6) | collective-permute-done | bytes 245792 | tf_op jit(solution)/shard_map/ppermute | solution.py:14
  84.1 0.6 shard_map.96
  84.8 1.0 multiply_convert_fusion
  85.8 20.3 %collective-permute-done.23.value_ref = bf16[320,768]{1,0:T(8,128)(2,1)S(1)} collective-permute-done((bf16[320,768]{1,0:T(8,128)(2,1)S(1)}, bf16[320,768]{1,0:T(8,128)(2,1)S(1)}, u32[]{:S(2)}, u32[]{:S(2)}) %collective-permute-start.23) | collective-permute-done | bytes 491552 | tf_op jit(solution)/shard_map/ppermute | solution.py:14
  106.1 0.7 shard_map.103
  106.7 1.6 collective-permute-start.24
  108.3 0.2 collective-permute-start.25
  108.5 1.8 %collective-permute-start.26 = (bf16[160,768]{1,0:T(8,128)(2,1)S(1)}, bf16[160,768]{1,0:T(8,128)(2,1)S(1)}, u32[]{:S(2)}, u32[]{:S(2)}) collective-permute-start(bf16[160,768]{1,0:T(8,128)(2,1)S(1)} %get-tuple-element.83), channel_id=1, source_target_pairs={{0,6},{1,7},{2,4},{3,5},{4,2},{5,3},{6,0},{7,1},{8,14},{9,15},{10,... | collective-permute-start | bytes 737288 | tf_op jit(solution)/shard_map/ppermute | solution.py:14
  110.3 0.7 shard_map.100
  111.0 1.6 collective-permute-start.17
  112.5 0.2 collective-permute-start.18
  112.8 2.9 %collective-permute-done.24.refs_1_.refs_13_ = bf16[160,768]{1,0:T(8,128)(2,1)S(1)} collective-permute-done((bf16[160,768]{1,0:T(8,128)(2,1)S(1)}, bf16[160,768]{1,0:T(8,128)(2,1)S(1)}, u32[]{:S(2)}, u32[]{:S(2)}) %collective-permute-start.24) | collective-permute-done | bytes 245792 | tf_op jit(solution)/shard_map/ppermute | solution.py:14
  115.7 1.1 collective-permute-start.19
  116.8 5.7 %collective-permute-done.25.refs_2_.refs_14_ = bf16[160,768]{1,0:T(8,128)(2,1)S(1)} collective-permute-done((bf16[160,768]{1,0:T(8,128)(2,1)S(1)}, bf16[160,768]{1,0:T(8,128)(2,1)S(1)}, u32[]{:S(2)}, u32[]{:S(2)}) %collective-permute-start.25) | collective-permute-done | bytes 245792 | tf_op jit(solution)/shard_map/ppermute | solution.py:14
  122.5 2.5 %shard_map.104 = (bf16[160,768]{1,0:T(8,128)(2,1)S(1)}, bf16[160,768]{1,0:T(8,128)(2,1)S(1)}, bf16[160,768]{1,0:T(8,128)(2,1)S(1)}, bf16[160,768]{1,0:T(8,128)(2...) custom-call(bf16[160,768]{1,0:T(8,128)(2,1)S(1)} %get-tuple-element.80.refs_0_.refs_12_, ...), custom_call_target="tpu_custom_call" | custom-call | tf_op jit(solution)/shard_map/pallas_call | solution.py:22
  125.1 1.5 collective-permute-start.28
  126.6 2.0 %collective-permute-start.29 = (bf16[160,768]{1,0:T(8,128)(2,1)S(1)}, bf16[160,768]{1,0:T(8,128)(2,1)S(1)}, u32[]{:S(2)}, u32[]{:S(2)}) collective-permute-start(bf16[160,768]{1,0:T(8,128)(2,1)S(1)} %get-tuple-element.89), channel_id=1, source_target_pairs={{0,6},{1,7},{2,4},{3,5},{4,2},{5,3},{6,0},{7,1},{8,14},{9,15},{10,... | collective-permute-start | bytes 737288 | tf_op jit(solution)/shard_map/ppermute | solution.py:14
  128.6 3.5 %collective-permute-done.18.refs_2_.refs_10_ = bf16[160,768]{1,0:T(8,128)(2,1)S(1)} collective-permute-done((bf16[160,768]{1,0:T(8,128)(2,1)S(1)}, bf16[160,768]{1,0:T(8,128)(2,1)S(1)}, u32[]{:S(2)}, u32[]{:S(2)}) %collective-permute-start.18) | collective-permute-done | bytes 245792 | tf_op jit(solution)/shard_map/ppermute | solution.py:14
  132.1 2.5 %shard_map.101 = (bf16[160,768]{1,0:T(8,128)(2,1)S(1)}, bf16[160,768]{1,0:T(8,128)(2,1)S(1)}, bf16[160,768]{1,0:T(8,128)(2,1)S(1)}, bf16[160,768]{1,0:T(8,128)(2...) custom-call(bf16[160,768]{1,0:T(8,128)(2,1)S(1)} %get-tuple-element.69.refs_0_.refs_8_, ...), custom_call_target="tpu_custom_call" | custom-call | tf_op jit(solution)/shard_map/pallas_call | solution.py:22
  134.6 2.3 %shard_map.107 = (bf16[768,512]{1,0:T(8,128)(2,1)S(1)}, bf16[512,768]{1,0:T(8,128)(2,1)}) custom-call(bf16[160,768]{1,0:T(8,128)(2,1)S(1)} %get-tuple-element.53.refs_0_, bf16[160,768]{1,0:T(8,128)(2,1)S(1)} %collective-permute-done.refs_1_, bf16[160,768]{1,0:T(8,128)(2,1)S(1)} %collective-permute-done.1.refs_2_, ...), custom_call_target="tpu_custom_call" | custom-call | tf_op jit(solution)/shard_map/pallas_call | solution.py:22
  136.9 0.4 collective-permute-done.28.refs_2_
  137.3 0.6 shard_map.105
  138.0 0.4 collective-permute-start.20
  138.5 1.5 collective-permute-start.21
  140.0 1.6 collective-permute-start.22
  141.6 5.3 %collective-permute-done.20.refs_1_ = bf16[160,768]{1,0:T(8,128)(2,1)S(1)} collective-permute-done((bf16[160,768]{1,0:T(8,128)(2,1)S(1)}, bf16[160,768]{1,0:T(8,128)(2,1)S(1)}, u32[]{:S(2)}, u32[]{:S(2)}) %collective-permute-start.20) | collective-permute-done | bytes 245792 | tf_op jit(solution)/shard_map/ppermute | solution.py:14
  146.9 4.6 %collective-permute-done.21.refs_2_ = bf16[160,768]{1,0:T(8,128)(2,1)S(1)} collective-permute-done((bf16[160,768]{1,0:T(8,128)(2,1)S(1)}, bf16[160,768]{1,0:T(8,128)(2,1)S(1)}, u32[]{:S(2)}, u32[]{:S(2)}) %collective-permute-start.21) | collective-permute-done | bytes 245792 | tf_op jit(solution)/shard_map/ppermute | solution.py:14
  151.5 0.6 shard_map.102
  152.1 2.7 %shard_map.106 = (f32[768,512]{1,0:T(8,128)}, f32[512,768]{1,0:T(8,128)}) custom-call(bf16[160,768]{1,0:T(8,128)(2,1)S(1)} %get-tuple-element.53.refs_0_, bf16[160,768]{1,0:T(8,128)(2,1)S(1)} %collective-permute-done.refs_1_, bf16[160,768]{1,0:T(8,128)(2,1)S(1)} %collective-permute-done.1.refs_2_, bf16[160,768]{1,0:T(8,128)(2,1)S(1)} %collective-permute-done.2.refs_3_, ...), custom_call_target="tpu_custom_call" | custom-call | tf_op jit(solution)/shard_map/pallas_call | solution.py:22
  154.8 7.9 %collective-permute-done.30 = bf16[320,768]{1,0:T(8,128)(2,1)S(1)} collective-permute-done((bf16[320,768]{1,0:T(8,128)(2,1)S(1)}, bf16[320,768]{1,0:T(8,128)(2,1)S(1)}, u32[]{:S(2)}, u32[]{:S(2)}) %collective-permute-start.30) | collective-permute-done | bytes 491552 | tf_op jit(solution)/shard_map/ppermute | solution.py:14
  162.7 0.9 add_convert_fusion.2
  163.6 2.7 %fusion = bf16[1,768,512]{2,1,0:T(8,128)(2,1)} fusion(f32[768,512]{1,0:T(8,128)} %get-tuple-element.94, bf16[768,512]{1,0:T(8,128)(2,1)S(1)} %collective-permute-done.31), kind=kLoop, calls=%fused_computation.6 | loop fusion | flops 1179648 | bytes 3145728 | tf_op jit(solution)/shard_map/broadcast_in_dim | solution.py:244
  166.3 1.1 fusion.1
  (41 shorter events, 0.4 us)
Async XLA Ops:
  0.6 41.3 %collective-permute-start.3 = (bf16[768,512]{1,0:T(8,128)(2,1)}, bf16[768,512]{1,0:T(8,128)(2,1)S(1)}, u32[]{:S(2)}, u32[]{:S(2)}) collective-permute-start(bf16[768,512]{1,0:T(8,128)(2,1)} %bitcast.8), channel_id=1, source_target_pairs={{0,1},{1,0},{2,3},{3,2},{4,5},{5,4},{6,7},{7,6},{8,9},{9,8},{10,11... | collective-permute-start | bytes 2359304 | tf_op jit(solution)/shard_map/ppermute | solution.py:14
  1.1 40.8 %collective-permute-start.4 = (bf16[512,768]{1,0:T(8,128)(2,1)}, bf16[512,768]{1,0:T(8,128)(2,1)S(1)}, u32[]{:S(2)}, u32[]{:S(2)}) collective-permute-start(bf16[512,768]{1,0:T(8,128)(2,1)} %bitcast.13), channel_id=1, source_target_pairs={{0,1},{1,0},{2,3},{3,2},{4,5},{5,4},{6,7},{7,6},{8,9},{9,8},{10,11... | collective-permute-start | bytes 2359304 | tf_op jit(solution)/shard_map/ppermute | solution.py:14
  1.2 26.3 %collective-permute-start.9 = (bf16[320,768]{1,0:T(8,128)(2,1)}, bf16[320,768]{1,0:T(8,128)(2,1)S(1)}, u32[]{:S(2)}, u32[]{:S(2)}) collective-permute-start(bf16[320,768]{1,0:T(8,128)(2,1)} %value_ref.1), channel_id=1, source_target_pairs={{0,16},{8,24},{16,0},{24,8},{1,17},{9,25},{17,1},{25,9},{2,18},{10... | collective-permute-start | bytes 1474568 | tf_op jit(solution)/shard_map/ppermute | solution.py:14
  6.7 20.9 %collective-permute-start.8 = (s32[1,320]{1,0:T(1,128)}, s32[1,320]{1,0:T(1,128)S(1)}, u32[]{:S(2)}, u32[]{:S(2)}) collective-permute-start(s32[1,320]{1,0:T(1,128)} %shard_map.93.slot_ref), channel_id=1, source_target_pairs={{0,16},{8,24},{16,0},{24,8},{1,17},{9,25},{17,1},{25,9},{2,18},{10... | collective-permute-start | bytes 3848 | tf_op jit(solution)/shard_map/ppermute | solution.py:14
  28.2 9.0 %collective-permute-start.10 = (bf16[160,768]{1,0:T(8,128)(2,1)S(1)}, bf16[160,768]{1,0:T(8,128)(2,1)S(1)}, u32[]{:S(2)}, u32[]{:S(2)}) collective-permute-start(bf16[160,768]{1,0:T(8,128)(2,1)S(1)} %get-tuple-element.62), channel_id=1, source_target_pairs={{0,2},{1,3},{2,0},{3,1},{4,6},{5,7},{6,4},{7,5},{8,10},{9,11},{10,... | collective-permute-start | bytes 737288 | tf_op jit(solution)/shard_map/ppermute | solution.py:14
  29.8 12.1 %collective-permute-start.11 = (bf16[160,768]{1,0:T(8,128)(2,1)S(1)}, bf16[160,768]{1,0:T(8,128)(2,1)S(1)}, u32[]{:S(2)}, u32[]{:S(2)}) collective-permute-start(bf16[160,768]{1,0:T(8,128)(2,1)S(1)} %get-tuple-element.63), channel_id=1, source_target_pairs={{0,4},{1,5},{2,6},{3,7},{4,0},{5,1},{6,2},{7,3},{8,12},{9,13},{10,... | collective-permute-start | bytes 737288 | tf_op jit(solution)/shard_map/ppermute | solution.py:14
  31.3 10.5 %collective-permute-start.12 = (bf16[160,768]{1,0:T(8,128)(2,1)S(1)}, bf16[160,768]{1,0:T(8,128)(2,1)S(1)}, u32[]{:S(2)}, u32[]{:S(2)}) collective-permute-start(bf16[160,768]{1,0:T(8,128)(2,1)S(1)} %get-tuple-element.64), channel_id=1, source_target_pairs={{0,6},{1,7},{2,4},{3,5},{4,2},{5,3},{6,0},{7,1},{8,14},{9,15},{10,... | collective-permute-start | bytes 737288 | tf_op jit(solution)/shard_map/ppermute | solution.py:14
  41.9 0.9 copy-start.6
  42.8 1.1 copy-start
  43.9 1.1 copy-start.2
  45.1 6.6 %copy-start.4 = (bf16[320,768]{1,0:T(8,128)(2,1)S(1)}, bf16[320,768]{1,0:T(8,128)(2,1)}, u32[]{:S(2)}) copy-start(bf16[320,768]{1,0:T(8,128)(2,1)} %value_ref.1) | copy-start | bytes 1474564
  45.1 6.6 %copy-start.5 = (s32[1,320]{1,0:T(1,128)S(1)}, s32[1,320]{1,0:T(1,128)}, u32[]{:S(2)}) copy-start(s32[1,320]{1,0:T(1,128)} %shard_map.93.slot_ref) | copy-start | bytes 3844
  48.1 23.0 %copy-start.1 = (bf16[1,768,512]{2,1,0:T(8,128)(2,1)S(1)}, bf16[1,768,512]{2,1,0:T(8,128)(2,1)}, u32[]{:S(2)}) copy-start(bf16[1,768,512]{2,1,0:T(8,128)(2,1)} %param.9) | copy-start | bytes 2359300
  48.1 23.0 %copy-start.3 = (bf16[1,512,768]{2,1,0:T(8,128)(2,1)S(1)}, bf16[1,512,768]{2,1,0:T(8,128)(2,1)}, u32[]{:S(2)}) copy-start(bf16[1,512,768]{2,1,0:T(8,128)(2,1)} %param.10) | copy-start | bytes 2359300
  48.1 9.0 %collective-permute-start.13 = (bf16[160,768]{1,0:T(8,128)(2,1)S(1)}, bf16[160,768]{1,0:T(8,128)(2,1)S(1)}, u32[]{:S(2)}, u32[]{:S(2)}) collective-permute-start(bf16[160,768]{1,0:T(8,128)(2,1)S(1)} %get-tuple-element.66), channel_id=1, source_target_pairs={{0,2},{1,3},{2,0},{3,1},{4,6},{5,7},{6,4},{7,5},{8,10},{9,11},{10,... | collective-permute-start | bytes 737288 | tf_op jit(solution)/shard_map/ppermute | solution.py:14
  49.4 14.2 %collective-permute-start.14 = (bf16[160,768]{1,0:T(8,128)(2,1)S(1)}, bf16[160,768]{1,0:T(8,128)(2,1)S(1)}, u32[]{:S(2)}, u32[]{:S(2)}) collective-permute-start(bf16[160,768]{1,0:T(8,128)(2,1)S(1)} %get-tuple-element.67), channel_id=1, source_target_pairs={{0,4},{1,5},{2,6},{3,7},{4,0},{5,1},{6,2},{7,3},{8,12},{9,13},{10,... | collective-permute-start | bytes 737288 | tf_op jit(solution)/shard_map/ppermute | solution.py:14
  50.2 13.4 %collective-permute-start.15 = (bf16[160,768]{1,0:T(8,128)(2,1)S(1)}, bf16[160,768]{1,0:T(8,128)(2,1)S(1)}, u32[]{:S(2)}, u32[]{:S(2)}) collective-permute-start(bf16[160,768]{1,0:T(8,128)(2,1)S(1)} %get-tuple-element.68), channel_id=1, source_target_pairs={{0,6},{1,7},{2,4},{3,5},{4,2},{5,3},{6,0},{7,1},{8,14},{9,15},{10,... | collective-permute-start | bytes 737288 | tf_op jit(solution)/shard_map/ppermute | solution.py:14
  52.3 14.9 %collective-permute-start = (bf16[160,768]{1,0:T(8,128)(2,1)S(1)}, bf16[160,768]{1,0:T(8,128)(2,1)S(1)}, u32[]{:S(2)}, u32[]{:S(2)}) collective-permute-start(bf16[160,768]{1,0:T(8,128)(2,1)S(1)} %get-tuple-element.54), channel_id=1, source_target_pairs={{0,2},{1,3},{2,0},{3,1},{4,6},{5,7},{6,4},{7,5},{8,10},{9,11},{10,... | collective-permute-start | bytes 737288 | tf_op jit(solution)/shard_map/ppermute | solution.py:14
  53.6 17.4 %collective-permute-start.1 = (bf16[160,768]{1,0:T(8,128)(2,1)S(1)}, bf16[160,768]{1,0:T(8,128)(2,1)S(1)}, u32[]{:S(2)}, u32[]{:S(2)}) collective-permute-start(bf16[160,768]{1,0:T(8,128)(2,1)S(1)} %get-tuple-element.55), channel_id=1, source_target_pairs={{0,4},{1,5},{2,6},{3,7},{4,0},{5,1},{6,2},{7,3},{8,12},{9,13},{10,... | collective-permute-start | bytes 737288 | tf_op jit(solution)/shard_map/ppermute | solution.py:14
  57.0 14.0 %collective-permute-start.2 = (bf16[160,768]{1,0:T(8,128)(2,1)S(1)}, bf16[160,768]{1,0:T(8,128)(2,1)S(1)}, u32[]{:S(2)}, u32[]{:S(2)}) collective-permute-start(bf16[160,768]{1,0:T(8,128)(2,1)S(1)} %get-tuple-element.56), channel_id=1, source_target_pairs={{0,6},{1,7},{2,4},{3,5},{4,2},{5,3},{6,0},{7,1},{8,14},{9,15},{10,... | collective-permute-start | bytes 737288 | tf_op jit(solution)/shard_map/ppermute | solution.py:14
  64.2 20.6 %collective-permute-start.16 = (bf16[320,768]{1,0:T(8,128)(2,1)S(1)}, bf16[320,768]{1,0:T(8,128)(2,1)S(1)}, u32[]{:S(2)}, u32[]{:S(2)}) collective-permute-start(bf16[320,768]{1,0:T(8,128)(2,1)S(1)} %shard_map.99), channel_id=1, source_target_pairs={{0,16},{8,24},{16,0},{24,8},{1,17},{9,25},{17,1},{25,9},{2,18},{10... | collective-permute-start | bytes 1474568 | tf_op jit(solution)/shard_map/ppermute | solution.py:14
  71.1 13.7 %copy-start.9 = (f32[320]{0:T(512)S(1)}, f32[320]{0:T(512)}, u32[]{:S(2)}) copy-start(f32[320]{0:T(512)} %param.7) | copy-start | bytes 3844
  74.0 10.7 %copy-start.8 = (bf16[320,768]{1,0:T(8,128)(2,1)S(1)}, bf16[320,768]{1,0:T(8,128)(2,1)}, u32[]{:S(2)}) copy-start(bf16[320,768]{1,0:T(8,128)(2,1)} %param.11) | copy-start | bytes 1474564
  74.0 6.4 %collective-permute-start.5 = (bf16[160,768]{1,0:T(8,128)(2,1)S(1)}, bf16[160,768]{1,0:T(8,128)(2,1)S(1)}, u32[]{:S(2)}, u32[]{:S(2)}) collective-permute-start(bf16[160,768]{1,0:T(8,128)(2,1)S(1)} %get-tuple-element.58), channel_id=1, source_target_pairs={{0,2},{1,3},{2,0},{3,1},{4,6},{5,7},{6,4},{7,5},{8,10},{9,11},{10,... | collective-permute-start | bytes 737288 | tf_op jit(solution)/shard_map/ppermute | solution.py:14
  74.7 9.4 %collective-permute-start.6 = (bf16[160,768]{1,0:T(8,128)(2,1)S(1)}, bf16[160,768]{1,0:T(8,128)(2,1)S(1)}, u32[]{:S(2)}, u32[]{:S(2)}) collective-permute-start(bf16[160,768]{1,0:T(8,128)(2,1)S(1)} %get-tuple-element.59), channel_id=1, source_target_pairs={{0,4},{1,5},{2,6},{3,7},{4,0},{5,1},{6,2},{7,3},{8,12},{9,13},{10,... | collective-permute-start | bytes 737288 | tf_op jit(solution)/shard_map/ppermute | solution.py:14
  76.1 8.0 %collective-permute-start.7 = (bf16[160,768]{1,0:T(8,128)(2,1)S(1)}, bf16[160,768]{1,0:T(8,128)(2,1)S(1)}, u32[]{:S(2)}, u32[]{:S(2)}) collective-permute-start(bf16[160,768]{1,0:T(8,128)(2,1)S(1)} %get-tuple-element.60), channel_id=1, source_target_pairs={{0,6},{1,7},{2,4},{3,5},{4,2},{5,3},{6,0},{7,1},{8,14},{9,15},{10,... | collective-permute-start | bytes 737288 | tf_op jit(solution)/shard_map/ppermute | solution.py:14
  85.8 20.3 %collective-permute-start.23 = (bf16[320,768]{1,0:T(8,128)(2,1)S(1)}, bf16[320,768]{1,0:T(8,128)(2,1)S(1)}, u32[]{:S(2)}, u32[]{:S(2)}) collective-permute-start(bf16[320,768]{1,0:T(8,128)(2,1)S(1)} %get-tuple-element.79.value_ref), channel_id=1, source_target_pairs={{0,16},{8,24},{16,0},{24,8},{1,17},{9,25},{17,1},{25,9},{2,18},{10... | collective-permute-start | bytes 1474568 | tf_op jit(solution)/shard_map/ppermute | solution.py:14
  106.7 9.0 %collective-permute-start.24 = (bf16[160,768]{1,0:T(8,128)(2,1)S(1)}, bf16[160,768]{1,0:T(8,128)(2,1)S(1)}, u32[]{:S(2)}, u32[]{:S(2)}) collective-permute-start(bf16[160,768]{1,0:T(8,128)(2,1)S(1)} %get-tuple-element.81), channel_id=1, source_target_pairs={{0,2},{1,3},{2,0},{3,1},{4,6},{5,7},{6,4},{7,5},{8,10},{9,11},{10,... | collective-permute-start | bytes 737288 | tf_op jit(solution)/shard_map/ppermute | solution.py:14
  108.3 14.2 %collective-permute-start.25 = (bf16[160,768]{1,0:T(8,128)(2,1)S(1)}, bf16[160,768]{1,0:T(8,128)(2,1)S(1)}, u32[]{:S(2)}, u32[]{:S(2)}) collective-permute-start(bf16[160,768]{1,0:T(8,128)(2,1)S(1)} %get-tuple-element.82), channel_id=1, source_target_pairs={{0,4},{1,5},{2,6},{3,7},{4,0},{5,1},{6,2},{7,3},{8,12},{9,13},{10,... | collective-permute-start | bytes 737288 | tf_op jit(solution)/shard_map/ppermute | solution.py:14
  108.5 14.0 %collective-permute-start.26 = (bf16[160,768]{1,0:T(8,128)(2,1)S(1)}, bf16[160,768]{1,0:T(8,128)(2,1)S(1)}, u32[]{:S(2)}, u32[]{:S(2)}) collective-permute-start(bf16[160,768]{1,0:T(8,128)(2,1)S(1)} %get-tuple-element.83), channel_id=1, source_target_pairs={{0,6},{1,7},{2,4},{3,5},{4,2},{5,3},{6,0},{7,1},{8,14},{9,15},{10,... | collective-permute-start | bytes 737288 | tf_op jit(solution)/shard_map/ppermute | solution.py:14
  111.0 15.6 %collective-permute-start.17 = (bf16[160,768]{1,0:T(8,128)(2,1)S(1)}, bf16[160,768]{1,0:T(8,128)(2,1)S(1)}, u32[]{:S(2)}, u32[]{:S(2)}) collective-permute-start(bf16[160,768]{1,0:T(8,128)(2,1)S(1)} %get-tuple-element.70), channel_id=1, source_target_pairs={{0,2},{1,3},{2,0},{3,1},{4,6},{5,7},{6,4},{7,5},{8,10},{9,11},{10,... | collective-permute-start | bytes 737288 | tf_op jit(solution)/shard_map/ppermute | solution.py:14
  112.5 19.5 %collective-permute-start.18 = (bf16[160,768]{1,0:T(8,128)(2,1)S(1)}, bf16[160,768]{1,0:T(8,128)(2,1)S(1)}, u32[]{:S(2)}, u32[]{:S(2)}) collective-permute-start(bf16[160,768]{1,0:T(8,128)(2,1)S(1)} %get-tuple-element.71), channel_id=1, source_target_pairs={{0,4},{1,5},{2,6},{3,7},{4,0},{5,1},{6,2},{7,3},{8,12},{9,13},{10,... | collective-permute-start | bytes 737288 | tf_op jit(solution)/shard_map/ppermute | solution.py:14
  115.7 16.4 %collective-permute-start.19 = (bf16[160,768]{1,0:T(8,128)(2,1)S(1)}, bf16[160,768]{1,0:T(8,128)(2,1)S(1)}, u32[]{:S(2)}, u32[]{:S(2)}) collective-permute-start(bf16[160,768]{1,0:T(8,128)(2,1)S(1)} %get-tuple-element.72), channel_id=1, source_target_pairs={{0,6},{1,7},{2,4},{3,5},{4,2},{5,3},{6,0},{7,1},{8,14},{9,15},{10,... | collective-permute-start | bytes 737288 | tf_op jit(solution)/shard_map/ppermute | solution.py:14
  125.0 11.9 %collective-permute-start.27 = (bf16[160,768]{1,0:T(8,128)(2,1)S(1)}, bf16[160,768]{1,0:T(8,128)(2,1)S(1)}, u32[]{:S(2)}, u32[]{:S(2)}) collective-permute-start(bf16[160,768]{1,0:T(8,128)(2,1)S(1)} %get-tuple-element.87), channel_id=1, source_target_pairs={{0,2},{1,3},{2,0},{3,1},{4,6},{5,7},{6,4},{7,5},{8,10},{9,11},{10,... | collective-permute-start | bytes 737288 | tf_op jit(solution)/shard_map/ppermute | solution.py:14
  125.1 12.2 %collective-permute-start.28 = (bf16[160,768]{1,0:T(8,128)(2,1)S(1)}, bf16[160,768]{1,0:T(8,128)(2,1)S(1)}, u32[]{:S(2)}, u32[]{:S(2)}) collective-permute-start(bf16[160,768]{1,0:T(8,128)(2,1)S(1)} %get-tuple-element.88), channel_id=1, source_target_pairs={{0,4},{1,5},{2,6},{3,7},{4,0},{5,1},{6,2},{7,3},{8,12},{9,13},{10,... | collective-permute-start | bytes 737288 | tf_op jit(solution)/shard_map/ppermute | solution.py:14
  126.6 10.7 %collective-permute-start.29 = (bf16[160,768]{1,0:T(8,128)(2,1)S(1)}, bf16[160,768]{1,0:T(8,128)(2,1)S(1)}, u32[]{:S(2)}, u32[]{:S(2)}) collective-permute-start(bf16[160,768]{1,0:T(8,128)(2,1)S(1)} %get-tuple-element.89), channel_id=1, source_target_pairs={{0,6},{1,7},{2,4},{3,5},{4,2},{5,3},{6,0},{7,1},{8,14},{9,15},{10,... | collective-permute-start | bytes 737288 | tf_op jit(solution)/shard_map/ppermute | solution.py:14
  136.9 26.7 %collective-permute-start.31 = (bf16[768,512]{1,0:T(8,128)(2,1)S(1)}, bf16[768,512]{1,0:T(8,128)(2,1)S(1)}, u32[]{:S(2)}, u32[]{:S(2)}) collective-permute-start(bf16[768,512]{1,0:T(8,128)(2,1)S(1)} %get-tuple-element.99), channel_id=1, source_target_pairs={{0,1},{1,0},{2,3},{3,2},{4,5},{5,4},{6,7},{7,6},{8,9},{9,8},{10,11... | collective-permute-start | bytes 2359304 | tf_op jit(solution)/shard_map/ppermute | solution.py:14
  138.0 24.8 %collective-permute-start.30 = (bf16[320,768]{1,0:T(8,128)(2,1)S(1)}, bf16[320,768]{1,0:T(8,128)(2,1)S(1)}, u32[]{:S(2)}, u32[]{:S(2)}) collective-permute-start(bf16[320,768]{1,0:T(8,128)(2,1)S(1)} %shard_map.105), channel_id=1, source_target_pairs={{0,16},{8,24},{16,0},{24,8},{1,17},{9,25},{17,1},{25,9},{2,18},{10... | collective-permute-start | bytes 1474568 | tf_op jit(solution)/shard_map/ppermute | solution.py:14
  138.0 8.9 %collective-permute-start.20 = (bf16[160,768]{1,0:T(8,128)(2,1)S(1)}, bf16[160,768]{1,0:T(8,128)(2,1)S(1)}, u32[]{:S(2)}, u32[]{:S(2)}) collective-permute-start(bf16[160,768]{1,0:T(8,128)(2,1)S(1)} %get-tuple-element.76), channel_id=1, source_target_pairs={{0,2},{1,3},{2,0},{3,1},{4,6},{5,7},{6,4},{7,5},{8,10},{9,11},{10,... | collective-permute-start | bytes 737288 | tf_op jit(solution)/shard_map/ppermute | solution.py:14
  138.5 13.0 %collective-permute-start.21 = (bf16[160,768]{1,0:T(8,128)(2,1)S(1)}, bf16[160,768]{1,0:T(8,128)(2,1)S(1)}, u32[]{:S(2)}, u32[]{:S(2)}) collective-permute-start(bf16[160,768]{1,0:T(8,128)(2,1)S(1)} %get-tuple-element.77), channel_id=1, source_target_pairs={{0,4},{1,5},{2,6},{3,7},{4,0},{5,1},{6,2},{7,3},{8,12},{9,13},{10,... | collective-permute-start | bytes 737288 | tf_op jit(solution)/shard_map/ppermute | solution.py:14
  140.0 11.5 %collective-permute-start.22 = (bf16[160,768]{1,0:T(8,128)(2,1)S(1)}, bf16[160,768]{1,0:T(8,128)(2,1)S(1)}, u32[]{:S(2)}, u32[]{:S(2)}) collective-permute-start(bf16[160,768]{1,0:T(8,128)(2,1)S(1)} %get-tuple-element.78), channel_id=1, source_target_pairs={{0,6},{1,7},{2,4},{3,5},{4,2},{5,3},{6,0},{7,1},{8,14},{9,15},{10,... | collective-permute-start | bytes 737288 | tf_op jit(solution)/shard_map/ppermute | solution.py:14
  146.9 19.4 %collective-permute-start.32 = (bf16[512,768]{1,0:T(8,128)(2,1)}, bf16[512,768]{1,0:T(8,128)(2,1)S(1)}, u32[]{:S(2)}, u32[]{:S(2)}) collective-permute-start(bf16[512,768]{1,0:T(8,128)(2,1)} %get-tuple-element.101), channel_id=1, source_target_pairs={{0,1},{1,0},{2,3},{3,2},{4,5},{5,4},{6,7},{7,6},{8,9},{9,8},{10,11... | collective-permute-start | bytes 2359304 | tf_op jit(solution)/shard_map/ppermute | solution.py:14
  163.6 2.7 %copy-start.7 = (f32[512,768]{1,0:T(8,128)S(1)}, f32[512,768]{1,0:T(8,128)}, u32[]{:S(2)}) copy-start(f32[512,768]{1,0:T(8,128)} %get-tuple-element.100) | copy-start | bytes 4718596

commit v2 on v1

v2 whole, which is shorter than its diff:
```python
import math

import jax
import jax.numpy as jnp
from jax import lax
from jax.experimental import pallas as pl
from jax.experimental.pallas import tpu as pltpu
from jax.sharding import PartitionSpec as P

F32 = jnp.float32
BF16 = jnp.bfloat16
VMEM_LIMIT = 48 * 1024 * 1024


def exchange(array, axis, flip):
    return lax.ppermute(array, axis, [(i, i ^ flip) for i in range(lax.axis_size(axis))])


def dot(a, b, contract):
    return lax.dot_general(a, b, (contract, ((), ())), preferred_element_type=F32)


def call(body, out_shape, *args, after=()):
    waits = len(after)

    def kernel(*refs):
        body(*refs[waits:])

    return pl.pallas_call(
        kernel,
        out_shape=out_shape,
        in_specs=[pl.BlockSpec(memory_space=pl.ANY)] * waits
        + [pl.BlockSpec(memory_space=pltpu.VMEM)] * len(args),
        cost_estimate=pl.CostEstimate(flops=1, bytes_accessed=1, transcendentals=0),
        compiler_params=pltpu.CompilerParams(vmem_limit_bytes=VMEM_LIMIT),
    )(*after, *args)


def column(row):
    count = row.shape[1]
    down = lax.broadcasted_iota(jnp.int32, (count, count), 0)
    along = lax.broadcasted_iota(jnp.int32, (count, count), 1)
    return jnp.sum(jnp.where(down == along, row, 0.0), axis=1, keepdims=True)


def shape(rows, columns, dtype=BF16):
    return jax.ShapeDtypeStruct((rows, columns), dtype)


def slot_positions(route_row, device, experts, capacity):
    local = route_row.shape[1]

    def body(device_ref, route_ref, slot_ref):
        route = route_ref[...]
        expert = lax.broadcasted_iota(jnp.int32, (experts, local), 0)
        choose = jnp.where(expert == route, 1.0, 0.0)
        earlier = lax.broadcasted_iota(jnp.int32, (local, local), 0)
        later = lax.broadcasted_iota(jnp.int32, (local, local), 1)
        upto = jnp.where(earlier <= later, 1.0, 0.0).astype(BF16)
        running = dot(choose.astype(BF16), upto, ((1,), (0,)))
        rank = jnp.sum(running * choose, axis=0, keepdims=True) - 1.0
        slot_ref[...] = (route ^ device_ref[0]) * capacity + rank.astype(jnp.int32)

    return pl.pallas_call(
        body,
        out_shape=shape(1, local, jnp.int32),
        in_specs=[
            pl.BlockSpec(memory_space=pltpu.SMEM),
            pl.BlockSpec(memory_space=pltpu.VMEM),
        ],
    )(device, route_row)


def dispatch(slots, tokens, scaling, blocks, rows, mode, after=()):
    local, width = tokens.shape
    placed_arrays = 2 if mode == "place" else 1

    def body(slot_ref, token_ref, *refs):
        outs = refs[len(scaling) :]
        values = [token_ref[...]]
        if scaling:
            scaled = column(refs[0][...]) * refs[1][...].astype(F32)
            values.append(scaled.astype(BF16))
        number = lax.broadcasted_iota(jnp.int32, (blocks * rows, local), 0)
        placing = jnp.where(number == slot_ref[...], 1.0, 0.0).astype(BF16)
        for which in range(placed_arrays):
            placed = dot(placing, values[which], ((1,), (0,))).astype(BF16)
            for block in range(blocks):
                outs[block][which * rows : (which + 1) * rows, :] = placed[
                    block * rows : (block + 1) * rows
                ]
        if mode == "give":
            outs[blocks][...] = values[1]

    shapes = [shape(placed_arrays * rows, width)] * blocks + [shape(local, width)] * (mode == "give")
    return call(body, shapes, slots, tokens, *scaling, after=after)


def picked(slot_row, refs, base, rows):
    wanted = column(slot_row.astype(F32)).astype(jnp.int32)
    number = lax.broadcasted_iota(jnp.int32, (slot_row.shape[1], len(refs) * rows), 1)
    picking = jnp.where(number == wanted, 1.0, 0.0).astype(BF16)
    every = jnp.concatenate([ref[base : base + rows, :] for ref in refs], axis=0)
    return dot(picking, every, ((1,), (0,)))


def collect(slots, parts, after=()):
    blocks = len(parts)
    rows, width = parts[0].shape

    def body(slot_ref, *refs):
        refs[-1][...] = picked(slot_ref[...], refs[:blocks], 0, rows).astype(BF16)

    return call(body, shape(slots.shape[1], width), slots, *parts, after=after)


def collect_own(slots, parts, other_out, gate, after=()):
    blocks = len(parts)
    rows, width = parts[0].shape[0] // 2, parts[0].shape[1]
    local = slots.shape[1]

    def body(slot_ref, *refs):
        parts, (other_ref, gate_ref, mixed_ref, back_ref) = refs[:blocks], refs[blocks:]
        out = picked(slot_ref[...], parts, 0, rows) + other_ref[...].astype(F32)
        mixed_ref[...] = (column(gate_ref[...]) * out.astype(BF16).astype(F32)).astype(BF16)
        back_ref[...] = picked(slot_ref[...], parts, rows, rows).astype(BF16)

    return call(body, [shape(local, width)] * 2, slots, *parts, other_out, gate, after=after)


def rows_of(refs, which, capacity, base=0):
    start = base + which * capacity
    return jnp.concatenate([ref[start : start + capacity, :] for ref in refs], axis=0)


def put_rows(refs, which, capacity, base, result):
    start = base + which * capacity
    for block, ref in enumerate(refs):
        ref[start : start + capacity, :] = result[block * capacity : (block + 1) * capacity]


def activation(preact):
    square = preact * preact
    tangent = jnp.tanh(0.7978845608 * (preact + 0.044715 * preact * square))
    hidden = 0.5 * preact * (1.0 + tangent)
    slope = 0.5 * (1.0 + tangent) + 0.5 * preact * (1.0 - tangent * tangent) * (
        0.7978845608 * (1.0 + 0.134145 * square)
    )
    return hidden.astype(BF16), slope


def forward(parts, ups, downs, capacity, after=()):
    blocks = len(parts)
    width, half = ups[0].shape
    count = blocks * capacity

    def body(*refs):
        tokens, refs = refs[:blocks], refs[blocks:]
        up, down, refs = refs[:2], refs[2:4], refs[4:]
        outs, hiddens, slopes = refs[:blocks], refs[blocks : blocks + 2], refs[blocks + 2 :]
        for which in range(2):
            preact = dot(rows_of(tokens, which, capacity), up[which][...], ((1,), (0,)))
            hidden, slope = activation(preact)
            hiddens[which][...] = hidden
            slopes[which][...] = slope.astype(BF16)
            result = dot(hidden, down[which][...], ((1,), (0,))).astype(BF16)
            put_rows(outs, which, capacity, 0, result)

    shapes = [shape(2 * capacity, width)] * blocks + [shape(count, half)] * 4
    results = call(body, shapes, *parts, *ups, *downs, after=after)
    return results[:blocks], results[blocks : blocks + 2], results[blocks + 2 :]


def backward(parts, slopes, ups, downs, capacity, after=()):
    blocks = len(parts)
    width, half = ups[0].shape
    count = blocks * capacity

    def body(*refs):
        grads, refs = refs[:blocks], refs[blocks:]
        slope, up, down, refs = refs[:2], refs[2:4], refs[4:6], refs[6:]
        outs, hidden_grads = refs[:blocks], refs[blocks:]
        for which in range(2):
            through = dot(rows_of(grads, which, capacity), down[which][...], ((1,), (1,)))
            hidden_grad = (through * slope[which][...].astype(F32)).astype(BF16)
            hidden_grads[which][...] = hidden_grad
            result = dot(hidden_grad, up[which][...], ((1,), (1,))).astype(BF16)
            put_rows(outs, which, capacity, 0, result)

    shapes = [shape(2 * capacity, width)] * blocks + [shape(count, half)] * 2
    results = call(body, shapes, *parts, *slopes, *ups, *downs, after=after)
    return results[:blocks], results[blocks:]


def both_ways(parts, ups, downs, capacity, after=()):
    blocks = len(parts)
    width, half = ups[0].shape
    count = blocks * capacity
    base = 2 * capacity

    def body(*refs):
        parts, refs = refs[:blocks], refs[blocks:]
        up, down, refs = refs[:2], refs[2:4], refs[4:]
        outs, hiddens, hidden_grads = refs[:blocks], refs[blocks : blocks + 2], refs[blocks + 2 :]
        for which in range(2):
            preact = dot(rows_of(parts, which, capacity), up[which][...], ((1,), (0,)))
            hidden, slope = activation(preact)
            hiddens[which][...] = hidden
            result = dot(hidden, down[which][...], ((1,), (0,))).astype(BF16)
            put_rows(outs, which, capacity, 0, result)
            through = dot(rows_of(parts, which, capacity, base), down[which][...], ((1,), (1,)))
            hidden_grad = (through * slope).astype(BF16)
            hidden_grads[which][...] = hidden_grad
            result = dot(hidden_grad, up[which][...], ((1,), (1,))).astype(BF16)
            put_rows(outs, which, capacity, base, result)

    shapes = [shape(2 * base, width)] * blocks + [shape(count, half)] * 4
    results = call(body, shapes, *parts, *ups, *downs, after=after)
    return results[:blocks], results[blocks : blocks + 2], results[blocks + 2 :]


def panels(array, size):
    return [array[:, start : start + size] for start in range(0, array.shape[1], size)]


def weight_gradients(which, own, pair_x, pair_c, hiddens, hidden_grads, capacity, peer=None, after=()):
    blocks = len(pair_x)
    width = pair_x[0].shape[1]
    half = hiddens[0].shape[1]
    size = math.gcd(width, half)
    more = () if peer is None else (peer,)

    def body(*refs):
        own, refs = refs[:blocks], refs[blocks:]
        tokens, grads, refs = refs[:blocks], refs[blocks : 2 * blocks], refs[2 * blocks :]
        hidden, hidden_grad, refs = refs[:2], refs[2:4], refs[4:]
        both = [jnp.concatenate([ref[...] for ref in pair], axis=0) for pair in (hidden, hidden_grad)]
        rows = [rows_of(own, which, capacity), rows_of(tokens, which, capacity)]
        up = dot(jnp.concatenate(rows, axis=0), both[1], ((0,), (0,)))
        rows = [rows_of(own, which, capacity, 2 * capacity), rows_of(grads, which, capacity)]
        down = dot(both[0], jnp.concatenate(rows, axis=0), ((0,), (0,)))
        start = 0
        for number, result in enumerate((up, down)):
            for place, panel in enumerate(panels(result, size)):
                stop = start + panel.shape[0]
                if peer is None:
                    refs[0][start:stop, :] = panel.astype(BF16)
                else:
                    total = panel + refs[0][start:stop, :].astype(F32)
                    refs[1 + number][:, place * size : (place + 1) * size] = total.astype(BF16)
                start = stop

    if peer is None:
        shapes = shape(2 * width * half // size, size)
    else:
        shapes = [shape(width, half), shape(half, width)]
    return call(body, shapes, *own, *pair_x, *pair_c, *hiddens, *hidden_grads, *more, after=after)


def added(one, other, after=()):
    def body(one_ref, other_ref, out):
        out[...] = (one_ref[...].astype(F32) + other_ref[...].astype(F32)).astype(BF16)

    return call(body, shape(*one.shape), one, other, after=after)


def spread(parts):
    return [parts[0]] + [exchange(part, "expert", 2 * m) for m, part in enumerate(parts) if m]


def shards(tokens, gate_prob, routing, up_weight, down_weight, cotangent):
    experts = lax.axis_size("expert")
    opposite = lax.axis_size("section") // 2
    local = tokens.shape[0]
    capacity = -(-2 * local // experts // 16) * 16
    blocks = experts // 2
    device = lax.axis_index("expert").astype(jnp.int32).reshape(1)

    def across(array):
        return exchange(array, "section", opposite)

    rows = 2 * capacity
    gate = gate_prob.reshape(1, local)
    pair_tokens = across(tokens)
    slots = slot_positions(routing.reshape(1, local), device, experts, capacity)
    pair_slots = across(slots)
    ups = (up_weight[0], exchange(up_weight[0], "expert", 1))
    downs = (down_weight[0], exchange(down_weight[0], "expert", 1))

    scaling = (gate, cotangent)
    sent = dispatch(slots, tokens, scaling, blocks, rows, "place", after=(ups[1], downs[1]))
    own = spread(sent)
    *sent, scaled = dispatch(
        pair_slots, pair_tokens, scaling, blocks, rows, "give", after=(sent[0],)
    )
    pair_x = spread(sent)
    pair_scaled = across(scaled)
    own_sent, own_hidden, own_hidden_grad = both_ways(
        own, ups, downs, capacity, after=(sent[0],)
    )
    sent, pair_hidden, pair_slope = forward(pair_x, ups, downs, capacity, after=(own_sent[0],))
    back = spread(sent)
    sent = dispatch(pair_slots, pair_scaled, (), blocks, rows, "", after=(sent[0],))
    pair_c = spread(sent)
    term = collect(pair_slots, back, after=(sent[0],))
    other_out = across(term)
    sent, pair_hidden_grad = backward(pair_c, pair_slope, ups, downs, capacity, after=(term,))
    back = spread(sent)

    def gradients(which, peer, after):
        return weight_gradients(
            which,
            own,
            pair_x,
            pair_c,
            (own_hidden[which], pair_hidden[which]),
            (own_hidden_grad[which], pair_hidden_grad[which]),
            capacity,
            peer,
            after,
        )

    term = collect(pair_slots, back, after=(other_out,))
    other_back = across(term)
    give = gradients(1, None, (term,))
    peer = exchange(give, "expert", 1)
    own_back = spread(own_sent)
    grad_up, grad_down = gradients(0, peer, ())
    mixed, own_term = collect_own(slots, own_back, other_out, gate, after=(grad_up,))
    token_grad = added(own_term, other_back, after=(mixed,))
    return (mixed, token_grad, grad_up[None], grad_down[None])


def solution(mesh):
    in_specs = (
        P(("section", "expert"), None),
        P(("section", "expert")),
        P(("section", "expert"), None),
        P(("section", "expert"), None, None),
        P(("section", "expert"), None, None),
        P(("section", "expert"), None),
    )
    out_specs = (
        P(("section", "expert"), None),
        P(("section", "expert"), None),
        P(("section", "expert"), None, None),
        P(("section", "expert"), None, None),
    )
    return jax.shard_map(shards, mesh=mesh, in_specs=in_specs, out_specs=out_specs, check_vma=False)
```

time: 168 us -> 122 us (0.73)
  waiting for transfers between devices: 103 us -> 61.9 us
  other arithmetic: 5.68 us -> 0 us
  starting transfers between devices: 32.6 us -> 29.2 us
  local copies, waits for them, and re-layouts: 3.18 us -> 5.89 us
    ppermute x33 -> x26, waiting for transfers between devices: 103 us -> 61.9 us  [exchange(): lax.ppermute(array, axis, [(i, i ^ flip) for i in range(lax.axis_size(axi...]
    broadcast_in_dim x2 -> x0, other arithmetic: 3.76 us -> none  [shards(): return (mixed, token_grad, grad_up[None], grad_down[None])]
    ppermute x33 -> x26, starting transfers between devices: 32.6 us -> 29.2 us  [exchange(): lax.ppermute(array, axis, [(i, i ^ flip) for i in range(lax.axis_size(axi...]
    unnamed x20 -> x22, local copies, waits for them, and re-layouts: 3.18 us -> 5.2 us
    convert_element_type x2 -> x0, other arithmetic: 1.92 us -> none  [the longest x1 1.03 us: shards(): scaled = (gate_prob[:, None] * cotangent.astype(F32)).astype(BF16)]
    pallas_call x14 -> x12, Pallas kernels: 21.2 us -> 22.8 us  [call(): pl.pallas_call(kernel, out_shape=out_shape, in_specs=[pl.BlockSpec(memory...]
  transfers between devices with their start and end apart: 33 -> 26, of which waited for: 17 -> 14; matrix products, arithmetic and copies ran while one was open for 2% -> 1% of each run, Pallas kernels for 11% -> 16%
where the time goes in v2:
time: 122 us
  waiting for transfers between devices  61.9 us (51%)
  starting transfers between devices  29.2 us (24%)
  Pallas kernels  24.2 us (20%)
  local copies, waits for them, and re-layouts  5.89 us (5%)
    ppermute x26, waiting for transfers between devices, exchange(): lax.ppermute(array, axis, [(i, i ^ flip) for i in range(lax.axis_size(axi...  61.9 us
    ppermute x26, starting transfers between devices, exchange(): lax.ppermute(array, axis, [(i, i ^ flip) for i in range(lax.axis_size(axi...  29.2 us
    pallas_call x12, Pallas kernels, call(): pl.pallas_call(kernel, out_shape=out_shape, in_specs=[pl.BlockSpec(memory...  22.8 us
    unnamed x22, local copies, waits for them, and re-layouts  5.2 us
  transfers between devices with their start and end apart: 26, of which 14 were waited for; matrix products, arithmetic and copies ran while one was open for 1% of the time, Pallas kernels for 16%

profile of v2, /device:TPU:0, one launch (start us, length us, event | category | flops | bytes accessed | tf_op | source)
XLA Modules:
  0.0 122.0 jit_solution(1640508830787153223)
XLA Ops:
  0.6 0.5 collective-permute-start
  1.1 0.1 collective-permute-start.1
  1.2 4.0 %collective-permute-start.6 = (bf16[320,768]{1,0:T(8,128)(2,1)}, bf16[320,768]{1,0:T(8,128)(2,1)S(1)}, u32[]{:S(2)}, u32[]{:S(2)}) collective-permute-start(bf16[320,768]{1,0:T(8,128)(2,1)} %refs_3_.1), channel_id=1, source_target_pairs={{0,16},{8,24},{16,0},{24,8},{1,17},{9,25},{17,1},{25,9},{2,18},{10... | collective-permute-start | bytes 1474568 | tf_op jit(solution)/shard_map/ppermute | solution.py:16
  5.2 0.7 reshape.19.refs_4_.refs_3_.refs_7_
  5.9 1.4 %shard_map.93.refs_2_.refs_1_ = s32[1,320]{1,0:T(1,128)} custom-call(s32[1]{0:T(128)} %bitcast.2.device_ref, s32[1,320]{1,0:T(1,128)} %bitcast.15), custom_call_target="tpu_custom_call" | custom-call | tf_op jit(solution)/shard_map/pallas_call | solution.py:64
  7.3 0.0 collective-permute-done.refs_0_.refs_6_.refs_8_
  7.3 0.0 collective-permute-done.1.refs_1_.refs_8_.refs_10_
  7.3 0.0 copy-start.5
  7.4 1.3 %copy-done.5 = bf16[320,768]{1,0:T(8,128)(2,1)S(1)} copy-done((bf16[320,768]{1,0:T(8,128)(2,1)S(1)}, bf16[320,768]{1,0:T(8,128)(2,1)}, u32[]{:S(2)}) %copy-start.5) | copy-done | bytes 491544
  8.7 1.0 copy-done.8
  9.7 0.7 copy-done.10
  10.4 1.2 shard_map.94
  11.6 1.6 %collective-permute-start.2 = (bf16[320,768]{1,0:T(8,128)(2,1)S(1)}, bf16[320,768]{1,0:T(8,128)(2,1)S(1)}, u32[]{:S(2)}, u32[]{:S(2)}) collective-permute-start(bf16[320,768]{1,0:T(8,128)(2,1)S(1)} %get-tuple-element.44), channel_id=1, source_target_pairs={{0,2},{1,3},{2,0},{3,1},{4,6},{5,7},{6,4},{7,5},{8,10},{9,11},{10,... | collective-permute-start | bytes 1474568 | tf_op jit(solution)/shard_map/ppermute | solution.py:16
  13.1 1.5 %collective-permute-start.3 = (bf16[320,768]{1,0:T(8,128)(2,1)S(1)}, bf16[320,768]{1,0:T(8,128)(2,1)S(1)}, u32[]{:S(2)}, u32[]{:S(2)}) collective-permute-start(bf16[320,768]{1,0:T(8,128)(2,1)S(1)} %get-tuple-element.45), channel_id=1, source_target_pairs={{0,4},{1,5},{2,6},{3,7},{4,0},{5,1},{6,2},{7,3},{8,12},{9,13},{10,... | collective-permute-start | bytes 1474568 | tf_op jit(solution)/shard_map/ppermute | solution.py:16
  14.6 0.5 collective-permute-start.4
  15.1 0.7 collective-permute-start.5
  15.8 11.7 %collective-permute-done.5.refs_1_ = s32[1,320]{1,0:T(1,128)S(1)} collective-permute-done((s32[1,320]{1,0:T(1,128)S(1)}, s32[1,320]{1,0:T(1,128)S(1)}, u32[]{:S(2)}, u32[]{:S(2)}) %collective-permute-start.5) | collective-permute-done | bytes 1312 | tf_op jit(solution)/shard_map/ppermute | solution.py:16
  27.5 0.0 collective-permute-done.6.refs_2_
  27.6 0.7 shard_map.95
  28.2 1.6 %collective-permute-start.7 = (bf16[160,768]{1,0:T(8,128)(2,1)S(1)}, bf16[160,768]{1,0:T(8,128)(2,1)S(1)}, u32[]{:S(2)}, u32[]{:S(2)}) collective-permute-start(bf16[160,768]{1,0:T(8,128)(2,1)S(1)} %get-tuple-element.48), channel_id=1, source_target_pairs={{0,2},{1,3},{2,0},{3,1},{4,6},{5,7},{6,4},{7,5},{8,10},{9,11},{10,... | collective-permute-start | bytes 737288 | tf_op jit(solution)/shard_map/ppermute | solution.py:16
  29.9 0.0 collective-permute-start.10
  29.9 1.5 %collective-permute-start.8 = (bf16[160,768]{1,0:T(8,128)(2,1)S(1)}, bf16[160,768]{1,0:T(8,128)(2,1)S(1)}, u32[]{:S(2)}, u32[]{:S(2)}) collective-permute-start(bf16[160,768]{1,0:T(8,128)(2,1)S(1)} %get-tuple-element.49), channel_id=1, source_target_pairs={{0,4},{1,5},{2,6},{3,7},{4,0},{5,1},{6,2},{7,3},{8,12},{9,13},{10,... | collective-permute-start | bytes 737288 | tf_op jit(solution)/shard_map/ppermute | solution.py:16
  31.4 5.1 %collective-permute-done.3.refs_3_.refs_2_ = bf16[320,768]{1,0:T(8,128)(2,1)S(1)} collective-permute-done((bf16[320,768]{1,0:T(8,128)(2,1)S(1)}, bf16[320,768]{1,0:T(8,128)(2,1)S(1)}, u32[]{:S(2)}, u32[]{:S(2)}) %collective-permute-start.3) | collective-permute-done | bytes 491552 | tf_op jit(solution)/shard_map/ppermute | solution.py:16
  36.5 0.7 collective-permute-start.9
  37.1 0.1 collective-permute-done.4.refs_4_.refs_3_
  37.3 4.7 %shard_map.96 = (bf16[320,768]{1,0:T(8,128)(2,1)S(1)}, bf16[320,768]{1,0:T(8,128)(2,1)S(1)}, bf16[320,768]{1,0:T(8,128)(2,1)S(1)}, bf16[320,768]{1,0:T(8,128)(2,...) custom-call(bf16[160,768]{1,0:T(8,128)(2,1)S(1)} %get-tuple-element., ...), custom_call_target="tpu_custom_call" | custom-call | flops 1 | bytes 1 | tf_op jit(solution)/shard_map/pallas_call | solution.py:29
  42.0 4.9 %collective-permute-done.8.refs_3_.refs_7_.refs_6_ = bf16[160,768]{1,0:T(8,128)(2,1)S(1)} collective-permute-done((bf16[160,768]{1,0:T(8,128)(2,1)S(1)}, bf16[160,768]{1,0:T(8,128)(2,1)S(1)}, u32[]{:S(2)}, u32[]{:S(2)}) %collective-permute-start.8) | collective-permute-done | bytes 245792 | tf_op jit(solution)/shard_map/ppermute | solution.py:16
  46.9 2.9 %shard_map.97 = (bf16[160,768]{1,0:T(8,128)(2,1)S(1)}, bf16[160,768]{1,0:T(8,128)(2,1)S(1)}, bf16[160,768]{1,0:T(8,128)(2,1)S(1)}, bf16[160,768]{1,0:T(8,128)(2,...) custom-call(bf16[320,768]{1,0:T(8,128)(2,1)S(1)} %get-tuple-element., ...), custom_call_target="tpu_custom_call" | custom-call | flops 1 | bytes 1 | tf_op jit(solution)/shard_map/pallas_call | solution.py:29
  49.8 1.3 %collective-permute-start.14 = (bf16[160,768]{1,0:T(8,128)(2,1)S(1)}, bf16[160,768]{1,0:T(8,128)(2,1)S(1)}, u32[]{:S(2)}, u32[]{:S(2)}) collective-permute-start(bf16[160,768]{1,0:T(8,128)(2,1)S(1)} %get-tuple-element.61), channel_id=1, source_target_pairs={{0,2},{1,3},{2,0},{3,1},{4,6},{5,7},{6,4},{7,5},{8,10},{9,11},{10,... | collective-permute-start | bytes 737288 | tf_op jit(solution)/shard_map/ppermute | solution.py:16
  51.2 0.8 collective-permute-start.15
  51.9 1.4 %collective-permute-start.16 = (bf16[160,768]{1,0:T(8,128)(2,1)S(1)}, bf16[160,768]{1,0:T(8,128)(2,1)S(1)}, u32[]{:S(2)}, u32[]{:S(2)}) collective-permute-start(bf16[160,768]{1,0:T(8,128)(2,1)S(1)} %get-tuple-element.63), channel_id=1, source_target_pairs={{0,6},{1,7},{2,4},{3,5},{4,2},{5,3},{6,0},{7,1},{8,14},{9,15},{10,... | collective-permute-start | bytes 737288 | tf_op jit(solution)/shard_map/ppermute | solution.py:16
  53.4 0.7 shard_map.98
  54.1 1.3 %collective-permute-start.11 = (bf16[160,768]{1,0:T(8,128)(2,1)S(1)}, bf16[160,768]{1,0:T(8,128)(2,1)S(1)}, u32[]{:S(2)}, u32[]{:S(2)}) collective-permute-start(bf16[160,768]{1,0:T(8,128)(2,1)S(1)} %get-tuple-element.55), channel_id=1, source_target_pairs={{0,2},{1,3},{2,0},{3,1},{4,6},{5,7},{6,4},{7,5},{8,10},{9,11},{10,... | collective-permute-start | bytes 737288 | tf_op jit(solution)/shard_map/ppermute | solution.py:16
  55.4 0.8 collective-permute-start.12
  56.2 2.5 %collective-permute-done.14.refs_3_ = bf16[160,768]{1,0:T(8,128)(2,1)S(1)} collective-permute-done((bf16[160,768]{1,0:T(8,128)(2,1)S(1)}, bf16[160,768]{1,0:T(8,128)(2,1)S(1)}, u32[]{:S(2)}, u32[]{:S(2)}) %collective-permute-start.14) | collective-permute-done | bytes 245792 | tf_op jit(solution)/shard_map/ppermute | solution.py:16
  58.7 1.5 %collective-permute-start.13 = (bf16[160,768]{1,0:T(8,128)(2,1)S(1)}, bf16[160,768]{1,0:T(8,128)(2,1)S(1)}, u32[]{:S(2)}, u32[]{:S(2)}) collective-permute-start(bf16[160,768]{1,0:T(8,128)(2,1)S(1)} %get-tuple-element.57), channel_id=1, source_target_pairs={{0,6},{1,7},{2,4},{3,5},{4,2},{5,3},{6,0},{7,1},{8,14},{9,15},{10,... | collective-permute-start | bytes 737288 | tf_op jit(solution)/shard_map/ppermute | solution.py:16
  60.2 4.9 %collective-permute-done.15.refs_4_ = bf16[160,768]{1,0:T(8,128)(2,1)S(1)} collective-permute-done((bf16[160,768]{1,0:T(8,128)(2,1)S(1)}, bf16[160,768]{1,0:T(8,128)(2,1)S(1)}, u32[]{:S(2)}, u32[]{:S(2)}) %collective-permute-start.15) | collective-permute-done | bytes 245792 | tf_op jit(solution)/shard_map/ppermute | solution.py:16
  65.1 0.6 shard_map.99.refs_0_
  65.7 1.3 %collective-permute-start.17 = (bf16[320,768]{1,0:T(8,128)(2,1)S(1)}, bf16[320,768]{1,0:T(8,128)(2,1)S(1)}, u32[]{:S(2)}, u32[]{:S(2)}) collective-permute-start(bf16[320,768]{1,0:T(8,128)(2,1)S(1)} %shard_map.99.refs_0_), channel_id=1, source_target_pairs={{0,16},{8,24},{16,0},{24,8},{1,17},{9,25},{17,1},{25,9},{2,18},{10... | collective-permute-start | bytes 1474568 | tf_op jit(solution)/shard_map/ppermute | solution.py:16
  67.1 2.2 %collective-permute-done.11.refs_2_.refs_10_.refs_9_ = bf16[160,768]{1,0:T(8,128)(2,1)S(1)} collective-permute-done((bf16[160,768]{1,0:T(8,128)(2,1)S(1)}, bf16[160,768]{1,0:T(8,128)(2,1)S(1)}, u32[]{:S(2)}, u32[]{:S(2)}) %collective-permute-start.11) | collective-permute-done | bytes 245792 | tf_op jit(solution)/shard_map/ppermute | solution.py:16
  69.3 1.1 collective-permute-done.12.refs_3_.refs_11_.refs_10_
  70.4 3.2 %collective-permute-done.13.refs_4_.refs_12_.refs_11_ = bf16[160,768]{1,0:T(8,128)(2,1)S(1)} collective-permute-done((bf16[160,768]{1,0:T(8,128)(2,1)S(1)}, bf16[160,768]{1,0:T(8,128)(2,1)S(1)}, u32[]{:S(2)}, u32[]{:S(2)}) %collective-permute-start.13) | collective-permute-done | bytes 245792 | tf_op jit(solution)/shard_map/ppermute | solution.py:16
  73.6 2.5 %shard_map.100 = (bf16[160,768]{1,0:T(8,128)(2,1)S(1)}, bf16[160,768]{1,0:T(8,128)(2,1)S(1)}, bf16[160,768]{1,0:T(8,128)(2,1)S(1)}, bf16[160,768]{1,0:T(8,128)(2...) custom-call(bf16[320,768]{1,0:T(8,128)(2,1)S(1)} %shard_map.99.refs_0_, ...), custom_call_target="tpu_custom_call" | custom-call | flops 1 | bytes 1 | tf_op jit(solution)/shard_map/pallas_call | solution.py:29
  76.2 1.7 %collective-permute-start.18 = (bf16[160,768]{1,0:T(8,128)(2,1)S(1)}, bf16[160,768]{1,0:T(8,128)(2,1)S(1)}, u32[]{:S(2)}, u32[]{:S(2)}) collective-permute-start(bf16[160,768]{1,0:T(8,128)(2,1)S(1)} %get-tuple-element.68), channel_id=1, source_target_pairs={{0,2},{1,3},{2,0},{3,1},{4,6},{5,7},{6,4},{7,5},{8,10},{9,11},{10,... | collective-permute-start | bytes 737288 | tf_op jit(solution)/shard_map/ppermute | solution.py:16
  77.9 0.5 collective-permute-start.19
  78.4 1.3 %collective-permute-start.20 = (bf16[160,768]{1,0:T(8,128)(2,1)S(1)}, bf16[160,768]{1,0:T(8,128)(2,1)S(1)}, u32[]{:S(2)}, u32[]{:S(2)}) collective-permute-start(bf16[160,768]{1,0:T(8,128)(2,1)S(1)} %get-tuple-element.70), channel_id=1, source_target_pairs={{0,6},{1,7},{2,4},{3,5},{4,2},{5,3},{6,0},{7,1},{8,14},{9,15},{10,... | collective-permute-start | bytes 737288 | tf_op jit(solution)/shard_map/ppermute | solution.py:16
  79.7 5.4 %collective-permute-done.18.refs_3_ = bf16[160,768]{1,0:T(8,128)(2,1)S(1)} collective-permute-done((bf16[160,768]{1,0:T(8,128)(2,1)S(1)}, bf16[160,768]{1,0:T(8,128)(2,1)S(1)}, u32[]{:S(2)}, u32[]{:S(2)}) %collective-permute-start.18) | collective-permute-done | bytes 245792 | tf_op jit(solution)/shard_map/ppermute | solution.py:16
  85.1 4.5 %collective-permute-done.19.refs_4_ = bf16[160,768]{1,0:T(8,128)(2,1)S(1)} collective-permute-done((bf16[160,768]{1,0:T(8,128)(2,1)S(1)}, bf16[160,768]{1,0:T(8,128)(2,1)S(1)}, u32[]{:S(2)}, u32[]{:S(2)}) %collective-permute-start.19) | collective-permute-done | bytes 245792 | tf_op jit(solution)/shard_map/ppermute | solution.py:16
  89.7 0.6 shard_map.101.refs_0_
  90.3 2.6 %shard_map.102 = bf16[3072,256]{1,0:T(8,128)(2,1)} custom-call(bf16[320,768]{1,0:T(8,128)(2,1)S(1)} %shard_map.101.refs_0_, bf16[320,768]{1,0:T(8,128)(2,1)S(1)} %get-tuple-element.43.refs_0_.refs_1_, bf16[320,768]{1,0:T(8,128)(2,1)S(1)} %collective-permute-done.2.refs_2_.refs_1_, bf16[320,768]{1,0:T(8,128)(2,1)S(1)} %collective-permute-done.3.refs_3_.refs_2_, ...), custom_call_target="tpu_custom_call" | custom-call | flops 1 | bytes 1 | tf_op jit(solution)/shard_map/pallas_call | solution.py:29
  92.9 0.0 collective-permute-start.21
  92.9 0.4 collective-permute-start.22
  93.3 1.7 %collective-permute-start.23 = (bf16[320,768]{1,0:T(8,128)(2,1)S(1)}, bf16[320,768]{1,0:T(8,128)(2,1)S(1)}, u32[]{:S(2)}, u32[]{:S(2)}) collective-permute-start(bf16[320,768]{1,0:T(8,128)(2,1)S(1)} %get-tuple-element.77), channel_id=1, source_target_pairs={{0,4},{1,5},{2,6},{3,7},{4,0},{5,1},{6,2},{7,3},{8,12},{9,13},{10,... | collective-permute-start | bytes 1474568 | tf_op jit(solution)/shard_map/ppermute | solution.py:16
  95.0 1.4 %collective-permute-start.24 = (bf16[320,768]{1,0:T(8,128)(2,1)S(1)}, bf16[320,768]{1,0:T(8,128)(2,1)S(1)}, u32[]{:S(2)}, u32[]{:S(2)}) collective-permute-start(bf16[320,768]{1,0:T(8,128)(2,1)S(1)} %get-tuple-element.78), channel_id=1, source_target_pairs={{0,6},{1,7},{2,4},{3,5},{4,2},{5,3},{6,0},{7,1},{8,14},{9,15},{10,... | collective-permute-start | bytes 1474568 | tf_op jit(solution)/shard_map/ppermute | solution.py:16
  96.4 1.0 collective-permute-start.25
  97.4 3.7 %shard_map.103 = (bf16[768,512]{1,0:T(8,128)(2,1)}, bf16[512,768]{1,0:T(8,128)(2,1)}) custom-call(bf16[320,768]{1,0:T(8,128)(2,1)S(1)} %get-tuple-element.43.refs_0_.refs_1_, bf16[320,768]{1,0:T(8,128)(2,1)S(1)} %collective-permute-done.2.refs_2_.refs_1_, bf16[320,768]{1,0:T(8,128)(2,1)S(1)} %collective-permute-done.3.refs_3_.refs_2_, ...), custom_call_target="tpu_custom_call" | custom-call | flops 1 | bytes 1 | tf_op jit(solution)/shard_map/pallas_call | solution.py:29
  101.2 5.8 %collective-permute-done.22.refs_3_ = bf16[320,768]{1,0:T(8,128)(2,1)S(1)} collective-permute-done((bf16[320,768]{1,0:T(8,128)(2,1)S(1)}, bf16[320,768]{1,0:T(8,128)(2,1)S(1)}, u32[]{:S(2)}, u32[]{:S(2)}) %collective-permute-start.22) | collective-permute-done | bytes 491552 | tf_op jit(solution)/shard_map/ppermute | solution.py:16
  106.9 10.2 %collective-permute-done.23.refs_4_ = bf16[320,768]{1,0:T(8,128)(2,1)S(1)} collective-permute-done((bf16[320,768]{1,0:T(8,128)(2,1)S(1)}, bf16[320,768]{1,0:T(8,128)(2,1)S(1)}, u32[]{:S(2)}, u32[]{:S(2)}) %collective-permute-start.23) | collective-permute-done | bytes 491552 | tf_op jit(solution)/shard_map/ppermute | solution.py:16
  117.2 0.0 collective-permute-done.24.refs_5_
  117.2 1.1 copy-done.7
  118.3 1.6 %shard_map.104 = (bf16[320,768]{1,0:T(8,128)(2,1)}, bf16[320,768]{1,0:T(8,128)(2,1)S(1)}) custom-call(bf16[768,512]{1,0:T(8,128)(2,1)S(1)} %copy-done.7, s32[1,320]{1,0:T(1,128)S(1)} %copy-done.10, bf16[320,768]{1,0:T(8,128)(2,1)S(1)} %get-tuple-element.51.refs_0_.refs_2_, bf16[320,768]{1,0:T(8,128)(2,1)S(1)} %collective-permute-done.22.refs_3_, ...), custom_call_target="tpu_custom_call" | custom-call | flops 1 | bytes 1 | tf_op jit(solution)/shard_map/pallas_call | solution.py:29
  119.9 0.1 collective-permute-done.25.refs_2_
  120.0 1.0 copy-done.9
  121.1 0.9 shard_map.105
  (24 shorter events, 0.0 us)
Async XLA Ops:
  0.6 6.7 %collective-permute-start = (bf16[768,512]{1,0:T(8,128)(2,1)}, bf16[768,512]{1,0:T(8,128)(2,1)S(1)}, u32[]{:S(2)}, u32[]{:S(2)}) collective-permute-start(bf16[768,512]{1,0:T(8,128)(2,1)} %bitcast.6), channel_id=1, source_target_pairs={{0,1},{1,0},{2,3},{3,2},{4,5},{5,4},{6,7},{7,6},{8,9},{9,8},{10,11... | collective-permute-start | bytes 2359304 | tf_op jit(solution)/shard_map/ppermute | solution.py:16
  1.1 6.2 %collective-permute-start.1 = (bf16[512,768]{1,0:T(8,128)(2,1)}, bf16[512,768]{1,0:T(8,128)(2,1)S(1)}, u32[]{:S(2)}, u32[]{:S(2)}) collective-permute-start(bf16[512,768]{1,0:T(8,128)(2,1)} %bitcast.10), channel_id=1, source_target_pairs={{0,1},{1,0},{2,3},{3,2},{4,5},{5,4},{6,7},{7,6},{8,9},{9,8},{10,11... | collective-permute-start | bytes 2359304 | tf_op jit(solution)/shard_map/ppermute | solution.py:16
  1.2 26.3 %collective-permute-start.6 = (bf16[320,768]{1,0:T(8,128)(2,1)}, bf16[320,768]{1,0:T(8,128)(2,1)S(1)}, u32[]{:S(2)}, u32[]{:S(2)}) collective-permute-start(bf16[320,768]{1,0:T(8,128)(2,1)} %refs_3_.1), channel_id=1, source_target_pairs={{0,16},{8,24},{16,0},{24,8},{1,17},{9,25},{17,1},{25,9},{2,18},{10... | collective-permute-start | bytes 1474568 | tf_op jit(solution)/shard_map/ppermute | solution.py:16
  7.3 20.9 %copy-start = (bf16[768,512]{1,0:T(8,128)(2,1)}, bf16[768,512]{1,0:T(8,128)(2,1)S(1)}, u32[]{:S(2)}) copy-start(bf16[768,512]{1,0:T(8,128)(2,1)S(1)} %collective-permute-done.refs_0_.refs_6_.refs_8_) | copy-start | bytes 2359300
  7.3 1.3 %copy-start.5 = (bf16[320,768]{1,0:T(8,128)(2,1)S(1)}, bf16[320,768]{1,0:T(8,128)(2,1)}, u32[]{:S(2)}) copy-start(bf16[320,768]{1,0:T(8,128)(2,1)} %refs_4_.1) | copy-start | bytes 1474564
  8.7 1.0 copy-start.8
  9.7 0.7 copy-start.10
  10.4 17.9 %copy-start.2 = (bf16[512,768]{1,0:T(8,128)(2,1)}, bf16[512,768]{1,0:T(8,128)(2,1)S(1)}, u32[]{:S(2)}) copy-start(bf16[512,768]{1,0:T(8,128)(2,1)S(1)} %collective-permute-done.1.refs_1_.refs_8_.refs_10_) | copy-start | bytes 2359300
  10.4 17.2 %copy-start.6 = (bf16[320,768]{1,0:T(8,128)(2,1)S(1)}, bf16[320,768]{1,0:T(8,128)(2,1)}, u32[]{:S(2)}) copy-start(bf16[320,768]{1,0:T(8,128)(2,1)} %refs_4_.1) | copy-start | bytes 1474564
  11.6 18.3 %collective-permute-start.2 = (bf16[320,768]{1,0:T(8,128)(2,1)S(1)}, bf16[320,768]{1,0:T(8,128)(2,1)S(1)}, u32[]{:S(2)}, u32[]{:S(2)}) collective-permute-start(bf16[320,768]{1,0:T(8,128)(2,1)S(1)} %get-tuple-element.44), channel_id=1, source_target_pairs={{0,2},{1,3},{2,0},{3,1},{4,6},{5,7},{6,4},{7,5},{8,10},{9,11},{10,... | collective-permute-start | bytes 1474568 | tf_op jit(solution)/shard_map/ppermute | solution.py:16
  13.1 23.3 %collective-permute-start.3 = (bf16[320,768]{1,0:T(8,128)(2,1)S(1)}, bf16[320,768]{1,0:T(8,128)(2,1)S(1)}, u32[]{:S(2)}, u32[]{:S(2)}) collective-permute-start(bf16[320,768]{1,0:T(8,128)(2,1)S(1)} %get-tuple-element.45), channel_id=1, source_target_pairs={{0,4},{1,5},{2,6},{3,7},{4,0},{5,1},{6,2},{7,3},{8,12},{9,13},{10,... | collective-permute-start | bytes 1474568 | tf_op jit(solution)/shard_map/ppermute | solution.py:16
  14.6 22.6 %collective-permute-start.4 = (bf16[320,768]{1,0:T(8,128)(2,1)S(1)}, bf16[320,768]{1,0:T(8,128)(2,1)S(1)}, u32[]{:S(2)}, u32[]{:S(2)}) collective-permute-start(bf16[320,768]{1,0:T(8,128)(2,1)S(1)} %get-tuple-element.46), channel_id=1, source_target_pairs={{0,6},{1,7},{2,4},{3,5},{4,2},{5,3},{6,0},{7,1},{8,14},{9,15},{10,... | collective-permute-start | bytes 1474568 | tf_op jit(solution)/shard_map/ppermute | solution.py:16
  15.1 12.4 %collective-permute-start.5 = (s32[1,320]{1,0:T(1,128)S(1)}, s32[1,320]{1,0:T(1,128)S(1)}, u32[]{:S(2)}, u32[]{:S(2)}) collective-permute-start(s32[1,320]{1,0:T(1,128)S(1)} %copy-done.10), channel_id=1, source_target_pairs={{0,16},{8,24},{16,0},{24,8},{1,17},{9,25},{17,1},{25,9},{2,18},{10... | collective-permute-start | bytes 3848 | tf_op jit(solution)/shard_map/ppermute | solution.py:16
  28.2 13.7 %collective-permute-start.7 = (bf16[160,768]{1,0:T(8,128)(2,1)S(1)}, bf16[160,768]{1,0:T(8,128)(2,1)S(1)}, u32[]{:S(2)}, u32[]{:S(2)}) collective-permute-start(bf16[160,768]{1,0:T(8,128)(2,1)S(1)} %get-tuple-element.48), channel_id=1, source_target_pairs={{0,2},{1,3},{2,0},{3,1},{4,6},{5,7},{6,4},{7,5},{8,10},{9,11},{10,... | collective-permute-start | bytes 737288 | tf_op jit(solution)/shard_map/ppermute | solution.py:16
  29.9 23.5 %collective-permute-start.10 = (bf16[320,768]{1,0:T(8,128)(2,1)S(1)}, bf16[320,768]{1,0:T(8,128)(2,1)S(1)}, u32[]{:S(2)}, u32[]{:S(2)}) collective-permute-start(bf16[320,768]{1,0:T(8,128)(2,1)S(1)} %get-tuple-element.53), channel_id=1, source_target_pairs={{0,16},{8,24},{16,0},{24,8},{1,17},{9,25},{17,1},{25,9},{2,18},{10... | collective-permute-start | bytes 1474568 | tf_op jit(solution)/shard_map/ppermute | solution.py:16
  29.9 17.0 %collective-permute-start.8 = (bf16[160,768]{1,0:T(8,128)(2,1)S(1)}, bf16[160,768]{1,0:T(8,128)(2,1)S(1)}, u32[]{:S(2)}, u32[]{:S(2)}) collective-permute-start(bf16[160,768]{1,0:T(8,128)(2,1)S(1)} %get-tuple-element.49), channel_id=1, source_target_pairs={{0,4},{1,5},{2,6},{3,7},{4,0},{5,1},{6,2},{7,3},{8,12},{9,13},{10,... | collective-permute-start | bytes 737288 | tf_op jit(solution)/shard_map/ppermute | solution.py:16
  36.5 10.4 %collective-permute-start.9 = (bf16[160,768]{1,0:T(8,128)(2,1)S(1)}, bf16[160,768]{1,0:T(8,128)(2,1)S(1)}, u32[]{:S(2)}, u32[]{:S(2)}) collective-permute-start(bf16[160,768]{1,0:T(8,128)(2,1)S(1)} %get-tuple-element.50), channel_id=1, source_target_pairs={{0,6},{1,7},{2,4},{3,5},{4,2},{5,3},{6,0},{7,1},{8,14},{9,15},{10,... | collective-permute-start | bytes 737288 | tf_op jit(solution)/shard_map/ppermute | solution.py:16
  37.3 9.6 %copy-start.1 = (bf16[768,512]{1,0:T(8,128)(2,1)S(1)}, bf16[768,512]{1,0:T(8,128)(2,1)}, u32[]{:S(2)}) copy-start(bf16[768,512]{1,0:T(8,128)(2,1)} %copy-done) | copy-start | bytes 2359300
  37.3 9.6 %copy-start.3 = (bf16[1,768,512]{2,1,0:T(8,128)(2,1)S(1)}, bf16[1,768,512]{2,1,0:T(8,128)(2,1)}, u32[]{:S(2)}) copy-start(bf16[1,768,512]{2,1,0:T(8,128)(2,1)} %param.9) | copy-start | bytes 2359300
  37.3 9.6 %copy-start.4 = (bf16[1,512,768]{2,1,0:T(8,128)(2,1)S(1)}, bf16[1,512,768]{2,1,0:T(8,128)(2,1)}, u32[]{:S(2)}) copy-start(bf16[1,512,768]{2,1,0:T(8,128)(2,1)} %param.10) | copy-start | bytes 2359300
  49.8 8.9 %collective-permute-start.14 = (bf16[160,768]{1,0:T(8,128)(2,1)S(1)}, bf16[160,768]{1,0:T(8,128)(2,1)S(1)}, u32[]{:S(2)}, u32[]{:S(2)}) collective-permute-start(bf16[160,768]{1,0:T(8,128)(2,1)S(1)} %get-tuple-element.61), channel_id=1, source_target_pairs={{0,2},{1,3},{2,0},{3,1},{4,6},{5,7},{6,4},{7,5},{8,10},{9,11},{10,... | collective-permute-start | bytes 737288 | tf_op jit(solution)/shard_map/ppermute | solution.py:16
  51.2 13.9 %collective-permute-start.15 = (bf16[160,768]{1,0:T(8,128)(2,1)S(1)}, bf16[160,768]{1,0:T(8,128)(2,1)S(1)}, u32[]{:S(2)}, u32[]{:S(2)}) collective-permute-start(bf16[160,768]{1,0:T(8,128)(2,1)S(1)} %get-tuple-element.62), channel_id=1, source_target_pairs={{0,4},{1,5},{2,6},{3,7},{4,0},{5,1},{6,2},{7,3},{8,12},{9,13},{10,... | collective-permute-start | bytes 737288 | tf_op jit(solution)/shard_map/ppermute | solution.py:16
  51.9 13.2 %collective-permute-start.16 = (bf16[160,768]{1,0:T(8,128)(2,1)S(1)}, bf16[160,768]{1,0:T(8,128)(2,1)S(1)}, u32[]{:S(2)}, u32[]{:S(2)}) collective-permute-start(bf16[160,768]{1,0:T(8,128)(2,1)S(1)} %get-tuple-element.63), channel_id=1, source_target_pairs={{0,6},{1,7},{2,4},{3,5},{4,2},{5,3},{6,0},{7,1},{8,14},{9,15},{10,... | collective-permute-start | bytes 737288 | tf_op jit(solution)/shard_map/ppermute | solution.py:16
  54.1 15.2 %collective-permute-start.11 = (bf16[160,768]{1,0:T(8,128)(2,1)S(1)}, bf16[160,768]{1,0:T(8,128)(2,1)S(1)}, u32[]{:S(2)}, u32[]{:S(2)}) collective-permute-start(bf16[160,768]{1,0:T(8,128)(2,1)S(1)} %get-tuple-element.55), channel_id=1, source_target_pairs={{0,2},{1,3},{2,0},{3,1},{4,6},{5,7},{6,4},{7,5},{8,10},{9,11},{10,... | collective-permute-start | bytes 737288 | tf_op jit(solution)/shard_map/ppermute | solution.py:16
  55.4 15.0 %collective-permute-start.12 = (bf16[160,768]{1,0:T(8,128)(2,1)S(1)}, bf16[160,768]{1,0:T(8,128)(2,1)S(1)}, u32[]{:S(2)}, u32[]{:S(2)}) collective-permute-start(bf16[160,768]{1,0:T(8,128)(2,1)S(1)} %get-tuple-element.56), channel_id=1, source_target_pairs={{0,4},{1,5},{2,6},{3,7},{4,0},{5,1},{6,2},{7,3},{8,12},{9,13},{10,... | collective-permute-start | bytes 737288 | tf_op jit(solution)/shard_map/ppermute | solution.py:16
  58.7 14.9 %collective-permute-start.13 = (bf16[160,768]{1,0:T(8,128)(2,1)S(1)}, bf16[160,768]{1,0:T(8,128)(2,1)S(1)}, u32[]{:S(2)}, u32[]{:S(2)}) collective-permute-start(bf16[160,768]{1,0:T(8,128)(2,1)S(1)} %get-tuple-element.57), channel_id=1, source_target_pairs={{0,6},{1,7},{2,4},{3,5},{4,2},{5,3},{6,0},{7,1},{8,14},{9,15},{10,... | collective-permute-start | bytes 737288 | tf_op jit(solution)/shard_map/ppermute | solution.py:16
  65.7 24.0 %collective-permute-start.17 = (bf16[320,768]{1,0:T(8,128)(2,1)S(1)}, bf16[320,768]{1,0:T(8,128)(2,1)S(1)}, u32[]{:S(2)}, u32[]{:S(2)}) collective-permute-start(bf16[320,768]{1,0:T(8,128)(2,1)S(1)} %shard_map.99.refs_0_), channel_id=1, source_target_pairs={{0,16},{8,24},{16,0},{24,8},{1,17},{9,25},{17,1},{25,9},{2,18},{10... | collective-permute-start | bytes 1474568 | tf_op jit(solution)/shard_map/ppermute | solution.py:16
  76.2 9.0 %collective-permute-start.18 = (bf16[160,768]{1,0:T(8,128)(2,1)S(1)}, bf16[160,768]{1,0:T(8,128)(2,1)S(1)}, u32[]{:S(2)}, u32[]{:S(2)}) collective-permute-start(bf16[160,768]{1,0:T(8,128)(2,1)S(1)} %get-tuple-element.68), channel_id=1, source_target_pairs={{0,2},{1,3},{2,0},{3,1},{4,6},{5,7},{6,4},{7,5},{8,10},{9,11},{10,... | collective-permute-start | bytes 737288 | tf_op jit(solution)/shard_map/ppermute | solution.py:16
  77.9 11.8 %collective-permute-start.19 = (bf16[160,768]{1,0:T(8,128)(2,1)S(1)}, bf16[160,768]{1,0:T(8,128)(2,1)S(1)}, u32[]{:S(2)}, u32[]{:S(2)}) collective-permute-start(bf16[160,768]{1,0:T(8,128)(2,1)S(1)} %get-tuple-element.69), channel_id=1, source_target_pairs={{0,4},{1,5},{2,6},{3,7},{4,0},{5,1},{6,2},{7,3},{8,12},{9,13},{10,... | collective-permute-start | bytes 737288 | tf_op jit(solution)/shard_map/ppermute | solution.py:16
  78.4 11.3 %collective-permute-start.20 = (bf16[160,768]{1,0:T(8,128)(2,1)S(1)}, bf16[160,768]{1,0:T(8,128)(2,1)S(1)}, u32[]{:S(2)}, u32[]{:S(2)}) collective-permute-start(bf16[160,768]{1,0:T(8,128)(2,1)S(1)} %get-tuple-element.70), channel_id=1, source_target_pairs={{0,6},{1,7},{2,4},{3,5},{4,2},{5,3},{6,0},{7,1},{8,14},{9,15},{10,... | collective-permute-start | bytes 737288 | tf_op jit(solution)/shard_map/ppermute | solution.py:16
  92.9 4.5 %collective-permute-start.21 = (bf16[3072,256]{1,0:T(8,128)(2,1)}, bf16[3072,256]{1,0:T(8,128)(2,1)}, u32[]{:S(2)}, u32[]{:S(2)}) collective-permute-start(bf16[3072,256]{1,0:T(8,128)(2,1)} %shard_map.102), channel_id=1, source_target_pairs={{0,1},{1,0},{2,3},{3,2},{4,5},{5,4},{6,7},{7,6},{8,9},{9,8},{10,11... | collective-permute-start | bytes 4718600 | tf_op jit(solution)/shard_map/ppermute | solution.py:16
  92.9 14.0 %collective-permute-start.22 = (bf16[320,768]{1,0:T(8,128)(2,1)S(1)}, bf16[320,768]{1,0:T(8,128)(2,1)S(1)}, u32[]{:S(2)}, u32[]{:S(2)}) collective-permute-start(bf16[320,768]{1,0:T(8,128)(2,1)S(1)} %get-tuple-element.76), channel_id=1, source_target_pairs={{0,2},{1,3},{2,0},{3,1},{4,6},{5,7},{6,4},{7,5},{8,10},{9,11},{10,... | collective-permute-start | bytes 1474568 | tf_op jit(solution)/shard_map/ppermute | solution.py:16
  93.3 23.9 %collective-permute-start.23 = (bf16[320,768]{1,0:T(8,128)(2,1)S(1)}, bf16[320,768]{1,0:T(8,128)(2,1)S(1)}, u32[]{:S(2)}, u32[]{:S(2)}) collective-permute-start(bf16[320,768]{1,0:T(8,128)(2,1)S(1)} %get-tuple-element.77), channel_id=1, source_target_pairs={{0,4},{1,5},{2,6},{3,7},{4,0},{5,1},{6,2},{7,3},{8,12},{9,13},{10,... | collective-permute-start | bytes 1474568 | tf_op jit(solution)/shard_map/ppermute | solution.py:16
  95.0 22.2 %collective-permute-start.24 = (bf16[320,768]{1,0:T(8,128)(2,1)S(1)}, bf16[320,768]{1,0:T(8,128)(2,1)S(1)}, u32[]{:S(2)}, u32[]{:S(2)}) collective-permute-start(bf16[320,768]{1,0:T(8,128)(2,1)S(1)} %get-tuple-element.78), channel_id=1, source_target_pairs={{0,6},{1,7},{2,4},{3,5},{4,2},{5,3},{6,0},{7,1},{8,14},{9,15},{10,... | collective-permute-start | bytes 1474568 | tf_op jit(solution)/shard_map/ppermute | solution.py:16
  96.4 23.6 %collective-permute-start.25 = (bf16[320,768]{1,0:T(8,128)(2,1)S(1)}, bf16[320,768]{1,0:T(8,128)(2,1)S(1)}, u32[]{:S(2)}, u32[]{:S(2)}) collective-permute-start(bf16[320,768]{1,0:T(8,128)(2,1)S(1)} %shard_map.101.refs_0_), channel_id=1, source_target_pairs={{0,16},{8,24},{16,0},{24,8},{1,17},{9,25},{17,1},{25,9},{2,18},{10... | collective-permute-start | bytes 1474568 | tf_op jit(solution)/shard_map/ppermute | solution.py:16
  117.2 1.1 copy-start.7
  120.0 1.0 copy-start.9

commit v3 on v2

--- a/solution.py
+++ b/solution.py
@@ -20,7 +20,7 @@
     return lax.dot_general(a, b, (contract, ((), ())), preferred_element_type=F32)
 
 
-def call(body, out_shape, *args, after=()):
+def call(body, out_shape, *args, after=(), space=pl.ANY, flops=1):
     waits = len(after)
 
     def kernel(*refs):
@@ -29,9 +29,9 @@
     return pl.pallas_call(
         kernel,
         out_shape=out_shape,
-        in_specs=[pl.BlockSpec(memory_space=pl.ANY)] * waits
+        in_specs=[pl.BlockSpec(memory_space=space)] * waits
         + [pl.BlockSpec(memory_space=pltpu.VMEM)] * len(args),
-        cost_estimate=pl.CostEstimate(flops=1, bytes_accessed=1, transcendentals=0),
+        cost_estimate=pl.CostEstimate(flops=flops, bytes_accessed=1, transcendentals=0),
         compiler_params=pltpu.CompilerParams(vmem_limit_bytes=VMEM_LIMIT),
     )(*after, *args)
 
@@ -47,10 +47,27 @@
     return jax.ShapeDtypeStruct((rows, columns), dtype)
 
 
-def slot_positions(route_row, device, experts, capacity):
-    local = route_row.shape[1]
-
-    def body(device_ref, route_ref, slot_ref):
+def prepare(device, route_row, gate, tokens, cotangent, blocks, capacity):
+    local, width = tokens.shape
+    experts = 2 * blocks
+    pieces = 4
+    piece = local // pieces
+
+    def body(device_ref, route_ref, gate_ref, token_ref, cotangent_ref, slot_ref, *refs):
+        token_out, scaled_out, cotangent_here, sems = refs
+        copies = [
+            pltpu.make_async_copy(
+                source.at[number * piece : (number + 1) * piece],
+                target.at[number * piece : (number + 1) * piece],
+                sems.at[array * pieces + number],
+            )
+            for array, (source, target) in enumerate(
+                ((token_ref, token_out), (cotangent_ref, cotangent_here))
+            )
+            for number in range(pieces)
+        ]
+        for copy in copies:
+            copy.start()
         route = route_ref[...]
         expert = lax.broadcasted_iota(jnp.int32, (experts, local), 0)
         choose = jnp.where(expert == route, 1.0, 0.0)
@@ -60,40 +77,53 @@
         running = dot(choose.astype(BF16), upto, ((1,), (0,)))
         rank = jnp.sum(running * choose, axis=0, keepdims=True) - 1.0
         slot_ref[...] = (route ^ device_ref[0]) * capacity + rank.astype(jnp.int32)
+        factor = column(gate_ref[...].reshape(1, local))
+        for copy in copies:
+            copy.wait()
+        scaled_out[...] = (factor * cotangent_here[...].astype(F32)).astype(BF16)
 
     return pl.pallas_call(
         body,
-        out_shape=shape(1, local, jnp.int32),
-        in_specs=[
-            pl.BlockSpec(memory_space=pltpu.SMEM),
-            pl.BlockSpec(memory_space=pltpu.VMEM),
+        out_shape=[shape(1, local, jnp.int32), shape(local, width), shape(local, width)],
+        in_specs=[pl.BlockSpec(memory_space=pltpu.SMEM)]
+        + [pl.BlockSpec(memory_space=pltpu.VMEM)] * 2
+        + [pl.BlockSpec(memory_space=pltpu.HBM)] * 2,
+        out_specs=[pl.BlockSpec(memory_space=pltpu.VMEM)] * 3,
+        scratch_shapes=[
+            pltpu.VMEM((local, width), BF16),
+            pltpu.SemaphoreType.DMA((2 * pieces,)),
         ],
-    )(device, route_row)
-
-
-def dispatch(slots, tokens, scaling, blocks, rows, mode, after=()):
-    local, width = tokens.shape
-    placed_arrays = 2 if mode == "place" else 1
-
-    def body(slot_ref, token_ref, *refs):
-        outs = refs[len(scaling) :]
-        values = [token_ref[...]]
-        if scaling:
-            scaled = column(refs[0][...]) * refs[1][...].astype(F32)
-            values.append(scaled.astype(BF16))
+        cost_estimate=pl.CostEstimate(flops=1, bytes_accessed=1, transcendentals=0),
+        compiler_params=pltpu.CompilerParams(vmem_limit_bytes=VMEM_LIMIT),
+    )(
+        device,
+        route_row,
+        gate,
+        pltpu.with_memory_space_constraint(tokens, pltpu.HBM),
+        pltpu.with_memory_space_constraint(cotangent, pltpu.HBM),
+    )
+
+
+def dispatch(slots, arrays, blocks, rows, given=None, after=()):
+    local, width = arrays[0].shape
+    several = len(arrays)
+    more = () if given is None else (given,)
+
+    def body(slot_ref, *refs):
+        values, outs = refs[:several], refs[several + len(more) :]
         number = lax.broadcasted_iota(jnp.int32, (blocks * rows, local), 0)
         placing = jnp.where(number == slot_ref[...], 1.0, 0.0).astype(BF16)
-        for which in range(placed_arrays):
-            placed = dot(placing, values[which], ((1,), (0,))).astype(BF16)
+        for which in range(several):
+            placed = dot(placing, values[which][...], ((1,), (0,))).astype(BF16)
             for block in range(blocks):
                 outs[block][which * rows : (which + 1) * rows, :] = placed[
                     block * rows : (block + 1) * rows
                 ]
-        if mode == "give":
-            outs[blocks][...] = values[1]
-
-    shapes = [shape(placed_arrays * rows, width)] * blocks + [shape(local, width)] * (mode == "give")
-    return call(body, shapes, slots, tokens, *scaling, after=after)
+        if more:
+            outs[blocks][...] = refs[several][...]
+
+    shapes = [shape(several * rows, width)] * blocks + [shape(local, width)] * len(more)
+    return call(body, shapes, slots, *arrays, *more, after=after)
 
 
 def picked(slot_row, refs, base, rows):
@@ -109,7 +139,7 @@
     rows, width = parts[0].shape
 
     def body(slot_ref, *refs):
-        refs[-1][...] = picked(slot_ref[...], refs[:blocks], 0, rows).astype(BF16)
+        refs[blocks][...] = picked(slot_ref[...], refs[:blocks], 0, rows).astype(BF16)
 
     return call(body, shape(slots.shape[1], width), slots, *parts, after=after)
 
@@ -122,10 +152,19 @@
     def body(slot_ref, *refs):
         parts, (other_ref, gate_ref, mixed_ref, back_ref) = refs[:blocks], refs[blocks:]
         out = picked(slot_ref[...], parts, 0, rows) + other_ref[...].astype(F32)
-        mixed_ref[...] = (column(gate_ref[...]) * out.astype(BF16).astype(F32)).astype(BF16)
+        mixed_ref[...] = (column(gate_ref[...].reshape(1, local)) * out.astype(BF16).astype(F32)).astype(BF16)
         back_ref[...] = picked(slot_ref[...], parts, rows, rows).astype(BF16)
 
-    return call(body, [shape(local, width)] * 2, slots, *parts, other_out, gate, after=after)
+    return call(
+        body,
+        [shape(local, width)] * 2,
+        slots,
+        *parts,
+        other_out,
+        gate,
+        after=after,
+        space=pltpu.HBM,
+    )
 
 
 def rows_of(refs, which, capacity, base=0):
@@ -223,45 +262,44 @@
     return [array[:, start : start + size] for start in range(0, array.shape[1], size)]
 
 
-def weight_gradients(which, own, pair_x, pair_c, hiddens, hidden_grads, capacity, peer=None, after=()):
+def weight_gradients(which, own, pair_x, pair_c, hiddens, hidden_grads, capacity, dtype, after=(), flops=1):
     blocks = len(pair_x)
     width = pair_x[0].shape[1]
     half = hiddens[0].shape[1]
     size = math.gcd(width, half)
-    more = () if peer is None else (peer,)
 
     def body(*refs):
         own, refs = refs[:blocks], refs[blocks:]
         tokens, grads, refs = refs[:blocks], refs[blocks : 2 * blocks], refs[2 * blocks :]
-        hidden, hidden_grad, refs = refs[:2], refs[2:4], refs[4:]
+        hidden, hidden_grad, out = refs[:2], refs[2:4], refs[4]
         both = [jnp.concatenate([ref[...] for ref in pair], axis=0) for pair in (hidden, hidden_grad)]
         rows = [rows_of(own, which, capacity), rows_of(tokens, which, capacity)]
         up = dot(jnp.concatenate(rows, axis=0), both[1], ((0,), (0,)))
         rows = [rows_of(own, which, capacity, 2 * capacity), rows_of(grads, which, capacity)]
         down = dot(both[0], jnp.concatenate(rows, axis=0), ((0,), (0,)))
         start = 0
-        for number, result in enumerate((up, down)):
-            for place, panel in enumerate(panels(result, size)):
-                stop = start + panel.shape[0]
-                if peer is None:
-                    refs[0][start:stop, :] = panel.astype(BF16)
-                else:
-                    total = panel + refs[0][start:stop, :].astype(F32)
-                    refs[1 + number][:, place * size : (place + 1) * size] = total.astype(BF16)
+        for result in (up, down):
+            for panel in panels(result, size):
+                out[start : start + panel.shape[0], :] = panel.astype(dtype)
+                start += panel.shape[0]
+
+    shapes = shape(2 * width * half // size, size, dtype)
+    return call(body, shapes, *own, *pair_x, *pair_c, *hiddens, *hidden_grads, after=after, flops=flops)
+
+
+def joined(terms, peer, width, half, after=()):
+    size = terms.shape[1]
+
+    def body(term_ref, peer_ref, up_ref, down_ref):
+        start = 0
+        for out in (up_ref, down_ref):
+            for place in range(out.shape[1] // size):
+                stop = start + out.shape[0]
+                total = term_ref[start:stop, :] + peer_ref[start:stop, :].astype(F32)
+                out[:, place * size : (place + 1) * size] = total.astype(BF16)
                 start = stop
 
-    if peer is None:
-        shapes = shape(2 * width * half // size, size)
-    else:
-        shapes = [shape(width, half), shape(half, width)]
-    return call(body, shapes, *own, *pair_x, *pair_c, *hiddens, *hidden_grads, *more, after=after)
-
-
-def added(one, other, after=()):
-    def body(one_ref, other_ref, out):
-        out[...] = (one_ref[...].astype(F32) + other_ref[...].astype(F32)).astype(BF16)
-
-    return call(body, shape(*one.shape), one, other, after=after)
+    return call(body, [shape(width, half), shape(half, width)], terms, peer, after=after)
 
 
 def spread(parts):
@@ -280,19 +318,17 @@
         return exchange(array, "section", opposite)
 
     rows = 2 * capacity
-    gate = gate_prob.reshape(1, local)
     pair_tokens = across(tokens)
-    slots = slot_positions(routing.reshape(1, local), device, experts, capacity)
-    pair_slots = across(slots)
     ups = (up_weight[0], exchange(up_weight[0], "expert", 1))
     downs = (down_weight[0], exchange(down_weight[0], "expert", 1))
 
-    scaling = (gate, cotangent)
-    sent = dispatch(slots, tokens, scaling, blocks, rows, "place", after=(ups[1], downs[1]))
+    slots, tokens, scaled = prepare(
+        device, routing.reshape(1, local), gate_prob, tokens, cotangent, blocks, capacity
+    )
+    sent = dispatch(slots, (tokens, scaled), blocks, rows, after=(ups[1], downs[1]))
     own = spread(sent)
-    *sent, scaled = dispatch(
-        pair_slots, pair_tokens, scaling, blocks, rows, "give", after=(sent[0],)
-    )
+    pair_slots = across(slots)
+    *sent, scaled = dispatch(pair_slots, (pair_tokens,), blocks, rows, scaled, after=(sent[0],))
     pair_x = spread(sent)
     pair_scaled = across(scaled)
     own_sent, own_hidden, own_hidden_grad = both_ways(
@@ -300,14 +336,14 @@
     )
     sent, pair_hidden, pair_slope = forward(pair_x, ups, downs, capacity, after=(own_sent[0],))
     back = spread(sent)
-    sent = dispatch(pair_slots, pair_scaled, (), blocks, rows, "", after=(sent[0],))
+    sent = dispatch(pair_slots, (pair_scaled,), blocks, rows, after=(sent[0],))
     pair_c = spread(sent)
     term = collect(pair_slots, back, after=(sent[0],))
     other_out = across(term)
     sent, pair_hidden_grad = backward(pair_c, pair_slope, ups, downs, capacity, after=(term,))
     back = spread(sent)
 
-    def gradients(which, peer, after):
+    def gradients(which, dtype, after, flops):
         return weight_gradients(
             which,
             own,
@@ -316,18 +352,20 @@
             (own_hidden[which], pair_hidden[which]),
             (own_hidden_grad[which], pair_hidden_grad[which]),
             capacity,
-            peer,
+            dtype,
             after,
+            flops,
         )
 
     term = collect(pair_slots, back, after=(other_out,))
     other_back = across(term)
-    give = gradients(1, None, (term,))
+    own_back = spread(own_sent)
+    give = gradients(1, BF16, (term,), 1 * 10**9)
+    keep = gradients(0, F32, (give,), 30 * 10**9)
     peer = exchange(give, "expert", 1)
-    own_back = spread(own_sent)
-    grad_up, grad_down = gradients(0, peer, ())
-    mixed, own_term = collect_own(slots, own_back, other_out, gate, after=(grad_up,))
-    token_grad = added(own_term, other_back, after=(mixed,))
+    grad_up, grad_down = joined(keep, peer, *ups[0].shape)
+    mixed, own_term = collect_own(slots, own_back, other_out, gate_prob, after=(pltpu.with_memory_space_constraint(grad_up, pltpu.HBM),))
+    token_grad = (own_term.astype(F32) + other_back.astype(F32)).astype(BF16)
     return (mixed, token_grad, grad_up[None], grad_down[None])
 
 

time: 122 us -> 110 us (0.902)
  waiting for transfers between devices: 61.9 us -> 51.4 us
  local copies, waits for them, and re-layouts: 5.89 us -> 3.28 us
    ppermute x26, waiting for transfers between devices: 61.9 us -> 51.4 us  [exchange(): lax.ppermute(array, axis, [(i, i ^ flip) for i in range(lax.axis_size(axi...]
    unnamed x22 -> x18, local copies, waits for them, and re-layouts: 5.2 us -> 3.28 us
  transfers between devices with their start and end apart: 26 -> 26, of which waited for: 14 -> 16; matrix products, arithmetic and copies ran while one was open for 1% -> 0% of each run, Pallas kernels for 16% -> 22%
where the time goes in v3:
time: 110 us; the launch traced here: 109 us
  waiting for transfers between devices  51.4 us (47%)
  starting transfers between devices  29.1 us (26%)
  Pallas kernels  24 us (22%)
  local copies, waits for them, and re-layouts  3.28 us (3%)
    ppermute x26, waiting for transfers between devices, exchange(): lax.ppermute(array, axis, [(i, i ^ flip) for i in range(lax.axis_size(axi...  51.4 us
    ppermute x26, starting transfers between devices, exchange(): lax.ppermute(array, axis, [(i, i ^ flip) for i in range(lax.axis_size(axi...  29.1 us
    pallas_call x12, Pallas kernels, call(): pl.pallas_call(kernel, out_shape=out_shape, in_specs=[pl.BlockSpec(memory...  22.5 us
    unnamed x18, local copies, waits for them, and re-layouts  3.28 us
  transfers between devices with their start and end apart: 26, of which 16 were waited for; matrix products, arithmetic and copies ran while one was open for 0% of the time, Pallas kernels for 22%

profile of v3, /device:TPU:0, one launch (start us, length us, event | category | flops | bytes accessed | tf_op | source)
XLA Modules:
  0.0 109.4 jit_solution(11915561513483379645)
XLA Ops:
  0.6 0.5 collective-permute-start
  1.1 0.1 collective-permute-start.1
  1.2 4.0 %collective-permute-start.3 = (bf16[320,768]{1,0:T(8,128)(2,1)}, bf16[320,768]{1,0:T(8,128)(2,1)S(1)}, u32[]{:S(2)}, u32[]{:S(2)}) collective-permute-start(bf16[320,768]{1,0:T(8,128)(2,1)} %token_ref.1), channel_id=1, source_target_pairs={{0,16},{8,24},{16,0},{24,8},{1,17},{9,25},{17,1},{25,9},{2,18},{10... | collective-permute-start | bytes 1474568 | tf_op jit(solution)/shard_map/ppermute | solution.py:16
  5.2 0.7 copy-done.6
  5.9 0.7 copy-done.8
  6.6 1.4 %shard_map.93 = (s32[1,320]{1,0:T(1,128)S(1)}, bf16[320,768]{1,0:T(8,128)(2,1)S(1)}, bf16[320,768]{1,0:T(8,128)(2,1)S(1)}) custom-call(s32[1]{0:T(128)} %bitcast.2.device_ref, s32[1,320]{1,0:T(1,128)S(1)} %bitcast.14, f32[320]{0:T(512)S(1)} %copy-done.6, bf16[320,768]{1,0:T(8,128)(2,1)} %token_ref.1, bf16[320,768]{1,0:T(8,128)(2,1)} %cotangent_ref.1), custom_call_target="tpu_custom_call" | custom-call | flops 1 | bytes 1 | tf_op jit(solution)/shard_map/pallas_call | solution.py:85
  8.1 0.0 copy-start
  8.1 0.0 collective-permute-done.1.refs_1_.refs_8_.refs_10_
  8.1 0.0 copy-start.2
  8.1 1.2 %shard_map.94 = (bf16[320,768]{1,0:T(8,128)(2,1)S(1)}, bf16[320,768]{1,0:T(8,128)(2,1)S(1)}, bf16[320,768]{1,0:T(8,128)(2,1)S(1)}, bf16[320,768]{1,0:T(8,128)(2,1)S(1)}) custom-call(bf16[768,512]{1,0:T(8,128)(2,1)S(1)} %collective-permute-done.refs_0_.refs_6_.refs_8_, bf16[512,768]{1,0:T(8,128)(2,1)S(1)} %collective-permute-done.1.refs_1_.refs_8_.refs_10_, ...), custom_call_target="tpu_custom_call" | custom-call | flops 1 | bytes 1 | tf_op jit(solution)/shard_map/pallas_call | solution.py:29
  9.3 1.6 %collective-permute-start.4 = (bf16[320,768]{1,0:T(8,128)(2,1)S(1)}, bf16[320,768]{1,0:T(8,128)(2,1)S(1)}, u32[]{:S(2)}, u32[]{:S(2)}) collective-permute-start(bf16[320,768]{1,0:T(8,128)(2,1)S(1)} %get-tuple-element.51), channel_id=1, source_target_pairs={{0,2},{1,3},{2,0},{3,1},{4,6},{5,7},{6,4},{7,5},{8,10},{9,11},{10,... | collective-permute-start | bytes 1474568 | tf_op jit(solution)/shard_map/ppermute | solution.py:16
  10.8 1.5 %collective-permute-start.5 = (bf16[320,768]{1,0:T(8,128)(2,1)S(1)}, bf16[320,768]{1,0:T(8,128)(2,1)S(1)}, u32[]{:S(2)}, u32[]{:S(2)}) collective-permute-start(bf16[320,768]{1,0:T(8,128)(2,1)S(1)} %get-tuple-element.52), channel_id=1, source_target_pairs={{0,4},{1,5},{2,6},{3,7},{4,0},{5,1},{6,2},{7,3},{8,12},{9,13},{10,... | collective-permute-start | bytes 1474568 | tf_op jit(solution)/shard_map/ppermute | solution.py:16
  12.4 0.5 collective-permute-start.6
  12.8 0.3 collective-permute-start.2
  13.1 14.4 %collective-permute-done.2.refs_1_ = s32[1,320]{1,0:T(1,128)S(1)} collective-permute-done((s32[1,320]{1,0:T(1,128)S(1)}, s32[1,320]{1,0:T(1,128)S(1)}, u32[]{:S(2)}, u32[]{:S(2)}) %collective-permute-start.2) | collective-permute-done | bytes 1312 | tf_op jit(solution)/shard_map/ppermute | solution.py:16
  27.5 0.7 shard_map.95
  28.2 1.6 %collective-permute-start.7 = (bf16[160,768]{1,0:T(8,128)(2,1)S(1)}, bf16[160,768]{1,0:T(8,128)(2,1)S(1)}, u32[]{:S(2)}, u32[]{:S(2)}) collective-permute-start(bf16[160,768]{1,0:T(8,128)(2,1)S(1)} %get-tuple-element.55), channel_id=1, source_target_pairs={{0,2},{1,3},{2,0},{3,1},{4,6},{5,7},{6,4},{7,5},{8,10},{9,11},{10,... | collective-permute-start | bytes 737288 | tf_op jit(solution)/shard_map/ppermute | solution.py:16
  29.9 1.5 %collective-permute-start.8 = (bf16[160,768]{1,0:T(8,128)(2,1)S(1)}, bf16[160,768]{1,0:T(8,128)(2,1)S(1)}, u32[]{:S(2)}, u32[]{:S(2)}) collective-permute-start(bf16[160,768]{1,0:T(8,128)(2,1)S(1)} %get-tuple-element.56), channel_id=1, source_target_pairs={{0,4},{1,5},{2,6},{3,7},{4,0},{5,1},{6,2},{7,3},{8,12},{9,13},{10,... | collective-permute-start | bytes 737288 | tf_op jit(solution)/shard_map/ppermute | solution.py:16
  31.4 0.0 collective-permute-start.10
  31.4 2.8 %collective-permute-done.5.refs_3_ = bf16[320,768]{1,0:T(8,128)(2,1)S(1)} collective-permute-done((bf16[320,768]{1,0:T(8,128)(2,1)S(1)}, bf16[320,768]{1,0:T(8,128)(2,1)S(1)}, u32[]{:S(2)}, u32[]{:S(2)}) %collective-permute-start.5) | collective-permute-done | bytes 491552 | tf_op jit(solution)/shard_map/ppermute | solution.py:16
  34.2 0.7 collective-permute-start.9
  34.9 0.1 collective-permute-done.6.refs_4_
  35.0 4.7 %shard_map.96 = (bf16[320,768]{1,0:T(8,128)(2,1)S(1)}, bf16[320,768]{1,0:T(8,128)(2,1)S(1)}, bf16[320,768]{1,0:T(8,128)(2,1)S(1)}, bf16[320,768]{1,0:T(8,128)(2,...) custom-call(bf16[160,768]{1,0:T(8,128)(2,1)S(1)} %get-tuple-element., ...), custom_call_target="tpu_custom_call" | custom-call | flops 1 | bytes 1 | tf_op jit(solution)/shard_map/pallas_call | solution.py:29
  39.7 0.0 collective-permute-done.7.refs_2_.refs_6_
  39.7 4.8 %collective-permute-done.8.refs_3_.refs_7_ = bf16[160,768]{1,0:T(8,128)(2,1)S(1)} collective-permute-done((bf16[160,768]{1,0:T(8,128)(2,1)S(1)}, bf16[160,768]{1,0:T(8,128)(2,1)S(1)}, u32[]{:S(2)}, u32[]{:S(2)}) %collective-permute-start.8) | collective-permute-done | bytes 245792 | tf_op jit(solution)/shard_map/ppermute | solution.py:16
  44.6 3.0 %shard_map.97 = (bf16[160,768]{1,0:T(8,128)(2,1)S(1)}, bf16[160,768]{1,0:T(8,128)(2,1)S(1)}, bf16[160,768]{1,0:T(8,128)(2,1)S(1)}, bf16[160,768]{1,0:T(8,128)(2,...) custom-call(bf16[320,768]{1,0:T(8,128)(2,1)S(1)} %get-tuple-element., ...), custom_call_target="tpu_custom_call" | custom-call | flops 1 | bytes 1 | tf_op jit(solution)/shard_map/pallas_call | solution.py:29
  47.5 1.3 %collective-permute-start.11 = (bf16[160,768]{1,0:T(8,128)(2,1)S(1)}, bf16[160,768]{1,0:T(8,128)(2,1)S(1)}, u32[]{:S(2)}, u32[]{:S(2)}) collective-permute-start(bf16[160,768]{1,0:T(8,128)(2,1)S(1)} %get-tuple-element.61), channel_id=1, source_target_pairs={{0,2},{1,3},{2,0},{3,1},{4,6},{5,7},{6,4},{7,5},{8,10},{9,11},{10,... | collective-permute-start | bytes 737288 | tf_op jit(solution)/shard_map/ppermute | solution.py:16
  48.9 0.8 collective-permute-start.12
  49.7 1.4 %collective-permute-start.13 = (bf16[160,768]{1,0:T(8,128)(2,1)S(1)}, bf16[160,768]{1,0:T(8,128)(2,1)S(1)}, u32[]{:S(2)}, u32[]{:S(2)}) collective-permute-start(bf16[160,768]{1,0:T(8,128)(2,1)S(1)} %get-tuple-element.63), channel_id=1, source_target_pairs={{0,6},{1,7},{2,4},{3,5},{4,2},{5,3},{6,0},{7,1},{8,14},{9,15},{10,... | collective-permute-start | bytes 737288 | tf_op jit(solution)/shard_map/ppermute | solution.py:16
  51.1 3.5 %collective-permute-done.10.refs_2_ = bf16[320,768]{1,0:T(8,128)(2,1)S(1)} collective-permute-done((bf16[320,768]{1,0:T(8,128)(2,1)S(1)}, bf16[320,768]{1,0:T(8,128)(2,1)S(1)}, u32[]{:S(2)}, u32[]{:S(2)}) %collective-permute-start.10) | collective-permute-done | bytes 491552 | tf_op jit(solution)/shard_map/ppermute | solution.py:16
  54.6 0.7 shard_map.98
  55.3 0.6 collective-permute-start.15
  55.9 0.8 collective-permute-start.16
  56.6 0.0 collective-permute-done.11.refs_3_
  56.6 2.2 %collective-permute-start.17 = (bf16[160,768]{1,0:T(8,128)(2,1)S(1)}, bf16[160,768]{1,0:T(8,128)(2,1)S(1)}, u32[]{:S(2)}, u32[]{:S(2)}) collective-permute-start(bf16[160,768]{1,0:T(8,128)(2,1)S(1)} %get-tuple-element.66), channel_id=1, source_target_pairs={{0,6},{1,7},{2,4},{3,5},{4,2},{5,3},{6,0},{7,1},{8,14},{9,15},{10,... | collective-permute-start | bytes 737288 | tf_op jit(solution)/shard_map/ppermute | solution.py:16
  58.8 0.4 collective-permute-done.12.refs_4_
  59.2 3.5 %collective-permute-done.13.refs_5_ = bf16[160,768]{1,0:T(8,128)(2,1)S(1)} collective-permute-done((bf16[160,768]{1,0:T(8,128)(2,1)S(1)}, bf16[160,768]{1,0:T(8,128)(2,1)S(1)}, u32[]{:S(2)}, u32[]{:S(2)}) %collective-permute-start.13) | collective-permute-done | bytes 245792 | tf_op jit(solution)/shard_map/ppermute | solution.py:16
  62.8 0.6 shard_map.99.refs_0_
  63.4 0.7 collective-permute-start.14
  64.1 3.0 %collective-permute-done.15.refs_2_.refs_10_ = bf16[160,768]{1,0:T(8,128)(2,1)S(1)} collective-permute-done((bf16[160,768]{1,0:T(8,128)(2,1)S(1)}, bf16[160,768]{1,0:T(8,128)(2,1)S(1)}, u32[]{:S(2)}, u32[]{:S(2)}) %collective-permute-start.15) | collective-permute-done | bytes 245792 | tf_op jit(solution)/shard_map/ppermute | solution.py:16
  67.0 2.4 %collective-permute-done.16.refs_3_.refs_11_ = bf16[160,768]{1,0:T(8,128)(2,1)S(1)} collective-permute-done((bf16[160,768]{1,0:T(8,128)(2,1)S(1)}, bf16[160,768]{1,0:T(8,128)(2,1)S(1)}, u32[]{:S(2)}, u32[]{:S(2)}) %collective-permute-start.16) | collective-permute-done | bytes 245792 | tf_op jit(solution)/shard_map/ppermute | solution.py:16
  69.4 1.9 %collective-permute-done.17.refs_4_.refs_12_ = bf16[160,768]{1,0:T(8,128)(2,1)S(1)} collective-permute-done((bf16[160,768]{1,0:T(8,128)(2,1)S(1)}, bf16[160,768]{1,0:T(8,128)(2,1)S(1)}, u32[]{:S(2)}, u32[]{:S(2)}) %collective-permute-start.17) | collective-permute-done | bytes 245792 | tf_op jit(solution)/shard_map/ppermute | solution.py:16
  71.3 2.5 %shard_map.100 = (bf16[160,768]{1,0:T(8,128)(2,1)S(1)}, bf16[160,768]{1,0:T(8,128)(2,1)S(1)}, bf16[160,768]{1,0:T(8,128)(2,1)S(1)}, bf16[160,768]{1,0:T(8,128)(2...) custom-call(bf16[320,768]{1,0:T(8,128)(2,1)S(1)} %shard_map.99.refs_0_, ...), custom_call_target="tpu_custom_call" | custom-call | flops 1 | bytes 1 | tf_op jit(solution)/shard_map/pallas_call | solution.py:29
  73.8 0.6 collective-permute-start.18
  74.4 1.7 %collective-permute-start.19 = (bf16[160,768]{1,0:T(8,128)(2,1)S(1)}, bf16[160,768]{1,0:T(8,128)(2,1)S(1)}, u32[]{:S(2)}, u32[]{:S(2)}) collective-permute-start(bf16[160,768]{1,0:T(8,128)(2,1)S(1)} %get-tuple-element.71), channel_id=1, source_target_pairs={{0,4},{1,5},{2,6},{3,7},{4,0},{5,1},{6,2},{7,3},{8,12},{9,13},{10,... | collective-permute-start | bytes 737288 | tf_op jit(solution)/shard_map/ppermute | solution.py:16
  76.2 1.2 %collective-permute-start.20 = (bf16[160,768]{1,0:T(8,128)(2,1)S(1)}, bf16[160,768]{1,0:T(8,128)(2,1)S(1)}, u32[]{:S(2)}, u32[]{:S(2)}) collective-permute-start(bf16[160,768]{1,0:T(8,128)(2,1)S(1)} %get-tuple-element.72), channel_id=1, source_target_pairs={{0,6},{1,7},{2,4},{3,5},{4,2},{5,3},{6,0},{7,1},{8,14},{9,15},{10,... | collective-permute-start | bytes 737288 | tf_op jit(solution)/shard_map/ppermute | solution.py:16
  77.4 0.5 collective-permute-start.22
  77.9 4.9 %collective-permute-done.18.refs_3_ = bf16[160,768]{1,0:T(8,128)(2,1)S(1)} collective-permute-done((bf16[160,768]{1,0:T(8,128)(2,1)S(1)}, bf16[160,768]{1,0:T(8,128)(2,1)S(1)}, u32[]{:S(2)}, u32[]{:S(2)}) %collective-permute-start.18) | collective-permute-done | bytes 245792 | tf_op jit(solution)/shard_map/ppermute | solution.py:16
  82.8 0.7 collective-permute-start.23
  83.4 2.9 %collective-permute-done.19.refs_4_ = bf16[160,768]{1,0:T(8,128)(2,1)S(1)} collective-permute-done((bf16[160,768]{1,0:T(8,128)(2,1)S(1)}, bf16[160,768]{1,0:T(8,128)(2,1)S(1)}, u32[]{:S(2)}, u32[]{:S(2)}) %collective-permute-start.19) | collective-permute-done | bytes 245792 | tf_op jit(solution)/shard_map/ppermute | solution.py:16
  86.4 1.3 %collective-permute-start.24 = (bf16[320,768]{1,0:T(8,128)(2,1)S(1)}, bf16[320,768]{1,0:T(8,128)(2,1)S(1)}, u32[]{:S(2)}, u32[]{:S(2)}) collective-permute-start(bf16[320,768]{1,0:T(8,128)(2,1)S(1)} %get-tuple-element.84), channel_id=1, source_target_pairs={{0,6},{1,7},{2,4},{3,5},{4,2},{5,3},{6,0},{7,1},{8,14},{9,15},{10,... | collective-permute-start | bytes 1474568 | tf_op jit(solution)/shard_map/ppermute | solution.py:16
  87.6 0.5 collective-permute-done.20.refs_5_
  88.1 0.0 collective-permute-done.14.refs_0_.refs_6_
  88.1 0.6 shard_map.101.refs_0_
  88.8 3.0 %collective-permute-start.25 = (bf16[320,768]{1,0:T(8,128)(2,1)S(1)}, bf16[320,768]{1,0:T(8,128)(2,1)S(1)}, u32[]{:S(2)}, u32[]{:S(2)}) collective-permute-start(bf16[320,768]{1,0:T(8,128)(2,1)S(1)} %shard_map.101.refs_0_), channel_id=1, source_target_pairs={{0,16},{8,24},{16,0},{24,8},{1,17},{9,25},{17,1},{25,9},{2,18},{10... | collective-permute-start | bytes 1474568 | tf_op jit(solution)/shard_map/ppermute | solution.py:16
  91.8 2.6 %shard_map.102.refs_0_ = bf16[3072,256]{1,0:T(8,128)(2,1)} custom-call(bf16[320,768]{1,0:T(8,128)(2,1)S(1)} %shard_map.101.refs_0_, bf16[320,768]{1,0:T(8,128)(2,1)S(1)} %get-tuple-element.49.refs_0_.refs_1_, bf16[320,768]{1,0:T(8,128)(2,1)S(1)} %collective-permute-done.4.refs_2_, bf16[320,768]{1,0:T(8,128)(2,1)S(1)} %collective-permute-done.5.refs_3_, ...), custom_call_target="tpu_custom_call" | custom-call | flops 1000000000 | bytes 1 | tf_op jit(solution)/shard_map/pallas_call | solution.py:29
  94.4 3.1 %shard_map.103.refs_0_ = f32[3072,256]{1,0:T(8,128)} custom-call(bf16[3072,256]{1,0:T(8,128)(2,1)} %shard_map.102.refs_0_, bf16[320,768]{1,0:T(8,128)(2,1)S(1)} %get-tuple-element.49.refs_0_.refs_1_, bf16[320,768]{1,0:T(8,128)(2,1)S(1)} %collective-permute-done.4.refs_2_, bf16[320,768]{1,0:T(8,128)(2,1)S(1)} %collective-permute-done.5.refs_3_, ...), custom_call_target="tpu_custom_call" | custom-call | flops 30000001024 | bytes 1 | tf_op jit(solution)/shard_map/pallas_call | solution.py:29
  97.5 0.5 collective-permute-done.21.refs_1_
  98.0 1.9 %copy-done.5 = f32[3072,256]{1,0:T(8,128)S(1)} copy-done((f32[3072,256]{1,0:T(8,128)S(1)}, f32[3072,256]{1,0:T(8,128)}, u32[]{:S(2)}) %copy-start.5) | copy-done | bytes 3145752
  99.9 1.3 %shard_map.104 = (bf16[768,512]{1,0:T(8,128)(2,1)}, bf16[512,768]{1,0:T(8,128)(2,1)}) custom-call(f32[3072,256]{1,0:T(8,128)S(1)} %copy-done.5, bf16[3072,256]{1,0:T(8,128)(2,1)S(1)} %collective-permute-done.21.refs_1_), custom_call_target="tpu_custom_call" | custom-call | flops 1 | bytes 1 | tf_op jit(solution)/shard_map/pallas_call | solution.py:29
  101.2 5.0 %collective-permute-done.23.refs_4_ = bf16[320,768]{1,0:T(8,128)(2,1)S(1)} collective-permute-done((bf16[320,768]{1,0:T(8,128)(2,1)S(1)}, bf16[320,768]{1,0:T(8,128)(2,1)S(1)}, u32[]{:S(2)}, u32[]{:S(2)}) %collective-permute-start.23) | collective-permute-done | bytes 491552 | tf_op jit(solution)/shard_map/ppermute | solution.py:16
  106.2 1.6 %shard_map.105 = (bf16[320,768]{1,0:T(8,128)(2,1)}, bf16[320,768]{1,0:T(8,128)(2,1)S(1)}) custom-call(bf16[768,512]{1,0:T(8,128)(2,1)} %get-tuple-element.81.refs_0_, s32[1,320]{1,0:T(1,128)S(1)} %get-tuple-element.46.refs_2_.refs_1_, bf16[320,768]{1,0:T(8,128)(2,1)S(1)} %get-tuple-element.54.refs_0_.refs_2_, ...), custom_call_target="tpu_custom_call" | custom-call | flops 1 | bytes 1 | tf_op jit(solution)/shard_map/pallas_call | solution.py:29
  107.8 0.7 collective-permute-done.25
  108.5 0.9 add_convert_fusion
  (20 shorter events, 0.0 us)
Async XLA Ops:
  0.6 7.4 %collective-permute-start = (bf16[768,512]{1,0:T(8,128)(2,1)}, bf16[768,512]{1,0:T(8,128)(2,1)S(1)}, u32[]{:S(2)}, u32[]{:S(2)}) collective-permute-start(bf16[768,512]{1,0:T(8,128)(2,1)} %bitcast.6), channel_id=1, source_target_pairs={{0,1},{1,0},{2,3},{3,2},{4,5},{5,4},{6,7},{7,6},{8,9},{9,8},{10,11... | collective-permute-start | bytes 2359304 | tf_op jit(solution)/shard_map/ppermute | solution.py:16
  1.1 6.9 %collective-permute-start.1 = (bf16[512,768]{1,0:T(8,128)(2,1)}, bf16[512,768]{1,0:T(8,128)(2,1)S(1)}, u32[]{:S(2)}, u32[]{:S(2)}) collective-permute-start(bf16[512,768]{1,0:T(8,128)(2,1)} %bitcast.10), channel_id=1, source_target_pairs={{0,1},{1,0},{2,3},{3,2},{4,5},{5,4},{6,7},{7,6},{8,9},{9,8},{10,11... | collective-permute-start | bytes 2359304 | tf_op jit(solution)/shard_map/ppermute | solution.py:16
  1.2 26.3 %collective-permute-start.3 = (bf16[320,768]{1,0:T(8,128)(2,1)}, bf16[320,768]{1,0:T(8,128)(2,1)S(1)}, u32[]{:S(2)}, u32[]{:S(2)}) collective-permute-start(bf16[320,768]{1,0:T(8,128)(2,1)} %token_ref.1), channel_id=1, source_target_pairs={{0,16},{8,24},{16,0},{24,8},{1,17},{9,25},{17,1},{25,9},{2,18},{10... | collective-permute-start | bytes 1474568 | tf_op jit(solution)/shard_map/ppermute | solution.py:16
  5.2 0.7 copy-start.6
  5.9 0.7 copy-start.8
  8.1 20.2 %copy-start = (bf16[768,512]{1,0:T(8,128)(2,1)}, bf16[768,512]{1,0:T(8,128)(2,1)S(1)}, u32[]{:S(2)}) copy-start(bf16[768,512]{1,0:T(8,128)(2,1)S(1)} %collective-permute-done.refs_0_.refs_6_.refs_8_) | copy-start | bytes 2359300
  8.1 20.2 %copy-start.2 = (bf16[512,768]{1,0:T(8,128)(2,1)}, bf16[512,768]{1,0:T(8,128)(2,1)S(1)}, u32[]{:S(2)}) copy-start(bf16[512,768]{1,0:T(8,128)(2,1)S(1)} %collective-permute-done.1.refs_1_.refs_8_.refs_10_) | copy-start | bytes 2359300
  9.3 22.1 %collective-permute-start.4 = (bf16[320,768]{1,0:T(8,128)(2,1)S(1)}, bf16[320,768]{1,0:T(8,128)(2,1)S(1)}, u32[]{:S(2)}, u32[]{:S(2)}) collective-permute-start(bf16[320,768]{1,0:T(8,128)(2,1)S(1)} %get-tuple-element.51), channel_id=1, source_target_pairs={{0,2},{1,3},{2,0},{3,1},{4,6},{5,7},{6,4},{7,5},{8,10},{9,11},{10,... | collective-permute-start | bytes 1474568 | tf_op jit(solution)/shard_map/ppermute | solution.py:16
  10.8 23.3 %collective-permute-start.5 = (bf16[320,768]{1,0:T(8,128)(2,1)S(1)}, bf16[320,768]{1,0:T(8,128)(2,1)S(1)}, u32[]{:S(2)}, u32[]{:S(2)}) collective-permute-start(bf16[320,768]{1,0:T(8,128)(2,1)S(1)} %get-tuple-element.52), channel_id=1, source_target_pairs={{0,4},{1,5},{2,6},{3,7},{4,0},{5,1},{6,2},{7,3},{8,12},{9,13},{10,... | collective-permute-start | bytes 1474568 | tf_op jit(solution)/shard_map/ppermute | solution.py:16
  12.4 22.6 %collective-permute-start.6 = (bf16[320,768]{1,0:T(8,128)(2,1)S(1)}, bf16[320,768]{1,0:T(8,128)(2,1)S(1)}, u32[]{:S(2)}, u32[]{:S(2)}) collective-permute-start(bf16[320,768]{1,0:T(8,128)(2,1)S(1)} %get-tuple-element.53), channel_id=1, source_target_pairs={{0,6},{1,7},{2,4},{3,5},{4,2},{5,3},{6,0},{7,1},{8,14},{9,15},{10,... | collective-permute-start | bytes 1474568 | tf_op jit(solution)/shard_map/ppermute | solution.py:16
  12.8 14.7 %collective-permute-start.2 = (s32[1,320]{1,0:T(1,128)S(1)}, s32[1,320]{1,0:T(1,128)S(1)}, u32[]{:S(2)}, u32[]{:S(2)}) collective-permute-start(s32[1,320]{1,0:T(1,128)S(1)} %get-tuple-element.46.refs_2_.refs_1_), channel_id=1, source_target_pairs={{0,16},{8,24},{16,0},{24,8},{1,17},{9,25},{17,1},{25,9},{2,18},{10... | collective-permute-start | bytes 3848 | tf_op jit(solution)/shard_map/ppermute | solution.py:16
  28.2 11.5 %collective-permute-start.7 = (bf16[160,768]{1,0:T(8,128)(2,1)S(1)}, bf16[160,768]{1,0:T(8,128)(2,1)S(1)}, u32[]{:S(2)}, u32[]{:S(2)}) collective-permute-start(bf16[160,768]{1,0:T(8,128)(2,1)S(1)} %get-tuple-element.55), channel_id=1, source_target_pairs={{0,2},{1,3},{2,0},{3,1},{4,6},{5,7},{6,4},{7,5},{8,10},{9,11},{10,... | collective-permute-start | bytes 737288 | tf_op jit(solution)/shard_map/ppermute | solution.py:16
  29.9 14.7 %collective-permute-start.8 = (bf16[160,768]{1,0:T(8,128)(2,1)S(1)}, bf16[160,768]{1,0:T(8,128)(2,1)S(1)}, u32[]{:S(2)}, u32[]{:S(2)}) collective-permute-start(bf16[160,768]{1,0:T(8,128)(2,1)S(1)} %get-tuple-element.56), channel_id=1, source_target_pairs={{0,4},{1,5},{2,6},{3,7},{4,0},{5,1},{6,2},{7,3},{8,12},{9,13},{10,... | collective-permute-start | bytes 737288 | tf_op jit(solution)/shard_map/ppermute | solution.py:16
  31.4 23.2 %collective-permute-start.10 = (bf16[320,768]{1,0:T(8,128)(2,1)S(1)}, bf16[320,768]{1,0:T(8,128)(2,1)S(1)}, u32[]{:S(2)}, u32[]{:S(2)}) collective-permute-start(bf16[320,768]{1,0:T(8,128)(2,1)S(1)} %get-tuple-element.59), channel_id=1, source_target_pairs={{0,16},{8,24},{16,0},{24,8},{1,17},{9,25},{17,1},{25,9},{2,18},{10... | collective-permute-start | bytes 1474568 | tf_op jit(solution)/shard_map/ppermute | solution.py:16
  34.2 10.4 %collective-permute-start.9 = (bf16[160,768]{1,0:T(8,128)(2,1)S(1)}, bf16[160,768]{1,0:T(8,128)(2,1)S(1)}, u32[]{:S(2)}, u32[]{:S(2)}) collective-permute-start(bf16[160,768]{1,0:T(8,128)(2,1)S(1)} %get-tuple-element.57), channel_id=1, source_target_pairs={{0,6},{1,7},{2,4},{3,5},{4,2},{5,3},{6,0},{7,1},{8,14},{9,15},{10,... | collective-permute-start | bytes 737288 | tf_op jit(solution)/shard_map/ppermute | solution.py:16
  35.0 9.6 %copy-start.1 = (bf16[768,512]{1,0:T(8,128)(2,1)S(1)}, bf16[768,512]{1,0:T(8,128)(2,1)}, u32[]{:S(2)}) copy-start(bf16[768,512]{1,0:T(8,128)(2,1)} %copy-done) | copy-start | bytes 2359300
  35.0 9.6 %copy-start.3 = (bf16[1,768,512]{2,1,0:T(8,128)(2,1)S(1)}, bf16[1,768,512]{2,1,0:T(8,128)(2,1)}, u32[]{:S(2)}) copy-start(bf16[1,768,512]{2,1,0:T(8,128)(2,1)} %param.9) | copy-start | bytes 2359300
  35.0 9.6 %copy-start.4 = (bf16[1,512,768]{2,1,0:T(8,128)(2,1)S(1)}, bf16[1,512,768]{2,1,0:T(8,128)(2,1)}, u32[]{:S(2)}) copy-start(bf16[1,512,768]{2,1,0:T(8,128)(2,1)} %param.10) | copy-start | bytes 2359300
  47.5 9.1 %collective-permute-start.11 = (bf16[160,768]{1,0:T(8,128)(2,1)S(1)}, bf16[160,768]{1,0:T(8,128)(2,1)S(1)}, u32[]{:S(2)}, u32[]{:S(2)}) collective-permute-start(bf16[160,768]{1,0:T(8,128)(2,1)S(1)} %get-tuple-element.61), channel_id=1, source_target_pairs={{0,2},{1,3},{2,0},{3,1},{4,6},{5,7},{6,4},{7,5},{8,10},{9,11},{10,... | collective-permute-start | bytes 737288 | tf_op jit(solution)/shard_map/ppermute | solution.py:16
  48.9 10.4 %collective-permute-start.12 = (bf16[160,768]{1,0:T(8,128)(2,1)S(1)}, bf16[160,768]{1,0:T(8,128)(2,1)S(1)}, u32[]{:S(2)}, u32[]{:S(2)}) collective-permute-start(bf16[160,768]{1,0:T(8,128)(2,1)S(1)} %get-tuple-element.62), channel_id=1, source_target_pairs={{0,4},{1,5},{2,6},{3,7},{4,0},{5,1},{6,2},{7,3},{8,12},{9,13},{10,... | collective-permute-start | bytes 737288 | tf_op jit(solution)/shard_map/ppermute | solution.py:16
  49.7 13.1 %collective-permute-start.13 = (bf16[160,768]{1,0:T(8,128)(2,1)S(1)}, bf16[160,768]{1,0:T(8,128)(2,1)S(1)}, u32[]{:S(2)}, u32[]{:S(2)}) collective-permute-start(bf16[160,768]{1,0:T(8,128)(2,1)S(1)} %get-tuple-element.63), channel_id=1, source_target_pairs={{0,6},{1,7},{2,4},{3,5},{4,2},{5,3},{6,0},{7,1},{8,14},{9,15},{10,... | collective-permute-start | bytes 737288 | tf_op jit(solution)/shard_map/ppermute | solution.py:16
  55.3 11.8 %collective-permute-start.15 = (bf16[160,768]{1,0:T(8,128)(2,1)S(1)}, bf16[160,768]{1,0:T(8,128)(2,1)S(1)}, u32[]{:S(2)}, u32[]{:S(2)}) collective-permute-start(bf16[160,768]{1,0:T(8,128)(2,1)S(1)} %get-tuple-element.64), channel_id=1, source_target_pairs={{0,2},{1,3},{2,0},{3,1},{4,6},{5,7},{6,4},{7,5},{8,10},{9,11},{10,... | collective-permute-start | bytes 737288 | tf_op jit(solution)/shard_map/ppermute | solution.py:16
  55.9 13.6 %collective-permute-start.16 = (bf16[160,768]{1,0:T(8,128)(2,1)S(1)}, bf16[160,768]{1,0:T(8,128)(2,1)S(1)}, u32[]{:S(2)}, u32[]{:S(2)}) collective-permute-start(bf16[160,768]{1,0:T(8,128)(2,1)S(1)} %get-tuple-element.65), channel_id=1, source_target_pairs={{0,4},{1,5},{2,6},{3,7},{4,0},{5,1},{6,2},{7,3},{8,12},{9,13},{10,... | collective-permute-start | bytes 737288 | tf_op jit(solution)/shard_map/ppermute | solution.py:16
  56.6 14.6 %collective-permute-start.17 = (bf16[160,768]{1,0:T(8,128)(2,1)S(1)}, bf16[160,768]{1,0:T(8,128)(2,1)S(1)}, u32[]{:S(2)}, u32[]{:S(2)}) collective-permute-start(bf16[160,768]{1,0:T(8,128)(2,1)S(1)} %get-tuple-element.66), channel_id=1, source_target_pairs={{0,6},{1,7},{2,4},{3,5},{4,2},{5,3},{6,0},{7,1},{8,14},{9,15},{10,... | collective-permute-start | bytes 737288 | tf_op jit(solution)/shard_map/ppermute | solution.py:16
  63.4 24.7 %collective-permute-start.14 = (bf16[320,768]{1,0:T(8,128)(2,1)S(1)}, bf16[320,768]{1,0:T(8,128)(2,1)S(1)}, u32[]{:S(2)}, u32[]{:S(2)}) collective-permute-start(bf16[320,768]{1,0:T(8,128)(2,1)S(1)} %shard_map.99.refs_0_), channel_id=1, source_target_pairs={{0,16},{8,24},{16,0},{24,8},{1,17},{9,25},{17,1},{25,9},{2,18},{10... | collective-permute-start | bytes 1474568 | tf_op jit(solution)/shard_map/ppermute | solution.py:16
  73.8 9.0 %collective-permute-start.18 = (bf16[160,768]{1,0:T(8,128)(2,1)S(1)}, bf16[160,768]{1,0:T(8,128)(2,1)S(1)}, u32[]{:S(2)}, u32[]{:S(2)}) collective-permute-start(bf16[160,768]{1,0:T(8,128)(2,1)S(1)} %get-tuple-element.70), channel_id=1, source_target_pairs={{0,2},{1,3},{2,0},{3,1},{4,6},{5,7},{6,4},{7,5},{8,10},{9,11},{10,... | collective-permute-start | bytes 737288 | tf_op jit(solution)/shard_map/ppermute | solution.py:16
  74.4 12.0 %collective-permute-start.19 = (bf16[160,768]{1,0:T(8,128)(2,1)S(1)}, bf16[160,768]{1,0:T(8,128)(2,1)S(1)}, u32[]{:S(2)}, u32[]{:S(2)}) collective-permute-start(bf16[160,768]{1,0:T(8,128)(2,1)S(1)} %get-tuple-element.71), channel_id=1, source_target_pairs={{0,4},{1,5},{2,6},{3,7},{4,0},{5,1},{6,2},{7,3},{8,12},{9,13},{10,... | collective-permute-start | bytes 737288 | tf_op jit(solution)/shard_map/ppermute | solution.py:16
  76.2 12.0 %collective-permute-start.20 = (bf16[160,768]{1,0:T(8,128)(2,1)S(1)}, bf16[160,768]{1,0:T(8,128)(2,1)S(1)}, u32[]{:S(2)}, u32[]{:S(2)}) collective-permute-start(bf16[160,768]{1,0:T(8,128)(2,1)S(1)} %get-tuple-element.72), channel_id=1, source_target_pairs={{0,6},{1,7},{2,4},{3,5},{4,2},{5,3},{6,0},{7,1},{8,14},{9,15},{10,... | collective-permute-start | bytes 737288 | tf_op jit(solution)/shard_map/ppermute | solution.py:16
  77.4 23.9 %collective-permute-start.22 = (bf16[320,768]{1,0:T(8,128)(2,1)S(1)}, bf16[320,768]{1,0:T(8,128)(2,1)S(1)}, u32[]{:S(2)}, u32[]{:S(2)}) collective-permute-start(bf16[320,768]{1,0:T(8,128)(2,1)S(1)} %get-tuple-element.82), channel_id=1, source_target_pairs={{0,2},{1,3},{2,0},{3,1},{4,6},{5,7},{6,4},{7,5},{8,10},{9,11},{10,... | collective-permute-start | bytes 1474568 | tf_op jit(solution)/shard_map/ppermute | solution.py:16
  82.8 23.5 %collective-permute-start.23 = (bf16[320,768]{1,0:T(8,128)(2,1)S(1)}, bf16[320,768]{1,0:T(8,128)(2,1)S(1)}, u32[]{:S(2)}, u32[]{:S(2)}) collective-permute-start(bf16[320,768]{1,0:T(8,128)(2,1)S(1)} %get-tuple-element.83), channel_id=1, source_target_pairs={{0,4},{1,5},{2,6},{3,7},{4,0},{5,1},{6,2},{7,3},{8,12},{9,13},{10,... | collective-permute-start | bytes 1474568 | tf_op jit(solution)/shard_map/ppermute | solution.py:16
  86.4 19.9 %collective-permute-start.24 = (bf16[320,768]{1,0:T(8,128)(2,1)S(1)}, bf16[320,768]{1,0:T(8,128)(2,1)S(1)}, u32[]{:S(2)}, u32[]{:S(2)}) collective-permute-start(bf16[320,768]{1,0:T(8,128)(2,1)S(1)} %get-tuple-element.84), channel_id=1, source_target_pairs={{0,6},{1,7},{2,4},{3,5},{4,2},{5,3},{6,0},{7,1},{8,14},{9,15},{10,... | collective-permute-start | bytes 1474568 | tf_op jit(solution)/shard_map/ppermute | solution.py:16
  88.8 19.8 %collective-permute-start.25 = (bf16[320,768]{1,0:T(8,128)(2,1)S(1)}, bf16[320,768]{1,0:T(8,128)(2,1)S(1)}, u32[]{:S(2)}, u32[]{:S(2)}) collective-permute-start(bf16[320,768]{1,0:T(8,128)(2,1)S(1)} %shard_map.101.refs_0_), channel_id=1, source_target_pairs={{0,16},{8,24},{16,0},{24,8},{1,17},{9,25},{17,1},{25,9},{2,18},{10... | collective-permute-start | bytes 1474568 | tf_op jit(solution)/shard_map/ppermute | solution.py:16
  94.4 3.6 %collective-permute-start.21 = (bf16[3072,256]{1,0:T(8,128)(2,1)}, bf16[3072,256]{1,0:T(8,128)(2,1)S(1)}, u32[]{:S(2)}, u32[]{:S(2)}) collective-permute-start(bf16[3072,256]{1,0:T(8,128)(2,1)} %shard_map.102.refs_0_), channel_id=1, source_target_pairs={{0,1},{1,0},{2,3},{3,2},{4,5},{5,4},{6,7},{7,6},{8,9},{9,8},{10,11... | collective-permute-start | bytes 4718600 | tf_op jit(solution)/shard_map/ppermute | solution.py:16
  98.0 1.9 %copy-start.5 = (f32[3072,256]{1,0:T(8,128)S(1)}, f32[3072,256]{1,0:T(8,128)}, u32[]{:S(2)}) copy-start(f32[3072,256]{1,0:T(8,128)} %shard_map.103.refs_0_) | copy-start | bytes 9437188
  99.9 6.3 %copy-start.7 = (f32[320]{0:T(512)S(1)}, f32[320]{0:T(512)}, u32[]{:S(2)}) copy-start(f32[320]{0:T(512)} %refs_7_.1) | copy-start | bytes 3844

commit v4 on v3

--- a/solution.py
+++ b/solution.py
@@ -10,6 +10,8 @@
 F32 = jnp.float32
 BF16 = jnp.bfloat16
 VMEM_LIMIT = 48 * 1024 * 1024
+HEAVY = pl.CostEstimate(flops=30 * 10**9, bytes_accessed=1, transcendentals=0)
+LIGHT = pl.CostEstimate(flops=1, bytes_accessed=1, transcendentals=0)
 
 
 def exchange(array, axis, flip):
@@ -20,7 +22,7 @@
     return lax.dot_general(a, b, (contract, ((), ())), preferred_element_type=F32)
 
 
-def call(body, out_shape, *args, after=(), space=pl.ANY, flops=1):
+def call(body, out_shape, *args, after=(), space=pl.ANY, weight=HEAVY):
     waits = len(after)
 
     def kernel(*refs):
@@ -31,7 +33,7 @@
         out_shape=out_shape,
         in_specs=[pl.BlockSpec(memory_space=space)] * waits
         + [pl.BlockSpec(memory_space=pltpu.VMEM)] * len(args),
-        cost_estimate=pl.CostEstimate(flops=flops, bytes_accessed=1, transcendentals=0),
+        cost_estimate=weight,
         compiler_params=pltpu.CompilerParams(vmem_limit_bytes=VMEM_LIMIT),
     )(*after, *args)
 
@@ -52,65 +54,61 @@
     experts = 2 * blocks
     pieces = 4
     piece = local // pieces
-
-    def body(device_ref, route_ref, gate_ref, token_ref, cotangent_ref, slot_ref, *refs):
-        token_out, scaled_out, cotangent_here, sems = refs
+    parts = [pl.ds(number * piece, piece) for number in range(pieces)]
+
+    def body(device_ref, route_ref, gate_ref, token_ref, cotangent_ref, *refs):
+        slot_ref, token_out, scaled_out, route_here, gate_here, cotangent_here, sems = refs
+        pairs = [(route_ref, route_here), (gate_ref, gate_here)]
+        pairs += [(cotangent_ref.at[part], cotangent_here.at[part]) for part in parts]
+        pairs += [(token_ref.at[part], token_out.at[part]) for part in parts]
         copies = [
-            pltpu.make_async_copy(
-                source.at[number * piece : (number + 1) * piece],
-                target.at[number * piece : (number + 1) * piece],
-                sems.at[array * pieces + number],
-            )
-            for array, (source, target) in enumerate(
-                ((token_ref, token_out), (cotangent_ref, cotangent_here))
-            )
-            for number in range(pieces)
+            pltpu.make_async_copy(source, target, sems.at[number])
+            for number, (source, target) in enumerate(pairs)
         ]
         for copy in copies:
             copy.start()
-        route = route_ref[...]
-        expert = lax.broadcasted_iota(jnp.int32, (experts, local), 0)
-        choose = jnp.where(expert == route, 1.0, 0.0)
         earlier = lax.broadcasted_iota(jnp.int32, (local, local), 0)
         later = lax.broadcasted_iota(jnp.int32, (local, local), 1)
         upto = jnp.where(earlier <= later, 1.0, 0.0).astype(BF16)
+        expert = lax.broadcasted_iota(jnp.int32, (experts, local), 0)
+        copies[0].wait()
+        route = route_here[...]
+        choose = jnp.where(expert == route, 1.0, 0.0)
         running = dot(choose.astype(BF16), upto, ((1,), (0,)))
         rank = jnp.sum(running * choose, axis=0, keepdims=True) - 1.0
         slot_ref[...] = (route ^ device_ref[0]) * capacity + rank.astype(jnp.int32)
-        factor = column(gate_ref[...].reshape(1, local))
-        for copy in copies:
+        copies[1].wait()
+        factor = column(gate_here[...].reshape(1, local))
+        for copy in copies[2:]:
             copy.wait()
         scaled_out[...] = (factor * cotangent_here[...].astype(F32)).astype(BF16)
+
+    def far(array):
+        return pltpu.with_memory_space_constraint(array, pltpu.HBM)
 
     return pl.pallas_call(
         body,
         out_shape=[shape(1, local, jnp.int32), shape(local, width), shape(local, width)],
         in_specs=[pl.BlockSpec(memory_space=pltpu.SMEM)]
-        + [pl.BlockSpec(memory_space=pltpu.VMEM)] * 2
-        + [pl.BlockSpec(memory_space=pltpu.HBM)] * 2,
+        + [pl.BlockSpec(memory_space=pltpu.HBM)] * 4,
         out_specs=[pl.BlockSpec(memory_space=pltpu.VMEM)] * 3,
         scratch_shapes=[
+            pltpu.VMEM((1, local), jnp.int32),
+            pltpu.VMEM((local,), F32),
             pltpu.VMEM((local, width), BF16),
-            pltpu.SemaphoreType.DMA((2 * pieces,)),
+            pltpu.SemaphoreType.DMA((2 + 2 * pieces,)),
         ],
-        cost_estimate=pl.CostEstimate(flops=1, bytes_accessed=1, transcendentals=0),
+        cost_estimate=LIGHT,
         compiler_params=pltpu.CompilerParams(vmem_limit_bytes=VMEM_LIMIT),
-    )(
-        device,
-        route_row,
-        gate,
-        pltpu.with_memory_space_constraint(tokens, pltpu.HBM),
-        pltpu.with_memory_space_constraint(cotangent, pltpu.HBM),
-    )
-
-
-def dispatch(slots, arrays, blocks, rows, given=None, after=()):
+    )(device, far(route_row), far(gate), far(tokens), far(cotangent))
+
+
+def dispatch(slots, arrays, blocks, rows, hand_on=False, after=(), weight=HEAVY):
     local, width = arrays[0].shape
     several = len(arrays)
-    more = () if given is None else (given,)
 
     def body(slot_ref, *refs):
-        values, outs = refs[:several], refs[several + len(more) :]
+        values, outs = refs[:several], refs[several:]
         number = lax.broadcasted_iota(jnp.int32, (blocks * rows, local), 0)
         placing = jnp.where(number == slot_ref[...], 1.0, 0.0).astype(BF16)
         for which in range(several):
@@ -119,11 +117,18 @@
                 outs[block][which * rows : (which + 1) * rows, :] = placed[
                     block * rows : (block + 1) * rows
                 ]
-        if more:
-            outs[blocks][...] = refs[several][...]
-
-    shapes = [shape(several * rows, width)] * blocks + [shape(local, width)] * len(more)
-    return call(body, shapes, slots, *arrays, *more, after=after)
+        if hand_on:
+            outs[blocks][...] = slot_ref[...]
+
+    shapes = [shape(several * rows, width)] * blocks + [shape(1, local, jnp.int32)] * hand_on
+    return call(body, shapes, slots, *arrays, after=after, weight=weight)
+
+
+def handed_on(array, after):
+    def body(array_ref, out):
+        out[...] = array_ref[...]
+
+    return call(body, shape(*array.shape), array, after=after)
 
 
 def picked(slot_row, refs, base, rows):
@@ -262,7 +267,7 @@
     return [array[:, start : start + size] for start in range(0, array.shape[1], size)]
 
 
-def weight_gradients(which, own, pair_x, pair_c, hiddens, hidden_grads, capacity, dtype, after=(), flops=1):
+def weight_gradients(which, own, pair_x, pair_c, hiddens, hidden_grads, capacity, dtype, after=()):
     blocks = len(pair_x)
     width = pair_x[0].shape[1]
     half = hiddens[0].shape[1]
@@ -271,7 +276,8 @@
     def body(*refs):
         own, refs = refs[:blocks], refs[blocks:]
         tokens, grads, refs = refs[:blocks], refs[blocks : 2 * blocks], refs[2 * blocks :]
-        hidden, hidden_grad, out = refs[:2], refs[2:4], refs[4]
+        groups = len(hiddens)
+        hidden, hidden_grad, out = refs[:groups], refs[groups:-1], refs[-1]
         both = [jnp.concatenate([ref[...] for ref in pair], axis=0) for pair in (hidden, hidden_grad)]
         rows = [rows_of(own, which, capacity), rows_of(tokens, which, capacity)]
         up = dot(jnp.concatenate(rows, axis=0), both[1], ((0,), (0,)))
@@ -284,7 +290,7 @@
                 start += panel.shape[0]
 
     shapes = shape(2 * width * half // size, size, dtype)
-    return call(body, shapes, *own, *pair_x, *pair_c, *hiddens, *hidden_grads, after=after, flops=flops)
+    return call(body, shapes, *own, *pair_x, *pair_c, *hiddens, *hidden_grads, after=after)
 
 
 def joined(terms, peer, width, half, after=()):
@@ -302,8 +308,14 @@
     return call(body, [shape(width, half), shape(half, width)], terms, peer, after=after)
 
 
+def spread_from(parts, first):
+    return [
+        exchange(part, "expert", 2 * m) if m else part for m, part in enumerate(parts, first)
+    ]
+
+
 def spread(parts):
-    return [parts[0]] + [exchange(part, "expert", 2 * m) for m, part in enumerate(parts) if m]
+    return spread_from(parts, 0)
 
 
 def shards(tokens, gate_prob, routing, up_weight, down_weight, cotangent):
@@ -325,43 +337,56 @@
     slots, tokens, scaled = prepare(
         device, routing.reshape(1, local), gate_prob, tokens, cotangent, blocks, capacity
     )
-    sent = dispatch(slots, (tokens, scaled), blocks, rows, after=(ups[1], downs[1]))
+    *sent, own_slots = dispatch(
+        slots, (tokens, scaled), blocks, rows, True, after=(ups[1], downs[1]), weight=LIGHT
+    )
     own = spread(sent)
-    pair_slots = across(slots)
-    *sent, scaled = dispatch(pair_slots, (pair_tokens,), blocks, rows, scaled, after=(sent[0],))
+    pair_slots = across(own_slots)
+    scaled = handed_on(scaled, (pair_tokens, pair_slots))
+    pair_scaled = across(scaled)
+    sent = dispatch(pair_slots, (pair_tokens,), blocks, rows, after=(scaled,))
     pair_x = spread(sent)
-    pair_scaled = across(scaled)
-    own_sent, own_hidden, own_hidden_grad = both_ways(
-        own, ups, downs, capacity, after=(sent[0],)
-    )
-    sent, pair_hidden, pair_slope = forward(pair_x, ups, downs, capacity, after=(own_sent[0],))
-    back = spread(sent)
-    sent = dispatch(pair_slots, (pair_scaled,), blocks, rows, after=(sent[0],))
+    own_sent, own_hidden, own_hidden_grad = both_ways(own, ups, downs, capacity, after=(sent[0],))
+    half = blocks // 2
+
+    def in_two(step, arrays, after):
+        first = step(0, arrays[:half], after)
+        second = step(1, arrays[half:], (first[0][0],))
+        return [spread_from(first[0], 0) + spread_from(second[0], half), first[1:], second[1:]]
+
+    back, *ahead = in_two(
+        lambda _, parts, after: forward(parts, ups, downs, capacity, after=after),
+        pair_x,
+        (own_sent[0],),
+    )
+    sent = dispatch(pair_slots, (pair_scaled,), blocks, rows, after=(ahead[1][0][0],))
     pair_c = spread(sent)
     term = collect(pair_slots, back, after=(sent[0],))
     other_out = across(term)
-    sent, pair_hidden_grad = backward(pair_c, pair_slope, ups, downs, capacity, after=(term,))
-    back = spread(sent)
-
-    def gradients(which, dtype, after, flops):
+    back, *behind = in_two(
+        lambda part, parts, after: backward(parts, ahead[part][1], ups, downs, capacity, after=after),
+        pair_c,
+        (term,),
+    )
+
+    def gradients(which, dtype, after):
         return weight_gradients(
             which,
             own,
             pair_x,
             pair_c,
-            (own_hidden[which], pair_hidden[which]),
-            (own_hidden_grad[which], pair_hidden_grad[which]),
+            (own_hidden[which], ahead[0][0][which], ahead[1][0][which]),
+            (own_hidden_grad[which], behind[0][0][which], behind[1][0][which]),
             capacity,
             dtype,
             after,
-            flops,
         )
 
     term = collect(pair_slots, back, after=(other_out,))
     other_back = across(term)
     own_back = spread(own_sent)
-    give = gradients(1, BF16, (term,), 1 * 10**9)
-    keep = gradients(0, F32, (give,), 30 * 10**9)
+    give = gradients(1, BF16, (term,))
+    keep = gradients(0, F32, (give,))
     peer = exchange(give, "expert", 1)
     grad_up, grad_down = joined(keep, peer, *ups[0].shape)
     mixed, own_term = collect_own(slots, own_back, other_out, gate_prob, after=(pltpu.with_memory_space_constraint(grad_up, pltpu.HBM),))

time: 110 us -> 105 us (0.955)
  waiting for transfers between devices: 51.4 us -> 44 us
  starting transfers between devices: 29.1 us -> 33.5 us
  local copies, waits for them, and re-layouts: 3.28 us -> 1.97 us
    ppermute x26, waiting for transfers between devices: 51.4 us -> 44 us  [exchange(): lax.ppermute(array, axis, [(i, i ^ flip) for i in range(lax.axis_size(axi...]
    ppermute x26, starting transfers between devices: 29.1 us -> 33.5 us  [exchange(): lax.ppermute(array, axis, [(i, i ^ flip) for i in range(lax.axis_size(axi...]
    unnamed x18 -> x40, local copies, waits for them, and re-layouts: 3.28 us -> 1.97 us
    pallas_call x12 -> x15, Pallas kernels: 22.5 us -> 22.2 us  [call(): pl.pallas_call(kernel, out_shape=out_shape, in_specs=[pl.BlockSpec(memory...]
  transfers between devices with their start and end apart: 26 -> 26, of which waited for: 16 -> 10; matrix products, arithmetic and copies ran while one was open for 0% -> 0% of each run, Pallas kernels for 22% -> 23%
where the time goes in v4:
time: 105 us
  waiting for transfers between devices  44 us (42%)
  starting transfers between devices  33.5 us (32%)
  Pallas kernels  23.7 us (23%)
  local copies, waits for them, and re-layouts  1.97 us (2%)
    ppermute x26, waiting for transfers between devices, exchange(): lax.ppermute(array, axis, [(i, i ^ flip) for i in range(lax.axis_size(axi...  44 us
    ppermute x26, starting transfers between devices, exchange(): lax.ppermute(array, axis, [(i, i ^ flip) for i in range(lax.axis_size(axi...  33.5 us
    pallas_call x15, Pallas kernels, call(): pl.pallas_call(kernel, out_shape=out_shape, in_specs=[pl.BlockSpec(memory...  22.2 us
  transfers between devices with their start and end apart: 26, of which 10 were waited for; matrix products, arithmetic and copies ran while one was open for 0% of the time, Pallas kernels for 23%

profile of v4, /device:TPU:0, one launch (start us, length us, event | category | flops | bytes accessed | tf_op | source)
XLA Modules:
  0.0 105.0 jit_solution(1621429298996609713)
XLA Ops:
  0.6 0.5 collective-permute-start.1
  1.1 0.1 collective-permute-start.2
  1.2 4.0 %collective-permute-start = (bf16[320,768]{1,0:T(8,128)(2,1)}, bf16[320,768]{1,0:T(8,128)(2,1)S(1)}, u32[]{:S(2)}, u32[]{:S(2)}) collective-permute-start(bf16[320,768]{1,0:T(8,128)(2,1)} %token_ref.1), channel_id=1, source_target_pairs={{0,16},{8,24},{16,0},{24,8},{1,17},{9,25},{17,1},{25,9},{2,18},{10... | collective-permute-start | bytes 1474568 | tf_op jit(solution)/shard_map/ppermute | solution.py:18
  5.2 1.5 %shard_map.93 = (s32[1,320]{1,0:T(1,128)S(1)}, bf16[320,768]{1,0:T(8,128)(2,1)S(1)}, bf16[320,768]{1,0:T(8,128)(2,1)S(1)}) custom-call(s32[1]{0:T(128)} %bitcast.2.device_ref, s32[1,320]{1,0:T(1,128)} %bitcast.18, f32[320]{0:T(512)} %refs_7_.1, bf16[320,768]{1,0:T(8,128)(2,1)} %token_ref.1, bf16[320,768]{1,0:T(8,128)(2,1)} %cotangent_ref.1), custom_call_target="tpu_custom_call" | custom-call | flops 1 | bytes 1 | tf_op jit(solution)/shard_map/pallas_call | solution.py:89
  6.7 0.0 copy-start
  6.8 0.0 collective-permute-done.2.refs_1_.refs_8_.refs_6_
  6.8 0.0 copy-start.2
  6.8 1.2 %shard_map.94 = (bf16[320,768]{1,0:T(8,128)(2,1)S(1)}, bf16[320,768]{1,0:T(8,128)(2,1)S(1)}, bf16[320,768]{1,0:T(8,128)(2,1)S(1)}, bf16[320,768]{1,0:T(8,128)(2,1)S(1)}, s32[1,320]{1,0:T(1,128)S(1)}) custom-call(bf16[768,512]{1,0:T(8,128)(2,1)S(1)} %collective-permute-done.1.refs_0_.refs_6_.refs_4_, ...), custom_call_target="tpu_custom_call" | custom-call | flops 1 | bytes 1 | tf_op jit(solution)/shard_map/pallas_call | solution.py:31
  8.0 1.6 %collective-permute-start.3 = (s32[1,320]{1,0:T(1,128)S(1)}, s32[1,320]{1,0:T(1,128)S(1)}, u32[]{:S(2)}, u32[]{:S(2)}) collective-permute-start(s32[1,320]{1,0:T(1,128)S(1)} %get-tuple-element.55), channel_id=1, source_target_pairs={{0,16},{8,24},{16,0},{24,8},{1,17},{9,25},{17,1},{25,9},{2,18},{10... | collective-permute-start | bytes 3848 | tf_op jit(solution)/shard_map/ppermute | solution.py:18
  9.6 1.5 %collective-permute-start.4 = (bf16[320,768]{1,0:T(8,128)(2,1)S(1)}, bf16[320,768]{1,0:T(8,128)(2,1)S(1)}, u32[]{:S(2)}, u32[]{:S(2)}) collective-permute-start(bf16[320,768]{1,0:T(8,128)(2,1)S(1)} %get-tuple-element.58), channel_id=1, source_target_pairs={{0,2},{1,3},{2,0},{3,1},{4,6},{5,7},{6,4},{7,5},{8,10},{9,11},{10,... | collective-permute-start | bytes 1474568 | tf_op jit(solution)/shard_map/ppermute | solution.py:18
  11.1 1.5 %collective-permute-start.5 = (bf16[320,768]{1,0:T(8,128)(2,1)S(1)}, bf16[320,768]{1,0:T(8,128)(2,1)S(1)}, u32[]{:S(2)}, u32[]{:S(2)}) collective-permute-start(bf16[320,768]{1,0:T(8,128)(2,1)S(1)} %get-tuple-element.59), channel_id=1, source_target_pairs={{0,4},{1,5},{2,6},{3,7},{4,0},{5,1},{6,2},{7,3},{8,12},{9,13},{10,... | collective-permute-start | bytes 1474568 | tf_op jit(solution)/shard_map/ppermute | solution.py:18
  12.6 0.5 collective-permute-start.6
  13.1 14.4 %collective-permute-done.refs_0_.refs_2_ = bf16[320,768]{1,0:T(8,128)(2,1)S(1)} collective-permute-done((bf16[320,768]{1,0:T(8,128)(2,1)}, bf16[320,768]{1,0:T(8,128)(2,1)S(1)}, u32[]{:S(2)}, u32[]{:S(2)}) %collective-permute-start) | collective-permute-done | bytes 491552 | tf_op jit(solution)/shard_map/ppermute | solution.py:18
  27.5 0.0 collective-permute-done.3.refs_1_
  27.6 0.1 collective-permute-start.10
  27.7 0.7 shard_map.96
  28.4 0.0 copy-start.16
  28.4 1.6 %collective-permute-start.7 = (bf16[160,768]{1,0:T(8,128)(2,1)S(1)}, bf16[160,768]{1,0:T(8,128)(2,1)S(1)}, u32[]{:S(2)}, u32[]{:S(2)}) collective-permute-start(bf16[160,768]{1,0:T(8,128)(2,1)S(1)} %get-tuple-element.62), channel_id=1, source_target_pairs={{0,2},{1,3},{2,0},{3,1},{4,6},{5,7},{6,4},{7,5},{8,10},{9,11},{10,... | collective-permute-start | bytes 737288 | tf_op jit(solution)/shard_map/ppermute | solution.py:18
  30.0 1.5 %collective-permute-start.8 = (bf16[160,768]{1,0:T(8,128)(2,1)S(1)}, bf16[160,768]{1,0:T(8,128)(2,1)S(1)}, u32[]{:S(2)}, u32[]{:S(2)}) collective-permute-start(bf16[160,768]{1,0:T(8,128)(2,1)S(1)} %get-tuple-element.64), channel_id=1, source_target_pairs={{0,4},{1,5},{2,6},{3,7},{4,0},{5,1},{6,2},{7,3},{8,12},{9,13},{10,... | collective-permute-start | bytes 737288 | tf_op jit(solution)/shard_map/ppermute | solution.py:18
  31.5 3.0 %collective-permute-done.5.refs_3_ = bf16[320,768]{1,0:T(8,128)(2,1)S(1)} collective-permute-done((bf16[320,768]{1,0:T(8,128)(2,1)S(1)}, bf16[320,768]{1,0:T(8,128)(2,1)S(1)}, u32[]{:S(2)}, u32[]{:S(2)}) %collective-permute-start.5) | collective-permute-done | bytes 491552 | tf_op jit(solution)/shard_map/ppermute | solution.py:18
  34.5 0.8 collective-permute-start.9
  35.3 0.0 collective-permute-done.6.refs_4_
  35.3 0.0 copy-start.8
  35.3 4.7 %shard_map.97 = (bf16[320,768]{1,0:T(8,128)(2,1)S(1)}, bf16[320,768]{1,0:T(8,128)(2,1)S(1)}, bf16[320,768]{1,0:T(8,128)(2,1)S(1)}, bf16[320,768]{1,0:T(8,128)(2,...) custom-call(bf16[160,768]{1,0:T(8,128)(2,1)S(1)} %get-tuple-element., ...), custom_call_target="tpu_custom_call" | custom-call | flops 30000001024 | bytes 1 | tf_op jit(solution)/shard_map/pallas_call | solution.py:31
  40.0 0.0 copy-start.14
  40.0 1.2 %shard_map.98 = (bf16[160,768]{1,0:T(8,128)(2,1)S(1)}, bf16[160,768]{1,0:T(8,128)(2,1)S(1)}, bf16[160,512]{1,0:T(8,128)(2,1)S(1)}, bf16[160,512]{1,0:T(8,128)(2,...) custom-call(bf16[320,768]{1,0:T(8,128)(2,1)S(1)} %get-tuple-element.61.refs_0_.refs_2_, ...), custom_call_target="tpu_custom_call" | custom-call | flops 30000001024 | bytes 1 | tf_op jit(solution)/shard_map/pallas_call | solution.py:31
  41.2 3.2 %collective-permute-start.11 = (bf16[160,768]{1,0:T(8,128)(2,1)S(1)}, bf16[160,768]{1,0:T(8,128)(2,1)S(1)}, u32[]{:S(2)}, u32[]{:S(2)}) collective-permute-start(bf16[160,768]{1,0:T(8,128)(2,1)S(1)} %get-tuple-element.68), channel_id=1, source_target_pairs={{0,2},{1,3},{2,0},{3,1},{4,6},{5,7},{6,4},{7,5},{8,10},{9,11},{10,... | collective-permute-start | bytes 737288 | tf_op jit(solution)/shard_map/ppermute | solution.py:18
  44.5 1.4 %collective-permute-done.9.refs_2_.refs_8_ = bf16[160,768]{1,0:T(8,128)(2,1)S(1)} collective-permute-done((bf16[160,768]{1,0:T(8,128)(2,1)S(1)}, bf16[160,768]{1,0:T(8,128)(2,1)S(1)}, u32[]{:S(2)}, u32[]{:S(2)}) %collective-permute-start.9) | collective-permute-done | bytes 245792 | tf_op jit(solution)/shard_map/ppermute | solution.py:18
  45.8 1.2 %shard_map.99 = (bf16[160,768]{1,0:T(8,128)(2,1)S(1)}, bf16[160,768]{1,0:T(8,128)(2,1)S(1)}, bf16[160,512]{1,0:T(8,128)(2,1)S(1)}, bf16[160,512]{1,0:T(8,128)(2,...) custom-call(bf16[160,768]{1,0:T(8,128)(2,1)S(1)} %get-tuple-element.63.refs_0_.refs_2_, ...), custom_call_target="tpu_custom_call" | custom-call | flops 30000001024 | bytes 1 | tf_op jit(solution)/shard_map/pallas_call | solution.py:31
  47.0 1.0 collective-permute-start.12
  48.1 1.9 %collective-permute-start.13 = (bf16[160,768]{1,0:T(8,128)(2,1)S(1)}, bf16[160,768]{1,0:T(8,128)(2,1)S(1)}, u32[]{:S(2)}, u32[]{:S(2)}) collective-permute-start(bf16[160,768]{1,0:T(8,128)(2,1)S(1)} %get-tuple-element.70), channel_id=1, source_target_pairs={{0,6},{1,7},{2,4},{3,5},{4,2},{5,3},{6,0},{7,1},{8,14},{9,15},{10,... | collective-permute-start | bytes 737288 | tf_op jit(solution)/shard_map/ppermute | solution.py:18
  50.0 1.8 %collective-permute-done.10.refs_2_ = bf16[320,768]{1,0:T(8,128)(2,1)S(1)} collective-permute-done((bf16[320,768]{1,0:T(8,128)(2,1)S(1)}, bf16[320,768]{1,0:T(8,128)(2,1)S(1)}, u32[]{:S(2)}, u32[]{:S(2)}) %collective-permute-start.10) | collective-permute-done | bytes 491552 | tf_op jit(solution)/shard_map/ppermute | solution.py:18
  51.8 0.7 shard_map.100
  52.4 1.3 %collective-permute-start.15 = (bf16[160,768]{1,0:T(8,128)(2,1)S(1)}, bf16[160,768]{1,0:T(8,128)(2,1)S(1)}, u32[]{:S(2)}, u32[]{:S(2)}) collective-permute-start(bf16[160,768]{1,0:T(8,128)(2,1)S(1)} %get-tuple-element.71), channel_id=1, source_target_pairs={{0,2},{1,3},{2,0},{3,1},{4,6},{5,7},{6,4},{7,5},{8,10},{9,11},{10,... | collective-permute-start | bytes 737288 | tf_op jit(solution)/shard_map/ppermute | solution.py:18
  53.7 1.5 %collective-permute-start.17 = (bf16[160,768]{1,0:T(8,128)(2,1)S(1)}, bf16[160,768]{1,0:T(8,128)(2,1)S(1)}, u32[]{:S(2)}, u32[]{:S(2)}) collective-permute-start(bf16[160,768]{1,0:T(8,128)(2,1)S(1)} %get-tuple-element.76), channel_id=1, source_target_pairs={{0,4},{1,5},{2,6},{3,7},{4,0},{5,1},{6,2},{7,3},{8,12},{9,13},{10,... | collective-permute-start | bytes 737288 | tf_op jit(solution)/shard_map/ppermute | solution.py:18
  55.3 0.7 collective-permute-start.18
  56.0 5.6 %collective-permute-done.12.refs_4_ = bf16[160,768]{1,0:T(8,128)(2,1)S(1)} collective-permute-done((bf16[160,768]{1,0:T(8,128)(2,1)S(1)}, bf16[160,768]{1,0:T(8,128)(2,1)S(1)}, u32[]{:S(2)}, u32[]{:S(2)}) %collective-permute-start.12) | collective-permute-done | bytes 245792 | tf_op jit(solution)/shard_map/ppermute | solution.py:18
  61.6 0.0 collective-permute-done.13.refs_5_
  61.6 0.6 shard_map.101.refs_0_
  62.2 1.8 %collective-permute-start.14 = (bf16[320,768]{1,0:T(8,128)(2,1)S(1)}, bf16[320,768]{1,0:T(8,128)(2,1)S(1)}, u32[]{:S(2)}, u32[]{:S(2)}) collective-permute-start(bf16[320,768]{1,0:T(8,128)(2,1)S(1)} %shard_map.101.refs_0_), channel_id=1, source_target_pairs={{0,16},{8,24},{16,0},{24,8},{1,17},{9,25},{17,1},{25,9},{2,18},{10... | collective-permute-start | bytes 1474568 | tf_op jit(solution)/shard_map/ppermute | solution.py:18
  64.1 0.0 collective-permute-done.15.refs_2_.refs_10_
  64.1 1.3 %shard_map.102 = (bf16[160,768]{1,0:T(8,128)(2,1)S(1)}, bf16[160,768]{1,0:T(8,128)(2,1)S(1)}, bf16[160,512]{1,0:T(8,128)(2,1)S(1)}, bf16[160,512]{1,0:T(8,128)(2,1)S(1)}) custom-call(bf16[320,768]{1,0:T(8,128)(2,1)S(1)} %shard_map.101.refs_0_, bf16[160,768]{1,0:T(8,128)(2,1)S(1)} %get-tuple-element.67.refs_0_.refs_1_.refs_9_, ...), custom_call_target="tpu_custom_call" | custom-call | flops 30000001024 | bytes 1 | tf_op jit(solution)/shard_map/pallas_call | solution.py:31
  65.3 1.5 %collective-permute-start.16 = (bf16[160,768]{1,0:T(8,128)(2,1)S(1)}, bf16[160,768]{1,0:T(8,128)(2,1)S(1)}, u32[]{:S(2)}, u32[]{:S(2)}) collective-permute-start(bf16[160,768]{1,0:T(8,128)(2,1)S(1)} %get-tuple-element.75), channel_id=1, source_target_pairs={{0,2},{1,3},{2,0},{3,1},{4,6},{5,7},{6,4},{7,5},{8,10},{9,11},{10,... | collective-permute-start | bytes 737288 | tf_op jit(solution)/shard_map/ppermute | solution.py:18
  66.9 1.9 %collective-permute-done.17.refs_1_.refs_11_ = bf16[160,768]{1,0:T(8,128)(2,1)S(1)} collective-permute-done((bf16[160,768]{1,0:T(8,128)(2,1)S(1)}, bf16[160,768]{1,0:T(8,128)(2,1)S(1)}, u32[]{:S(2)}, u32[]{:S(2)}) %collective-permute-start.17) | collective-permute-done | bytes 245792 | tf_op jit(solution)/shard_map/ppermute | solution.py:18
  68.8 0.0 collective-permute-done.18.refs_2_.refs_12_
  68.8 1.3 %shard_map.103 = (bf16[160,768]{1,0:T(8,128)(2,1)S(1)}, bf16[160,768]{1,0:T(8,128)(2,1)S(1)}, bf16[160,512]{1,0:T(8,128)(2,1)S(1)}, bf16[160,512]{1,0:T(8,128)(2,1)S(1)}) custom-call(bf16[160,768]{1,0:T(8,128)(2,1)S(1)} %get-tuple-element.74.refs_0_.refs_2_, bf16[160,768]{1,0:T(8,128)(2,1)S(1)} %collective-permute-done.17.refs_1_.refs_11_, ...), custom_call_target="tpu_custom_call" | custom-call | flops 30000001024 | bytes 1 | tf_op jit(solution)/shard_map/pallas_call | solution.py:31
  70.1 0.3 collective-permute-start.19
  70.4 2.5 %collective-permute-start.20 = (bf16[160,768]{1,0:T(8,128)(2,1)S(1)}, bf16[160,768]{1,0:T(8,128)(2,1)S(1)}, u32[]{:S(2)}, u32[]{:S(2)}) collective-permute-start(bf16[160,768]{1,0:T(8,128)(2,1)S(1)} %get-tuple-element.81), channel_id=1, source_target_pairs={{0,6},{1,7},{2,4},{3,5},{4,2},{5,3},{6,0},{7,1},{8,14},{9,15},{10,... | collective-permute-start | bytes 737288 | tf_op jit(solution)/shard_map/ppermute | solution.py:18
  72.9 0.7 collective-permute-start.22
  73.6 0.0 collective-permute-done.16.refs_3_
  73.6 0.4 collective-permute-start.23
  74.1 8.4 %collective-permute-done.19.refs_4_ = bf16[160,768]{1,0:T(8,128)(2,1)S(1)} collective-permute-done((bf16[160,768]{1,0:T(8,128)(2,1)S(1)}, bf16[160,768]{1,0:T(8,128)(2,1)S(1)}, u32[]{:S(2)}, u32[]{:S(2)}) %collective-permute-start.19) | collective-permute-done | bytes 245792 | tf_op jit(solution)/shard_map/ppermute | solution.py:18
  82.5 2.1 %collective-permute-start.24 = (bf16[320,768]{1,0:T(8,128)(2,1)S(1)}, bf16[320,768]{1,0:T(8,128)(2,1)S(1)}, u32[]{:S(2)}, u32[]{:S(2)}) collective-permute-start(bf16[320,768]{1,0:T(8,128)(2,1)S(1)} %get-tuple-element.96), channel_id=1, source_target_pairs={{0,6},{1,7},{2,4},{3,5},{4,2},{5,3},{6,0},{7,1},{8,14},{9,15},{10,... | collective-permute-start | bytes 1474568 | tf_op jit(solution)/shard_map/ppermute | solution.py:18
  84.6 0.6 shard_map.104.refs_0_
  85.2 0.6 collective-permute-start.25
  85.8 2.8 %shard_map.105.refs_0_ = bf16[3072,256]{1,0:T(8,128)(2,1)} custom-call(bf16[320,768]{1,0:T(8,128)(2,1)S(1)} %shard_map.104.refs_0_, bf16[320,768]{1,0:T(8,128)(2,1)S(1)} %get-tuple-element.57.refs_1_, bf16[320,768]{1,0:T(8,128)(2,1)S(1)} %collective-permute-done.4.refs_2_, bf16[320,768]{1,0:T(8,128)(2,1)S(1)} %collective-permute-done.5.refs_3_, ...), custom_call_target="tpu_custom_call" | custom-call | flops 30000001024 | bytes 1 | tf_op jit(solution)/shard_map/pallas_call | solution.py:31
  88.6 3.1 %shard_map.106.refs_0_ = f32[3072,256]{1,0:T(8,128)} custom-call(bf16[3072,256]{1,0:T(8,128)(2,1)} %shard_map.105.refs_0_, bf16[320,768]{1,0:T(8,128)(2,1)S(1)} %get-tuple-element.57.refs_1_, bf16[320,768]{1,0:T(8,128)(2,1)S(1)} %collective-permute-done.4.refs_2_, bf16[320,768]{1,0:T(8,128)(2,1)S(1)} %collective-permute-done.5.refs_3_, ...), custom_call_target="tpu_custom_call" | custom-call | flops 30000001024 | bytes 1 | tf_op jit(solution)/shard_map/pallas_call | solution.py:31
  91.7 0.5 collective-permute-done.21.refs_1_
  92.2 1.9 %copy-done.13 = f32[3072,256]{1,0:T(8,128)S(1)} copy-done((f32[3072,256]{1,0:T(8,128)S(1)}, f32[3072,256]{1,0:T(8,128)}, u32[]{:S(2)}) %copy-start.13) | copy-done | bytes 3145752
  94.1 1.3 %shard_map.107 = (bf16[768,512]{1,0:T(8,128)(2,1)}, bf16[512,768]{1,0:T(8,128)(2,1)}) custom-call(f32[3072,256]{1,0:T(8,128)S(1)} %copy-done.13, bf16[3072,256]{1,0:T(8,128)(2,1)S(1)} %collective-permute-done.21.refs_1_), custom_call_target="tpu_custom_call" | custom-call | flops 30000001024 | bytes 1 | tf_op jit(solution)/shard_map/pallas_call | solution.py:31
  95.5 6.2 %collective-permute-done.23.refs_4_ = bf16[320,768]{1,0:T(8,128)(2,1)S(1)} collective-permute-done((bf16[320,768]{1,0:T(8,128)(2,1)S(1)}, bf16[320,768]{1,0:T(8,128)(2,1)S(1)}, u32[]{:S(2)}, u32[]{:S(2)}) %collective-permute-start.23) | collective-permute-done | bytes 491552 | tf_op jit(solution)/shard_map/ppermute | solution.py:18
  101.7 1.6 %shard_map.108 = (bf16[320,768]{1,0:T(8,128)(2,1)}, bf16[320,768]{1,0:T(8,128)(2,1)S(1)}) custom-call(bf16[768,512]{1,0:T(8,128)(2,1)} %get-tuple-element.93.refs_0_, s32[1,320]{1,0:T(1,128)S(1)} %copy-done.6, bf16[320,768]{1,0:T(8,128)(2,1)S(1)} %copy-done.15, bf16[320,768]{1,0:T(8,128)(2,1)S(1)} %collective-permute-done.22.refs_3_, ...), custom_call_target="tpu_custom_call" | custom-call | flops 30000001024 | bytes 1 | tf_op jit(solution)/shard_map/pallas_call | solution.py:31
  103.3 0.8 collective-permute-done.25
  104.1 0.9 add_convert_fusion
  (45 shorter events, 0.1 us)
Async XLA Ops:
  0.6 6.1 %collective-permute-start.1 = (bf16[768,512]{1,0:T(8,128)(2,1)}, bf16[768,512]{1,0:T(8,128)(2,1)S(1)}, u32[]{:S(2)}, u32[]{:S(2)}) collective-permute-start(bf16[768,512]{1,0:T(8,128)(2,1)} %bitcast.6), channel_id=1, source_target_pairs={{0,1},{1,0},{2,3},{3,2},{4,5},{5,4},{6,7},{7,6},{8,9},{9,8},{10,11... | collective-permute-start | bytes 2359304 | tf_op jit(solution)/shard_map/ppermute | solution.py:18
  1.1 5.6 %collective-permute-start.2 = (bf16[512,768]{1,0:T(8,128)(2,1)}, bf16[512,768]{1,0:T(8,128)(2,1)S(1)}, u32[]{:S(2)}, u32[]{:S(2)}) collective-permute-start(bf16[512,768]{1,0:T(8,128)(2,1)} %bitcast.12), channel_id=1, source_target_pairs={{0,1},{1,0},{2,3},{3,2},{4,5},{5,4},{6,7},{7,6},{8,9},{9,8},{10,11... | collective-permute-start | bytes 2359304 | tf_op jit(solution)/shard_map/ppermute | solution.py:18
  1.2 26.3 %collective-permute-start = (bf16[320,768]{1,0:T(8,128)(2,1)}, bf16[320,768]{1,0:T(8,128)(2,1)S(1)}, u32[]{:S(2)}, u32[]{:S(2)}) collective-permute-start(bf16[320,768]{1,0:T(8,128)(2,1)} %token_ref.1), channel_id=1, source_target_pairs={{0,16},{8,24},{16,0},{24,8},{1,17},{9,25},{17,1},{25,9},{2,18},{10... | collective-permute-start | bytes 1474568 | tf_op jit(solution)/shard_map/ppermute | solution.py:18
  6.7 20.9 %copy-start.5 = (s32[1,320]{1,0:T(1,128)}, s32[1,320]{1,0:T(1,128)S(1)}, u32[]{:S(2)}) copy-start(s32[1,320]{1,0:T(1,128)S(1)} %get-tuple-element.52.refs_2_.refs_1_) | copy-start | bytes 3844
  6.7 20.9 %copy-start = (bf16[768,512]{1,0:T(8,128)(2,1)}, bf16[768,512]{1,0:T(8,128)(2,1)S(1)}, u32[]{:S(2)}) copy-start(bf16[768,512]{1,0:T(8,128)(2,1)S(1)} %collective-permute-done.1.refs_0_.refs_6_.refs_4_) | copy-start | bytes 2359300
  6.8 20.8 %copy-start.2 = (bf16[512,768]{1,0:T(8,128)(2,1)}, bf16[512,768]{1,0:T(8,128)(2,1)S(1)}, u32[]{:S(2)}) copy-start(bf16[512,768]{1,0:T(8,128)(2,1)S(1)} %collective-permute-done.2.refs_1_.refs_8_.refs_6_) | copy-start | bytes 2359300
  8.0 19.6 %collective-permute-start.3 = (s32[1,320]{1,0:T(1,128)S(1)}, s32[1,320]{1,0:T(1,128)S(1)}, u32[]{:S(2)}, u32[]{:S(2)}) collective-permute-start(s32[1,320]{1,0:T(1,128)S(1)} %get-tuple-element.55), channel_id=1, source_target_pairs={{0,16},{8,24},{16,0},{24,8},{1,17},{9,25},{17,1},{25,9},{2,18},{10... | collective-permute-start | bytes 3848 | tf_op jit(solution)/shard_map/ppermute | solution.py:18
  9.6 20.4 %collective-permute-start.4 = (bf16[320,768]{1,0:T(8,128)(2,1)S(1)}, bf16[320,768]{1,0:T(8,128)(2,1)S(1)}, u32[]{:S(2)}, u32[]{:S(2)}) collective-permute-start(bf16[320,768]{1,0:T(8,128)(2,1)S(1)} %get-tuple-element.58), channel_id=1, source_target_pairs={{0,2},{1,3},{2,0},{3,1},{4,6},{5,7},{6,4},{7,5},{8,10},{9,11},{10,... | collective-permute-start | bytes 1474568 | tf_op jit(solution)/shard_map/ppermute | solution.py:18
  11.1 23.4 %collective-permute-start.5 = (bf16[320,768]{1,0:T(8,128)(2,1)S(1)}, bf16[320,768]{1,0:T(8,128)(2,1)S(1)}, u32[]{:S(2)}, u32[]{:S(2)}) collective-permute-start(bf16[320,768]{1,0:T(8,128)(2,1)S(1)} %get-tuple-element.59), channel_id=1, source_target_pairs={{0,4},{1,5},{2,6},{3,7},{4,0},{5,1},{6,2},{7,3},{8,12},{9,13},{10,... | collective-permute-start | bytes 1474568 | tf_op jit(solution)/shard_map/ppermute | solution.py:18
  12.6 22.6 %collective-permute-start.6 = (bf16[320,768]{1,0:T(8,128)(2,1)S(1)}, bf16[320,768]{1,0:T(8,128)(2,1)S(1)}, u32[]{:S(2)}, u32[]{:S(2)}) collective-permute-start(bf16[320,768]{1,0:T(8,128)(2,1)S(1)} %get-tuple-element.60), channel_id=1, source_target_pairs={{0,6},{1,7},{2,4},{3,5},{4,2},{5,3},{6,0},{7,1},{8,14},{9,15},{10,... | collective-permute-start | bytes 1474568 | tf_op jit(solution)/shard_map/ppermute | solution.py:18
  27.6 24.2 %collective-permute-start.10 = (bf16[320,768]{1,0:T(8,128)(2,1)S(1)}, bf16[320,768]{1,0:T(8,128)(2,1)S(1)}, u32[]{:S(2)}, u32[]{:S(2)}) collective-permute-start(bf16[320,768]{1,0:T(8,128)(2,1)S(1)} %shard_map.95.refs_0_), channel_id=1, source_target_pairs={{0,16},{8,24},{16,0},{24,8},{1,17},{9,25},{17,1},{25,9},{2,18},{10... | collective-permute-start | bytes 1474568 | tf_op jit(solution)/shard_map/ppermute | solution.py:18
  28.4 11.6 %copy-start.16 = (bf16[160,768]{1,0:T(8,128)(2,1)}, bf16[160,768]{1,0:T(8,128)(2,1)S(1)}, u32[]{:S(2)}) copy-start(bf16[160,768]{1,0:T(8,128)(2,1)S(1)} %get-tuple-element.56.refs_0_.refs_1_.refs_5_) | copy-start | bytes 737284
  28.4 11.6 %collective-permute-start.7 = (bf16[160,768]{1,0:T(8,128)(2,1)S(1)}, bf16[160,768]{1,0:T(8,128)(2,1)S(1)}, u32[]{:S(2)}, u32[]{:S(2)}) collective-permute-start(bf16[160,768]{1,0:T(8,128)(2,1)S(1)} %get-tuple-element.62), channel_id=1, source_target_pairs={{0,2},{1,3},{2,0},{3,1},{4,6},{5,7},{6,4},{7,5},{8,10},{9,11},{10,... | collective-permute-start | bytes 737288 | tf_op jit(solution)/shard_map/ppermute | solution.py:18
  30.0 14.5 %collective-permute-start.8 = (bf16[160,768]{1,0:T(8,128)(2,1)S(1)}, bf16[160,768]{1,0:T(8,128)(2,1)S(1)}, u32[]{:S(2)}, u32[]{:S(2)}) collective-permute-start(bf16[160,768]{1,0:T(8,128)(2,1)S(1)} %get-tuple-element.64), channel_id=1, source_target_pairs={{0,4},{1,5},{2,6},{3,7},{4,0},{5,1},{6,2},{7,3},{8,12},{9,13},{10,... | collective-permute-start | bytes 737288 | tf_op jit(solution)/shard_map/ppermute | solution.py:18
  34.5 11.3 %collective-permute-start.9 = (bf16[160,768]{1,0:T(8,128)(2,1)S(1)}, bf16[160,768]{1,0:T(8,128)(2,1)S(1)}, u32[]{:S(2)}, u32[]{:S(2)}) collective-permute-start(bf16[160,768]{1,0:T(8,128)(2,1)S(1)} %get-tuple-element.65), channel_id=1, source_target_pairs={{0,6},{1,7},{2,4},{3,5},{4,2},{5,3},{6,0},{7,1},{8,14},{9,15},{10,... | collective-permute-start | bytes 737288 | tf_op jit(solution)/shard_map/ppermute | solution.py:18
  35.3 4.7 %copy-start.1 = (bf16[768,512]{1,0:T(8,128)(2,1)S(1)}, bf16[768,512]{1,0:T(8,128)(2,1)}, u32[]{:S(2)}) copy-start(bf16[768,512]{1,0:T(8,128)(2,1)} %copy-done) | copy-start | bytes 2359300
  35.3 4.8 %copy-start.3 = (bf16[512,768]{1,0:T(8,128)(2,1)S(1)}, bf16[512,768]{1,0:T(8,128)(2,1)}, u32[]{:S(2)}) copy-start(bf16[512,768]{1,0:T(8,128)(2,1)} %copy-done.2) | copy-start | bytes 2359300
  35.3 4.8 %copy-start.7 = (bf16[1,768,512]{2,1,0:T(8,128)(2,1)S(1)}, bf16[1,768,512]{2,1,0:T(8,128)(2,1)}, u32[]{:S(2)}) copy-start(bf16[1,768,512]{2,1,0:T(8,128)(2,1)} %param.9) | copy-start | bytes 2359300
  35.3 4.8 %copy-start.8 = (bf16[1,512,768]{2,1,0:T(8,128)(2,1)S(1)}, bf16[1,512,768]{2,1,0:T(8,128)(2,1)}, u32[]{:S(2)}) copy-start(bf16[1,512,768]{2,1,0:T(8,128)(2,1)} %param.10) | copy-start | bytes 2359300
  40.0 1.3 %copy-start.14 = (bf16[320,768]{1,0:T(8,128)(2,1)}, bf16[320,768]{1,0:T(8,128)(2,1)S(1)}, u32[]{:S(2)}) copy-start(bf16[320,768]{1,0:T(8,128)(2,1)S(1)} %get-tuple-element.61.refs_0_.refs_2_) | copy-start | bytes 1474564
  41.2 14.0 %collective-permute-start.11 = (bf16[160,768]{1,0:T(8,128)(2,1)S(1)}, bf16[160,768]{1,0:T(8,128)(2,1)S(1)}, u32[]{:S(2)}, u32[]{:S(2)}) collective-permute-start(bf16[160,768]{1,0:T(8,128)(2,1)S(1)} %get-tuple-element.68), channel_id=1, source_target_pairs={{0,2},{1,3},{2,0},{3,1},{4,6},{5,7},{6,4},{7,5},{8,10},{9,11},{10,... | collective-permute-start | bytes 737288 | tf_op jit(solution)/shard_map/ppermute | solution.py:18
  44.5 2.5 %copy-start.9 = (bf16[160,768]{1,0:T(8,128)(2,1)}, bf16[160,768]{1,0:T(8,128)(2,1)S(1)}, u32[]{:S(2)}) copy-start(bf16[160,768]{1,0:T(8,128)(2,1)S(1)} %collective-permute-done.8.refs_1_.refs_7_) | copy-start | bytes 737284
  45.8 1.2 %copy-start.11 = (bf16[160,768]{1,0:T(8,128)(2,1)}, bf16[160,768]{1,0:T(8,128)(2,1)S(1)}, u32[]{:S(2)}) copy-start(bf16[160,768]{1,0:T(8,128)(2,1)S(1)} %collective-permute-done.9.refs_2_.refs_8_) | copy-start | bytes 737284
  47.0 5.4 %copy-start.18 = (bf16[160,512]{1,0:T(8,128)(2,1)}, bf16[160,512]{1,0:T(8,128)(2,1)S(1)}, u32[]{:S(2)}) copy-start(bf16[160,512]{1,0:T(8,128)(2,1)S(1)} %get-tuple-element.66.refs_0_.refs_15_) | copy-start | bytes 491524
  47.0 14.6 %collective-permute-start.12 = (bf16[160,768]{1,0:T(8,128)(2,1)S(1)}, bf16[160,768]{1,0:T(8,128)(2,1)S(1)}, u32[]{:S(2)}, u32[]{:S(2)}) collective-permute-start(bf16[160,768]{1,0:T(8,128)(2,1)S(1)} %get-tuple-element.69), channel_id=1, source_target_pairs={{0,4},{1,5},{2,6},{3,7},{4,0},{5,1},{6,2},{7,3},{8,12},{9,13},{10,... | collective-permute-start | bytes 737288 | tf_op jit(solution)/shard_map/ppermute | solution.py:18
  48.1 13.5 %collective-permute-start.13 = (bf16[160,768]{1,0:T(8,128)(2,1)S(1)}, bf16[160,768]{1,0:T(8,128)(2,1)S(1)}, u32[]{:S(2)}, u32[]{:S(2)}) collective-permute-start(bf16[160,768]{1,0:T(8,128)(2,1)S(1)} %get-tuple-element.70), channel_id=1, source_target_pairs={{0,6},{1,7},{2,4},{3,5},{4,2},{5,3},{6,0},{7,1},{8,14},{9,15},{10,... | collective-permute-start | bytes 737288 | tf_op jit(solution)/shard_map/ppermute | solution.py:18
  52.4 11.6 %collective-permute-start.15 = (bf16[160,768]{1,0:T(8,128)(2,1)S(1)}, bf16[160,768]{1,0:T(8,128)(2,1)S(1)}, u32[]{:S(2)}, u32[]{:S(2)}) collective-permute-start(bf16[160,768]{1,0:T(8,128)(2,1)S(1)} %get-tuple-element.71), channel_id=1, source_target_pairs={{0,2},{1,3},{2,0},{3,1},{4,6},{5,7},{6,4},{7,5},{8,10},{9,11},{10,... | collective-permute-start | bytes 737288 | tf_op jit(solution)/shard_map/ppermute | solution.py:18
  53.7 15.0 %collective-permute-start.17 = (bf16[160,768]{1,0:T(8,128)(2,1)S(1)}, bf16[160,768]{1,0:T(8,128)(2,1)S(1)}, u32[]{:S(2)}, u32[]{:S(2)}) collective-permute-start(bf16[160,768]{1,0:T(8,128)(2,1)S(1)} %get-tuple-element.76), channel_id=1, source_target_pairs={{0,4},{1,5},{2,6},{3,7},{4,0},{5,1},{6,2},{7,3},{8,12},{9,13},{10,... | collective-permute-start | bytes 737288 | tf_op jit(solution)/shard_map/ppermute | solution.py:18
  55.3 13.5 %collective-permute-start.18 = (bf16[160,768]{1,0:T(8,128)(2,1)S(1)}, bf16[160,768]{1,0:T(8,128)(2,1)S(1)}, u32[]{:S(2)}, u32[]{:S(2)}) collective-permute-start(bf16[160,768]{1,0:T(8,128)(2,1)S(1)} %get-tuple-element.77), channel_id=1, source_target_pairs={{0,6},{1,7},{2,4},{3,5},{4,2},{5,3},{6,0},{7,1},{8,14},{9,15},{10,... | collective-permute-start | bytes 737288 | tf_op jit(solution)/shard_map/ppermute | solution.py:18
  62.2 22.3 %collective-permute-start.14 = (bf16[320,768]{1,0:T(8,128)(2,1)S(1)}, bf16[320,768]{1,0:T(8,128)(2,1)S(1)}, u32[]{:S(2)}, u32[]{:S(2)}) collective-permute-start(bf16[320,768]{1,0:T(8,128)(2,1)S(1)} %shard_map.101.refs_0_), channel_id=1, source_target_pairs={{0,16},{8,24},{16,0},{24,8},{1,17},{9,25},{17,1},{25,9},{2,18},{10... | collective-permute-start | bytes 1474568 | tf_op jit(solution)/shard_map/ppermute | solution.py:18
  65.3 8.3 %collective-permute-start.16 = (bf16[160,768]{1,0:T(8,128)(2,1)S(1)}, bf16[160,768]{1,0:T(8,128)(2,1)S(1)}, u32[]{:S(2)}, u32[]{:S(2)}) collective-permute-start(bf16[160,768]{1,0:T(8,128)(2,1)S(1)} %get-tuple-element.75), channel_id=1, source_target_pairs={{0,2},{1,3},{2,0},{3,1},{4,6},{5,7},{6,4},{7,5},{8,10},{9,11},{10,... | collective-permute-start | bytes 737288 | tf_op jit(solution)/shard_map/ppermute | solution.py:18
  70.1 12.4 %collective-permute-start.19 = (bf16[160,768]{1,0:T(8,128)(2,1)S(1)}, bf16[160,768]{1,0:T(8,128)(2,1)S(1)}, u32[]{:S(2)}, u32[]{:S(2)}) collective-permute-start(bf16[160,768]{1,0:T(8,128)(2,1)S(1)} %get-tuple-element.80), channel_id=1, source_target_pairs={{0,4},{1,5},{2,6},{3,7},{4,0},{5,1},{6,2},{7,3},{8,12},{9,13},{10,... | collective-permute-start | bytes 737288 | tf_op jit(solution)/shard_map/ppermute | solution.py:18
  70.4 14.2 %collective-permute-start.20 = (bf16[160,768]{1,0:T(8,128)(2,1)S(1)}, bf16[160,768]{1,0:T(8,128)(2,1)S(1)}, u32[]{:S(2)}, u32[]{:S(2)}) collective-permute-start(bf16[160,768]{1,0:T(8,128)(2,1)S(1)} %get-tuple-element.81), channel_id=1, source_target_pairs={{0,6},{1,7},{2,4},{3,5},{4,2},{5,3},{6,0},{7,1},{8,14},{9,15},{10,... | collective-permute-start | bytes 737288 | tf_op jit(solution)/shard_map/ppermute | solution.py:18
  72.9 22.6 %collective-permute-start.22 = (bf16[320,768]{1,0:T(8,128)(2,1)S(1)}, bf16[320,768]{1,0:T(8,128)(2,1)S(1)}, u32[]{:S(2)}, u32[]{:S(2)}) collective-permute-start(bf16[320,768]{1,0:T(8,128)(2,1)S(1)} %get-tuple-element.94), channel_id=1, source_target_pairs={{0,2},{1,3},{2,0},{3,1},{4,6},{5,7},{6,4},{7,5},{8,10},{9,11},{10,... | collective-permute-start | bytes 1474568 | tf_op jit(solution)/shard_map/ppermute | solution.py:18
  73.6 28.1 %collective-permute-start.23 = (bf16[320,768]{1,0:T(8,128)(2,1)S(1)}, bf16[320,768]{1,0:T(8,128)(2,1)S(1)}, u32[]{:S(2)}, u32[]{:S(2)}) collective-permute-start(bf16[320,768]{1,0:T(8,128)(2,1)S(1)} %get-tuple-element.95), channel_id=1, source_target_pairs={{0,4},{1,5},{2,6},{3,7},{4,0},{5,1},{6,2},{7,3},{8,12},{9,13},{10,... | collective-permute-start | bytes 1474568 | tf_op jit(solution)/shard_map/ppermute | solution.py:18
  82.4 3.3 %copy-start.10 = (bf16[160,768]{1,0:T(8,128)(2,1)S(1)}, bf16[160,768]{1,0:T(8,128)(2,1)}, u32[]{:S(2)}) copy-start(bf16[160,768]{1,0:T(8,128)(2,1)} %copy-done.9) | copy-start | bytes 737284
  82.5 3.3 %copy-start.12 = (bf16[160,768]{1,0:T(8,128)(2,1)S(1)}, bf16[160,768]{1,0:T(8,128)(2,1)}, u32[]{:S(2)}) copy-start(bf16[160,768]{1,0:T(8,128)(2,1)} %copy-done.11) | copy-start | bytes 737284
  82.5 3.3 %copy-start.17 = (bf16[160,768]{1,0:T(8,128)(2,1)S(1)}, bf16[160,768]{1,0:T(8,128)(2,1)}, u32[]{:S(2)}) copy-start(bf16[160,768]{1,0:T(8,128)(2,1)} %copy-done.16) | copy-start | bytes 737284
  82.5 19.2 %collective-permute-start.24 = (bf16[320,768]{1,0:T(8,128)(2,1)S(1)}, bf16[320,768]{1,0:T(8,128)(2,1)S(1)}, u32[]{:S(2)}, u32[]{:S(2)}) collective-permute-start(bf16[320,768]{1,0:T(8,128)(2,1)S(1)} %get-tuple-element.96), channel_id=1, source_target_pairs={{0,6},{1,7},{2,4},{3,5},{4,2},{5,3},{6,0},{7,1},{8,14},{9,15},{10,... | collective-permute-start | bytes 1474568 | tf_op jit(solution)/shard_map/ppermute | solution.py:18
  85.2 18.9 %collective-permute-start.25 = (bf16[320,768]{1,0:T(8,128)(2,1)S(1)}, bf16[320,768]{1,0:T(8,128)(2,1)S(1)}, u32[]{:S(2)}, u32[]{:S(2)}) collective-permute-start(bf16[320,768]{1,0:T(8,128)(2,1)S(1)} %shard_map.104.refs_0_), channel_id=1, source_target_pairs={{0,16},{8,24},{16,0},{24,8},{1,17},{9,25},{17,1},{25,9},{2,18},{10... | collective-permute-start | bytes 1474568 | tf_op jit(solution)/shard_map/ppermute | solution.py:18
  85.8 2.8 %copy-start.19 = (bf16[160,512]{1,0:T(8,128)(2,1)S(1)}, bf16[160,512]{1,0:T(8,128)(2,1)}, u32[]{:S(2)}) copy-start(bf16[160,512]{1,0:T(8,128)(2,1)} %copy-done.18) | copy-start | bytes 491524
  88.6 3.6 %collective-permute-start.21 = (bf16[3072,256]{1,0:T(8,128)(2,1)}, bf16[3072,256]{1,0:T(8,128)(2,1)S(1)}, u32[]{:S(2)}, u32[]{:S(2)}) collective-permute-start(bf16[3072,256]{1,0:T(8,128)(2,1)} %shard_map.105.refs_0_), channel_id=1, source_target_pairs={{0,1},{1,0},{2,3},{3,2},{4,5},{5,4},{6,7},{7,6},{8,9},{9,8},{10,11... | collective-permute-start | bytes 4718600 | tf_op jit(solution)/shard_map/ppermute | solution.py:18
  91.7 10.0 %copy-start.4 = (f32[320]{0:T(512)S(1)}, f32[320]{0:T(512)}, u32[]{:S(2)}) copy-start(f32[320]{0:T(512)} %refs_7_.1) | copy-start | bytes 3844
  91.7 10.0 %copy-start.6 = (s32[1,320]{1,0:T(1,128)S(1)}, s32[1,320]{1,0:T(1,128)}, u32[]{:S(2)}) copy-start(s32[1,320]{1,0:T(1,128)} %copy-done.5) | copy-start | bytes 3844
  92.2 1.9 %copy-start.13 = (f32[3072,256]{1,0:T(8,128)S(1)}, f32[3072,256]{1,0:T(8,128)}, u32[]{:S(2)}) copy-start(f32[3072,256]{1,0:T(8,128)} %shard_map.106.refs_0_) | copy-start | bytes 9437188
  94.1 7.6 %copy-start.15 = (bf16[320,768]{1,0:T(8,128)(2,1)S(1)}, bf16[320,768]{1,0:T(8,128)(2,1)}, u32[]{:S(2)}) copy-start(bf16[320,768]{1,0:T(8,128)(2,1)} %copy-done.14) | copy-start | bytes 1474564

commit v5 on v4

--- a/solution.py
+++ b/solution.py
@@ -128,7 +128,7 @@
     def body(array_ref, out):
         out[...] = array_ref[...]
 
-    return call(body, shape(*array.shape), array, after=after)
+    return call(body, shape(*array.shape, array.dtype), array, after=after)
 
 
 def picked(slot_row, refs, base, rows):
@@ -338,9 +338,10 @@
         device, routing.reshape(1, local), gate_prob, tokens, cotangent, blocks, capacity
     )
     *sent, own_slots = dispatch(
-        slots, (tokens, scaled), blocks, rows, True, after=(ups[1], downs[1]), weight=LIGHT
+        slots, (tokens, scaled), blocks, rows, True, weight=LIGHT
     )
     own = spread(sent)
+    own_slots = handed_on(own_slots, (ups[1], downs[1]))
     pair_slots = across(own_slots)
     scaled = handed_on(scaled, (pair_tokens, pair_slots))
     pair_scaled = across(scaled)

time: 105 us -> 102 us (0.971)
  waiting for transfers between devices: 44 us -> 39.9 us
  local copies, waits for them, and re-layouts: 1.97 us -> 3.07 us
    ppermute x26, waiting for transfers between devices: 44 us -> 39.9 us  [exchange(): lax.ppermute(array, axis, [(i, i ^ flip) for i in range(lax.axis_size(axi...]
    unnamed x40 -> x44, local copies, waits for them, and re-layouts: 1.97 us -> 3.07 us
    pallas_call x15 -> x16, Pallas kernels: 22.2 us -> 22.1 us  [call(): pl.pallas_call(kernel, out_shape=out_shape, in_specs=[pl.BlockSpec(memory...]
  transfers between devices with their start and end apart: 26 -> 26, of which waited for: 10 -> 11; matrix products, arithmetic and copies ran while one was open for 0% -> 0% of each run, Pallas kernels for 23% -> 23%
where the time goes in v5:
time: 102 us
  waiting for transfers between devices  39.9 us (39%)
  starting transfers between devices  33.9 us (33%)
  Pallas kernels  23.6 us (23%)
  local copies, waits for them, and re-layouts  3.07 us (3%)
    ppermute x26, waiting for transfers between devices, exchange(): lax.ppermute(array, axis, [(i, i ^ flip) for i in range(lax.axis_size(axi...  39.9 us
    ppermute x26, starting transfers between devices, exchange(): lax.ppermute(array, axis, [(i, i ^ flip) for i in range(lax.axis_size(axi...  33.9 us
    pallas_call x16, Pallas kernels, call(): pl.pallas_call(kernel, out_shape=out_shape, in_specs=[pl.BlockSpec(memory...  22.1 us
    unnamed x44, local copies, waits for them, and re-layouts  3.07 us
  transfers between devices with their start and end apart: 26, of which 11 were waited for; matrix products, arithmetic and copies ran while one was open for 0% of the time, Pallas kernels for 23%

profile of v5, /device:TPU:0, one launch (start us, length us, event | category | flops | bytes accessed | tf_op | source)
XLA Modules:
  0.0 102.3 jit_solution(8799453001417315949)
XLA Ops:
  0.6 0.5 collective-permute-start.1
  1.1 0.1 collective-permute-start.2
  1.2 4.0 %collective-permute-start = (bf16[320,768]{1,0:T(8,128)(2,1)}, bf16[320,768]{1,0:T(8,128)(2,1)S(1)}, u32[]{:S(2)}, u32[]{:S(2)}) collective-permute-start(bf16[320,768]{1,0:T(8,128)(2,1)} %token_ref.1), channel_id=1, source_target_pairs={{0,16},{8,24},{16,0},{24,8},{1,17},{9,25},{17,1},{25,9},{2,18},{10... | collective-permute-start | bytes 1474568 | tf_op jit(solution)/shard_map/ppermute | solution.py:18
  5.2 1.5 %shard_map.93 = (s32[1,320]{1,0:T(1,128)S(1)}, bf16[320,768]{1,0:T(8,128)(2,1)S(1)}, bf16[320,768]{1,0:T(8,128)(2,1)S(1)}) custom-call(s32[1]{0:T(128)} %bitcast.2.device_ref, s32[1,320]{1,0:T(1,128)} %bitcast.18, f32[320]{0:T(512)} %refs_7_.1, bf16[320,768]{1,0:T(8,128)(2,1)} %token_ref.1, bf16[320,768]{1,0:T(8,128)(2,1)} %cotangent_ref.1), custom_call_target="tpu_custom_call" | custom-call | flops 1 | bytes 1 | tf_op jit(solution)/shard_map/pallas_call | solution.py:89
  6.7 1.2 %shard_map.94 = (bf16[320,768]{1,0:T(8,128)(2,1)S(1)}, bf16[320,768]{1,0:T(8,128)(2,1)S(1)}, bf16[320,768]{1,0:T(8,128)(2,1)S(1)}, bf16[320,768]{1,0:T(8,128)(2,1)S(1)}, s32[1,320]{1,0:T(1,128)S(1)}) custom-call(s32[1,320]{1,0:T(1,128)S(1)} %get-tuple-element.52.refs_0_.refs_1_, bf16[320,768]{1,0:T(8,128)(2,1)S(1)} %get-tuple-element.53.refs_1_, ...), custom_call_target="tpu_custom_call" | custom-call | flops 1 | bytes 1 | tf_op jit(solution)/shard_map/pallas_call | solution.py:31
  7.9 0.0 copy-start.5
  8.0 0.0 collective-permute-done.2.refs_1_.refs_8_.refs_6_
  8.0 0.0 copy-start.7
  8.0 0.8 copy-done.5
  8.8 0.3 copy-done.7
  9.1 0.2 collective-permute-start.3
  9.2 1.7 %collective-permute-start.4 = (bf16[320,768]{1,0:T(8,128)(2,1)S(1)}, bf16[320,768]{1,0:T(8,128)(2,1)S(1)}, u32[]{:S(2)}, u32[]{:S(2)}) collective-permute-start(bf16[320,768]{1,0:T(8,128)(2,1)S(1)} %get-tuple-element.58), channel_id=1, source_target_pairs={{0,2},{1,3},{2,0},{3,1},{4,6},{5,7},{6,4},{7,5},{8,10},{9,11},{10,... | collective-permute-start | bytes 1474568 | tf_op jit(solution)/shard_map/ppermute | solution.py:18
  10.9 1.5 %collective-permute-start.5 = (bf16[320,768]{1,0:T(8,128)(2,1)S(1)}, bf16[320,768]{1,0:T(8,128)(2,1)S(1)}, u32[]{:S(2)}, u32[]{:S(2)}) collective-permute-start(bf16[320,768]{1,0:T(8,128)(2,1)S(1)} %get-tuple-element.59), channel_id=1, source_target_pairs={{0,4},{1,5},{2,6},{3,7},{4,0},{5,1},{6,2},{7,3},{8,12},{9,13},{10,... | collective-permute-start | bytes 1474568 | tf_op jit(solution)/shard_map/ppermute | solution.py:18
  12.4 0.3 collective-permute-start.6
  12.7 14.8 %collective-permute-done.refs_0_.refs_2_ = bf16[320,768]{1,0:T(8,128)(2,1)S(1)} collective-permute-done((bf16[320,768]{1,0:T(8,128)(2,1)}, bf16[320,768]{1,0:T(8,128)(2,1)S(1)}, u32[]{:S(2)}, u32[]{:S(2)}) %collective-permute-start) | collective-permute-done | bytes 491552 | tf_op jit(solution)/shard_map/ppermute | solution.py:18
  27.5 0.0 collective-permute-done.3.refs_1_
  27.6 0.1 collective-permute-start.10
  27.7 0.7 shard_map.97
  28.3 0.0 copy-start.18
  28.3 1.6 %collective-permute-start.7 = (bf16[160,768]{1,0:T(8,128)(2,1)S(1)}, bf16[160,768]{1,0:T(8,128)(2,1)S(1)}, u32[]{:S(2)}, u32[]{:S(2)}) collective-permute-start(bf16[160,768]{1,0:T(8,128)(2,1)S(1)} %get-tuple-element.62), channel_id=1, source_target_pairs={{0,2},{1,3},{2,0},{3,1},{4,6},{5,7},{6,4},{7,5},{8,10},{9,11},{10,... | collective-permute-start | bytes 737288 | tf_op jit(solution)/shard_map/ppermute | solution.py:18
  30.0 1.5 %collective-permute-start.8 = (bf16[160,768]{1,0:T(8,128)(2,1)S(1)}, bf16[160,768]{1,0:T(8,128)(2,1)S(1)}, u32[]{:S(2)}, u32[]{:S(2)}) collective-permute-start(bf16[160,768]{1,0:T(8,128)(2,1)S(1)} %get-tuple-element.64), channel_id=1, source_target_pairs={{0,4},{1,5},{2,6},{3,7},{4,0},{5,1},{6,2},{7,3},{8,12},{9,13},{10,... | collective-permute-start | bytes 737288 | tf_op jit(solution)/shard_map/ppermute | solution.py:18
  31.5 2.6 %collective-permute-done.5.refs_3_ = bf16[320,768]{1,0:T(8,128)(2,1)S(1)} collective-permute-done((bf16[320,768]{1,0:T(8,128)(2,1)S(1)}, bf16[320,768]{1,0:T(8,128)(2,1)S(1)}, u32[]{:S(2)}, u32[]{:S(2)}) %collective-permute-start.5) | collective-permute-done | bytes 491552 | tf_op jit(solution)/shard_map/ppermute | solution.py:18
  34.1 0.6 collective-permute-start.9
  34.7 0.4 collective-permute-done.6.refs_4_
  35.1 4.7 %shard_map.98 = (bf16[320,768]{1,0:T(8,128)(2,1)S(1)}, bf16[320,768]{1,0:T(8,128)(2,1)S(1)}, bf16[320,768]{1,0:T(8,128)(2,1)S(1)}, bf16[320,768]{1,0:T(8,128)(2,...) custom-call(bf16[160,768]{1,0:T(8,128)(2,1)S(1)} %get-tuple-element., ...), custom_call_target="tpu_custom_call" | custom-call | flops 30000001024 | bytes 1 | tf_op jit(solution)/shard_map/pallas_call | solution.py:31
  39.8 0.0 copy-start.16
  39.9 1.2 %shard_map.99 = (bf16[160,768]{1,0:T(8,128)(2,1)S(1)}, bf16[160,768]{1,0:T(8,128)(2,1)S(1)}, bf16[160,512]{1,0:T(8,128)(2,1)S(1)}, bf16[160,512]{1,0:T(8,128)(2,...) custom-call(bf16[320,768]{1,0:T(8,128)(2,1)S(1)} %get-tuple-element.61.refs_0_.refs_2_, ...), custom_call_target="tpu_custom_call" | custom-call | flops 30000001024 | bytes 1 | tf_op jit(solution)/shard_map/pallas_call | solution.py:31
  41.0 3.0 %collective-permute-start.11 = (bf16[160,768]{1,0:T(8,128)(2,1)S(1)}, bf16[160,768]{1,0:T(8,128)(2,1)S(1)}, u32[]{:S(2)}, u32[]{:S(2)}) collective-permute-start(bf16[160,768]{1,0:T(8,128)(2,1)S(1)} %get-tuple-element.68), channel_id=1, source_target_pairs={{0,2},{1,3},{2,0},{3,1},{4,6},{5,7},{6,4},{7,5},{8,10},{9,11},{10,... | collective-permute-start | bytes 737288 | tf_op jit(solution)/shard_map/ppermute | solution.py:18
  44.1 1.6 %collective-permute-done.9.refs_2_.refs_8_ = bf16[160,768]{1,0:T(8,128)(2,1)S(1)} collective-permute-done((bf16[160,768]{1,0:T(8,128)(2,1)S(1)}, bf16[160,768]{1,0:T(8,128)(2,1)S(1)}, u32[]{:S(2)}, u32[]{:S(2)}) %collective-permute-start.9) | collective-permute-done | bytes 245792 | tf_op jit(solution)/shard_map/ppermute | solution.py:18
  45.7 1.2 %shard_map.100 = (bf16[160,768]{1,0:T(8,128)(2,1)S(1)}, bf16[160,768]{1,0:T(8,128)(2,1)S(1)}, bf16[160,512]{1,0:T(8,128)(2,1)S(1)}, bf16[160,512]{1,0:T(8,128)(2...) custom-call(bf16[160,768]{1,0:T(8,128)(2,1)S(1)} %get-tuple-element.63.refs_0_.refs_2_, ...), custom_call_target="tpu_custom_call" | custom-call | flops 30000001024 | bytes 1 | tf_op jit(solution)/shard_map/pallas_call | solution.py:31
  46.9 0.8 collective-permute-start.12
  47.7 2.1 %collective-permute-start.13 = (bf16[160,768]{1,0:T(8,128)(2,1)S(1)}, bf16[160,768]{1,0:T(8,128)(2,1)S(1)}, u32[]{:S(2)}, u32[]{:S(2)}) collective-permute-start(bf16[160,768]{1,0:T(8,128)(2,1)S(1)} %get-tuple-element.70), channel_id=1, source_target_pairs={{0,6},{1,7},{2,4},{3,5},{4,2},{5,3},{6,0},{7,1},{8,14},{9,15},{10,... | collective-permute-start | bytes 737288 | tf_op jit(solution)/shard_map/ppermute | solution.py:18
  49.8 1.9 %collective-permute-done.10.refs_2_ = bf16[320,768]{1,0:T(8,128)(2,1)S(1)} collective-permute-done((bf16[320,768]{1,0:T(8,128)(2,1)S(1)}, bf16[320,768]{1,0:T(8,128)(2,1)S(1)}, u32[]{:S(2)}, u32[]{:S(2)}) %collective-permute-start.10) | collective-permute-done | bytes 491552 | tf_op jit(solution)/shard_map/ppermute | solution.py:18
  51.7 0.7 shard_map.101
  52.4 1.3 %collective-permute-start.15 = (bf16[160,768]{1,0:T(8,128)(2,1)S(1)}, bf16[160,768]{1,0:T(8,128)(2,1)S(1)}, u32[]{:S(2)}, u32[]{:S(2)}) collective-permute-start(bf16[160,768]{1,0:T(8,128)(2,1)S(1)} %get-tuple-element.71), channel_id=1, source_target_pairs={{0,2},{1,3},{2,0},{3,1},{4,6},{5,7},{6,4},{7,5},{8,10},{9,11},{10,... | collective-permute-start | bytes 737288 | tf_op jit(solution)/shard_map/ppermute | solution.py:18
  53.7 1.5 %collective-permute-start.17 = (bf16[160,768]{1,0:T(8,128)(2,1)S(1)}, bf16[160,768]{1,0:T(8,128)(2,1)S(1)}, u32[]{:S(2)}, u32[]{:S(2)}) collective-permute-start(bf16[160,768]{1,0:T(8,128)(2,1)S(1)} %get-tuple-element.76), channel_id=1, source_target_pairs={{0,4},{1,5},{2,6},{3,7},{4,0},{5,1},{6,2},{7,3},{8,12},{9,13},{10,... | collective-permute-start | bytes 737288 | tf_op jit(solution)/shard_map/ppermute | solution.py:18
  55.2 0.0 collective-permute-done.11.refs_3_
  55.2 0.7 collective-permute-start.18
  56.0 5.7 %collective-permute-done.12.refs_4_ = bf16[160,768]{1,0:T(8,128)(2,1)S(1)} collective-permute-done((bf16[160,768]{1,0:T(8,128)(2,1)S(1)}, bf16[160,768]{1,0:T(8,128)(2,1)S(1)}, u32[]{:S(2)}, u32[]{:S(2)}) %collective-permute-start.12) | collective-permute-done | bytes 245792 | tf_op jit(solution)/shard_map/ppermute | solution.py:18
  61.6 0.6 shard_map.102.refs_0_
  62.3 3.1 %collective-permute-start.14 = (bf16[320,768]{1,0:T(8,128)(2,1)S(1)}, bf16[320,768]{1,0:T(8,128)(2,1)S(1)}, u32[]{:S(2)}, u32[]{:S(2)}) collective-permute-start(bf16[320,768]{1,0:T(8,128)(2,1)S(1)} %shard_map.102.refs_0_), channel_id=1, source_target_pairs={{0,16},{8,24},{16,0},{24,8},{1,17},{9,25},{17,1},{25,9},{2,18},{10... | collective-permute-start | bytes 1474568 | tf_op jit(solution)/shard_map/ppermute | solution.py:18
  65.4 0.0 collective-permute-done.15.refs_2_.refs_10_
  65.4 1.3 %shard_map.103 = (bf16[160,768]{1,0:T(8,128)(2,1)S(1)}, bf16[160,768]{1,0:T(8,128)(2,1)S(1)}, bf16[160,512]{1,0:T(8,128)(2,1)S(1)}, bf16[160,512]{1,0:T(8,128)(2,1)S(1)}) custom-call(bf16[320,768]{1,0:T(8,128)(2,1)S(1)} %shard_map.102.refs_0_, bf16[160,768]{1,0:T(8,128)(2,1)S(1)} %get-tuple-element.67.refs_0_.refs_1_.refs_9_, ...), custom_call_target="tpu_custom_call" | custom-call | flops 30000001024 | bytes 1 | tf_op jit(solution)/shard_map/pallas_call | solution.py:31
  66.6 1.1 %collective-permute-start.16 = (bf16[160,768]{1,0:T(8,128)(2,1)S(1)}, bf16[160,768]{1,0:T(8,128)(2,1)S(1)}, u32[]{:S(2)}, u32[]{:S(2)}) collective-permute-start(bf16[160,768]{1,0:T(8,128)(2,1)S(1)} %get-tuple-element.75), channel_id=1, source_target_pairs={{0,2},{1,3},{2,0},{3,1},{4,6},{5,7},{6,4},{7,5},{8,10},{9,11},{10,... | collective-permute-start | bytes 737288 | tf_op jit(solution)/shard_map/ppermute | solution.py:18
  67.7 0.3 collective-permute-done.17.refs_1_.refs_11_
  68.0 0.0 collective-permute-done.18.refs_2_.refs_12_
  68.0 1.3 %shard_map.104 = (bf16[160,768]{1,0:T(8,128)(2,1)S(1)}, bf16[160,768]{1,0:T(8,128)(2,1)S(1)}, bf16[160,512]{1,0:T(8,128)(2,1)S(1)}, bf16[160,512]{1,0:T(8,128)(2,1)S(1)}) custom-call(bf16[160,768]{1,0:T(8,128)(2,1)S(1)} %get-tuple-element.74.refs_0_.refs_2_, bf16[160,768]{1,0:T(8,128)(2,1)S(1)} %collective-permute-done.17.refs_1_.refs_11_, ...), custom_call_target="tpu_custom_call" | custom-call | flops 30000001024 | bytes 1 | tf_op jit(solution)/shard_map/pallas_call | solution.py:31
  69.3 1.2 %collective-permute-start.19 = (bf16[160,768]{1,0:T(8,128)(2,1)S(1)}, bf16[160,768]{1,0:T(8,128)(2,1)S(1)}, u32[]{:S(2)}, u32[]{:S(2)}) collective-permute-start(bf16[160,768]{1,0:T(8,128)(2,1)S(1)} %get-tuple-element.80), channel_id=1, source_target_pairs={{0,4},{1,5},{2,6},{3,7},{4,0},{5,1},{6,2},{7,3},{8,12},{9,13},{10,... | collective-permute-start | bytes 737288 | tf_op jit(solution)/shard_map/ppermute | solution.py:18
  70.5 1.8 %collective-permute-start.20 = (bf16[160,768]{1,0:T(8,128)(2,1)S(1)}, bf16[160,768]{1,0:T(8,128)(2,1)S(1)}, u32[]{:S(2)}, u32[]{:S(2)}) collective-permute-start(bf16[160,768]{1,0:T(8,128)(2,1)S(1)} %get-tuple-element.81), channel_id=1, source_target_pairs={{0,6},{1,7},{2,4},{3,5},{4,2},{5,3},{6,0},{7,1},{8,14},{9,15},{10,... | collective-permute-start | bytes 737288 | tf_op jit(solution)/shard_map/ppermute | solution.py:18
  72.3 0.6 collective-permute-start.22
  72.9 2.6 %collective-permute-done.16.refs_3_ = bf16[160,768]{1,0:T(8,128)(2,1)S(1)} collective-permute-done((bf16[160,768]{1,0:T(8,128)(2,1)S(1)}, bf16[160,768]{1,0:T(8,128)(2,1)S(1)}, u32[]{:S(2)}, u32[]{:S(2)}) %collective-permute-start.16) | collective-permute-done | bytes 245792 | tf_op jit(solution)/shard_map/ppermute | solution.py:18
  75.5 1.1 %collective-permute-start.23 = (bf16[320,768]{1,0:T(8,128)(2,1)S(1)}, bf16[320,768]{1,0:T(8,128)(2,1)S(1)}, u32[]{:S(2)}, u32[]{:S(2)}) collective-permute-start(bf16[320,768]{1,0:T(8,128)(2,1)S(1)} %get-tuple-element.95), channel_id=1, source_target_pairs={{0,4},{1,5},{2,6},{3,7},{4,0},{5,1},{6,2},{7,3},{8,12},{9,13},{10,... | collective-permute-start | bytes 1474568 | tf_op jit(solution)/shard_map/ppermute | solution.py:18
  76.6 5.5 %collective-permute-done.19.refs_4_ = bf16[160,768]{1,0:T(8,128)(2,1)S(1)} collective-permute-done((bf16[160,768]{1,0:T(8,128)(2,1)S(1)}, bf16[160,768]{1,0:T(8,128)(2,1)S(1)}, u32[]{:S(2)}, u32[]{:S(2)}) %collective-permute-start.19) | collective-permute-done | bytes 245792 | tf_op jit(solution)/shard_map/ppermute | solution.py:18
  82.2 1.2 %collective-permute-start.24 = (bf16[320,768]{1,0:T(8,128)(2,1)S(1)}, bf16[320,768]{1,0:T(8,128)(2,1)S(1)}, u32[]{:S(2)}, u32[]{:S(2)}) collective-permute-start(bf16[320,768]{1,0:T(8,128)(2,1)S(1)} %get-tuple-element.96), channel_id=1, source_target_pairs={{0,6},{1,7},{2,4},{3,5},{4,2},{5,3},{6,0},{7,1},{8,14},{9,15},{10,... | collective-permute-start | bytes 1474568 | tf_op jit(solution)/shard_map/ppermute | solution.py:18
  83.4 0.6 shard_map.105.refs_0_
  84.0 2.3 %collective-permute-start.25 = (bf16[320,768]{1,0:T(8,128)(2,1)S(1)}, bf16[320,768]{1,0:T(8,128)(2,1)S(1)}, u32[]{:S(2)}, u32[]{:S(2)}) collective-permute-start(bf16[320,768]{1,0:T(8,128)(2,1)S(1)} %shard_map.105.refs_0_), channel_id=1, source_target_pairs={{0,16},{8,24},{16,0},{24,8},{1,17},{9,25},{17,1},{25,9},{2,18},{10... | collective-permute-start | bytes 1474568 | tf_op jit(solution)/shard_map/ppermute | solution.py:18
  86.3 2.8 %shard_map.106.refs_0_ = bf16[3072,256]{1,0:T(8,128)(2,1)} custom-call(bf16[320,768]{1,0:T(8,128)(2,1)S(1)} %shard_map.105.refs_0_, bf16[320,768]{1,0:T(8,128)(2,1)S(1)} %get-tuple-element.57.refs_1_, bf16[320,768]{1,0:T(8,128)(2,1)S(1)} %collective-permute-done.4.refs_2_, bf16[320,768]{1,0:T(8,128)(2,1)S(1)} %collective-permute-done.5.refs_3_, ...), custom_call_target="tpu_custom_call" | custom-call | flops 30000001024 | bytes 1 | tf_op jit(solution)/shard_map/pallas_call | solution.py:31
  89.1 3.1 %shard_map.107.refs_0_ = f32[3072,256]{1,0:T(8,128)} custom-call(bf16[3072,256]{1,0:T(8,128)(2,1)} %shard_map.106.refs_0_, bf16[320,768]{1,0:T(8,128)(2,1)S(1)} %get-tuple-element.57.refs_1_, bf16[320,768]{1,0:T(8,128)(2,1)S(1)} %collective-permute-done.4.refs_2_, bf16[320,768]{1,0:T(8,128)(2,1)S(1)} %collective-permute-done.5.refs_3_, ...), custom_call_target="tpu_custom_call" | custom-call | flops 30000001024 | bytes 1 | tf_op jit(solution)/shard_map/pallas_call | solution.py:31
  92.2 0.5 collective-permute-done.21.refs_1_
  92.7 1.9 %copy-done.15 = f32[3072,256]{1,0:T(8,128)S(1)} copy-done((f32[3072,256]{1,0:T(8,128)S(1)}, f32[3072,256]{1,0:T(8,128)}, u32[]{:S(2)}) %copy-start.15) | copy-done | bytes 3145752
  94.6 1.3 %shard_map.108 = (bf16[768,512]{1,0:T(8,128)(2,1)}, bf16[512,768]{1,0:T(8,128)(2,1)}) custom-call(f32[3072,256]{1,0:T(8,128)S(1)} %copy-done.15, bf16[3072,256]{1,0:T(8,128)(2,1)S(1)} %collective-permute-done.21.refs_1_), custom_call_target="tpu_custom_call" | custom-call | flops 30000001024 | bytes 1 | tf_op jit(solution)/shard_map/pallas_call | solution.py:31
  96.0 3.8 %collective-permute-done.23.refs_4_ = bf16[320,768]{1,0:T(8,128)(2,1)S(1)} collective-permute-done((bf16[320,768]{1,0:T(8,128)(2,1)S(1)}, bf16[320,768]{1,0:T(8,128)(2,1)S(1)}, u32[]{:S(2)}, u32[]{:S(2)}) %collective-permute-start.23) | collective-permute-done | bytes 491552 | tf_op jit(solution)/shard_map/ppermute | solution.py:18
  99.8 1.6 %shard_map.109 = (bf16[320,768]{1,0:T(8,128)(2,1)}, bf16[320,768]{1,0:T(8,128)(2,1)S(1)}) custom-call(bf16[768,512]{1,0:T(8,128)(2,1)} %get-tuple-element.93.refs_0_, s32[1,320]{1,0:T(1,128)S(1)} %copy-done.2, bf16[320,768]{1,0:T(8,128)(2,1)S(1)} %copy-done.17, bf16[320,768]{1,0:T(8,128)(2,1)S(1)} %collective-permute-done.22.refs_3_, ...), custom_call_target="tpu_custom_call" | custom-call | flops 30000001024 | bytes 1 | tf_op jit(solution)/shard_map/pallas_call | solution.py:31
  101.4 0.9 add_convert_fusion
  (50 shorter events, 0.1 us)
Async XLA Ops:
  0.6 7.3 %collective-permute-start.1 = (bf16[768,512]{1,0:T(8,128)(2,1)}, bf16[768,512]{1,0:T(8,128)(2,1)S(1)}, u32[]{:S(2)}, u32[]{:S(2)}) collective-permute-start(bf16[768,512]{1,0:T(8,128)(2,1)} %bitcast.6), channel_id=1, source_target_pairs={{0,1},{1,0},{2,3},{3,2},{4,5},{5,4},{6,7},{7,6},{8,9},{9,8},{10,11... | collective-permute-start | bytes 2359304 | tf_op jit(solution)/shard_map/ppermute | solution.py:18
  1.1 6.8 %collective-permute-start.2 = (bf16[512,768]{1,0:T(8,128)(2,1)}, bf16[512,768]{1,0:T(8,128)(2,1)S(1)}, u32[]{:S(2)}, u32[]{:S(2)}) collective-permute-start(bf16[512,768]{1,0:T(8,128)(2,1)} %bitcast.12), channel_id=1, source_target_pairs={{0,1},{1,0},{2,3},{3,2},{4,5},{5,4},{6,7},{7,6},{8,9},{9,8},{10,11... | collective-permute-start | bytes 2359304 | tf_op jit(solution)/shard_map/ppermute | solution.py:18
  1.2 26.3 %collective-permute-start = (bf16[320,768]{1,0:T(8,128)(2,1)}, bf16[320,768]{1,0:T(8,128)(2,1)S(1)}, u32[]{:S(2)}, u32[]{:S(2)}) collective-permute-start(bf16[320,768]{1,0:T(8,128)(2,1)} %token_ref.1), channel_id=1, source_target_pairs={{0,16},{8,24},{16,0},{24,8},{1,17},{9,25},{17,1},{25,9},{2,18},{10... | collective-permute-start | bytes 1474568 | tf_op jit(solution)/shard_map/ppermute | solution.py:18
  6.7 1.2 %copy-start.1 = (s32[1,320]{1,0:T(1,128)}, s32[1,320]{1,0:T(1,128)S(1)}, u32[]{:S(2)}) copy-start(s32[1,320]{1,0:T(1,128)S(1)} %get-tuple-element.52.refs_0_.refs_1_) | copy-start | bytes 3844
  7.9 0.9 copy-start.5
  8.0 1.1 %copy-start.7 = (bf16[512,768]{1,0:T(8,128)(2,1)}, bf16[512,768]{1,0:T(8,128)(2,1)S(1)}, u32[]{:S(2)}) copy-start(bf16[512,768]{1,0:T(8,128)(2,1)S(1)} %collective-permute-done.2.refs_1_.refs_8_.refs_6_) | copy-start | bytes 2359300
  9.1 18.5 %collective-permute-start.3 = (s32[1,320]{1,0:T(1,128)S(1)}, s32[1,320]{1,0:T(1,128)S(1)}, u32[]{:S(2)}, u32[]{:S(2)}) collective-permute-start(s32[1,320]{1,0:T(1,128)S(1)} %shard_map.95), channel_id=1, source_target_pairs={{0,16},{8,24},{16,0},{24,8},{1,17},{9,25},{17,1},{25,9},{2,18},{10... | collective-permute-start | bytes 3848 | tf_op jit(solution)/shard_map/ppermute | solution.py:18
  9.2 20.7 %collective-permute-start.4 = (bf16[320,768]{1,0:T(8,128)(2,1)S(1)}, bf16[320,768]{1,0:T(8,128)(2,1)S(1)}, u32[]{:S(2)}, u32[]{:S(2)}) collective-permute-start(bf16[320,768]{1,0:T(8,128)(2,1)S(1)} %get-tuple-element.58), channel_id=1, source_target_pairs={{0,2},{1,3},{2,0},{3,1},{4,6},{5,7},{6,4},{7,5},{8,10},{9,11},{10,... | collective-permute-start | bytes 1474568 | tf_op jit(solution)/shard_map/ppermute | solution.py:18
  10.9 23.2 %collective-permute-start.5 = (bf16[320,768]{1,0:T(8,128)(2,1)S(1)}, bf16[320,768]{1,0:T(8,128)(2,1)S(1)}, u32[]{:S(2)}, u32[]{:S(2)}) collective-permute-start(bf16[320,768]{1,0:T(8,128)(2,1)S(1)} %get-tuple-element.59), channel_id=1, source_target_pairs={{0,4},{1,5},{2,6},{3,7},{4,0},{5,1},{6,2},{7,3},{8,12},{9,13},{10,... | collective-permute-start | bytes 1474568 | tf_op jit(solution)/shard_map/ppermute | solution.py:18
  12.4 22.7 %collective-permute-start.6 = (bf16[320,768]{1,0:T(8,128)(2,1)S(1)}, bf16[320,768]{1,0:T(8,128)(2,1)S(1)}, u32[]{:S(2)}, u32[]{:S(2)}) collective-permute-start(bf16[320,768]{1,0:T(8,128)(2,1)S(1)} %get-tuple-element.60), channel_id=1, source_target_pairs={{0,6},{1,7},{2,4},{3,5},{4,2},{5,3},{6,0},{7,1},{8,14},{9,15},{10,... | collective-permute-start | bytes 1474568 | tf_op jit(solution)/shard_map/ppermute | solution.py:18
  27.6 24.2 %collective-permute-start.10 = (bf16[320,768]{1,0:T(8,128)(2,1)S(1)}, bf16[320,768]{1,0:T(8,128)(2,1)S(1)}, u32[]{:S(2)}, u32[]{:S(2)}) collective-permute-start(bf16[320,768]{1,0:T(8,128)(2,1)S(1)} %shard_map.96.refs_0_), channel_id=1, source_target_pairs={{0,16},{8,24},{16,0},{24,8},{1,17},{9,25},{17,1},{25,9},{2,18},{10... | collective-permute-start | bytes 1474568 | tf_op jit(solution)/shard_map/ppermute | solution.py:18
  28.3 11.5 %copy-start.18 = (bf16[160,768]{1,0:T(8,128)(2,1)}, bf16[160,768]{1,0:T(8,128)(2,1)S(1)}, u32[]{:S(2)}) copy-start(bf16[160,768]{1,0:T(8,128)(2,1)S(1)} %get-tuple-element.56.refs_0_.refs_1_.refs_5_) | copy-start | bytes 737284
  28.3 11.5 %collective-permute-start.7 = (bf16[160,768]{1,0:T(8,128)(2,1)S(1)}, bf16[160,768]{1,0:T(8,128)(2,1)S(1)}, u32[]{:S(2)}, u32[]{:S(2)}) collective-permute-start(bf16[160,768]{1,0:T(8,128)(2,1)S(1)} %get-tuple-element.62), channel_id=1, source_target_pairs={{0,2},{1,3},{2,0},{3,1},{4,6},{5,7},{6,4},{7,5},{8,10},{9,11},{10,... | collective-permute-start | bytes 737288 | tf_op jit(solution)/shard_map/ppermute | solution.py:18
  30.0 14.1 %collective-permute-start.8 = (bf16[160,768]{1,0:T(8,128)(2,1)S(1)}, bf16[160,768]{1,0:T(8,128)(2,1)S(1)}, u32[]{:S(2)}, u32[]{:S(2)}) collective-permute-start(bf16[160,768]{1,0:T(8,128)(2,1)S(1)} %get-tuple-element.64), channel_id=1, source_target_pairs={{0,4},{1,5},{2,6},{3,7},{4,0},{5,1},{6,2},{7,3},{8,12},{9,13},{10,... | collective-permute-start | bytes 737288 | tf_op jit(solution)/shard_map/ppermute | solution.py:18
  34.1 11.6 %collective-permute-start.9 = (bf16[160,768]{1,0:T(8,128)(2,1)S(1)}, bf16[160,768]{1,0:T(8,128)(2,1)S(1)}, u32[]{:S(2)}, u32[]{:S(2)}) collective-permute-start(bf16[160,768]{1,0:T(8,128)(2,1)S(1)} %get-tuple-element.65), channel_id=1, source_target_pairs={{0,6},{1,7},{2,4},{3,5},{4,2},{5,3},{6,0},{7,1},{8,14},{9,15},{10,... | collective-permute-start | bytes 737288 | tf_op jit(solution)/shard_map/ppermute | solution.py:18
  35.1 4.7 %copy-start.3 = (bf16[1,768,512]{2,1,0:T(8,128)(2,1)S(1)}, bf16[1,768,512]{2,1,0:T(8,128)(2,1)}, u32[]{:S(2)}) copy-start(bf16[1,768,512]{2,1,0:T(8,128)(2,1)} %param.9) | copy-start | bytes 2359300
  35.1 4.8 %copy-start.4 = (bf16[1,512,768]{2,1,0:T(8,128)(2,1)S(1)}, bf16[1,512,768]{2,1,0:T(8,128)(2,1)}, u32[]{:S(2)}) copy-start(bf16[1,512,768]{2,1,0:T(8,128)(2,1)} %param.10) | copy-start | bytes 2359300
  35.1 4.8 %copy-start.6 = (bf16[768,512]{1,0:T(8,128)(2,1)S(1)}, bf16[768,512]{1,0:T(8,128)(2,1)}, u32[]{:S(2)}) copy-start(bf16[768,512]{1,0:T(8,128)(2,1)} %copy-done.5) | copy-start | bytes 2359300
  35.1 4.8 %copy-start.8 = (bf16[512,768]{1,0:T(8,128)(2,1)S(1)}, bf16[512,768]{1,0:T(8,128)(2,1)}, u32[]{:S(2)}) copy-start(bf16[512,768]{1,0:T(8,128)(2,1)} %copy-done.7) | copy-start | bytes 2359300
  39.8 1.2 %copy-start.16 = (bf16[320,768]{1,0:T(8,128)(2,1)}, bf16[320,768]{1,0:T(8,128)(2,1)S(1)}, u32[]{:S(2)}) copy-start(bf16[320,768]{1,0:T(8,128)(2,1)S(1)} %get-tuple-element.61.refs_0_.refs_2_) | copy-start | bytes 1474564
  39.8 1.2 %copy-start.9 = (bf16[160,768]{1,0:T(8,128)(2,1)}, bf16[160,768]{1,0:T(8,128)(2,1)S(1)}, u32[]{:S(2)}) copy-start(bf16[160,768]{1,0:T(8,128)(2,1)S(1)} %collective-permute-done.7.refs_2_.refs_6_) | copy-start | bytes 737284
  41.0 14.2 %collective-permute-start.11 = (bf16[160,768]{1,0:T(8,128)(2,1)S(1)}, bf16[160,768]{1,0:T(8,128)(2,1)S(1)}, u32[]{:S(2)}, u32[]{:S(2)}) collective-permute-start(bf16[160,768]{1,0:T(8,128)(2,1)S(1)} %get-tuple-element.68), channel_id=1, source_target_pairs={{0,2},{1,3},{2,0},{3,1},{4,6},{5,7},{6,4},{7,5},{8,10},{9,11},{10,... | collective-permute-start | bytes 737288 | tf_op jit(solution)/shard_map/ppermute | solution.py:18
  44.1 2.7 %copy-start.11 = (bf16[160,768]{1,0:T(8,128)(2,1)}, bf16[160,768]{1,0:T(8,128)(2,1)S(1)}, u32[]{:S(2)}) copy-start(bf16[160,768]{1,0:T(8,128)(2,1)S(1)} %collective-permute-done.8.refs_1_.refs_7_) | copy-start | bytes 737284
  45.7 1.2 %copy-start.13 = (bf16[160,768]{1,0:T(8,128)(2,1)}, bf16[160,768]{1,0:T(8,128)(2,1)S(1)}, u32[]{:S(2)}) copy-start(bf16[160,768]{1,0:T(8,128)(2,1)S(1)} %collective-permute-done.9.refs_2_.refs_8_) | copy-start | bytes 737284
  46.8 5.6 %copy-start.20 = (bf16[160,512]{1,0:T(8,128)(2,1)}, bf16[160,512]{1,0:T(8,128)(2,1)S(1)}, u32[]{:S(2)}) copy-start(bf16[160,512]{1,0:T(8,128)(2,1)S(1)} %get-tuple-element.66.refs_0_.refs_15_) | copy-start | bytes 491524
  46.9 14.8 %collective-permute-start.12 = (bf16[160,768]{1,0:T(8,128)(2,1)S(1)}, bf16[160,768]{1,0:T(8,128)(2,1)S(1)}, u32[]{:S(2)}, u32[]{:S(2)}) collective-permute-start(bf16[160,768]{1,0:T(8,128)(2,1)S(1)} %get-tuple-element.69), channel_id=1, source_target_pairs={{0,4},{1,5},{2,6},{3,7},{4,0},{5,1},{6,2},{7,3},{8,12},{9,13},{10,... | collective-permute-start | bytes 737288 | tf_op jit(solution)/shard_map/ppermute | solution.py:18
  47.7 14.0 %collective-permute-start.13 = (bf16[160,768]{1,0:T(8,128)(2,1)S(1)}, bf16[160,768]{1,0:T(8,128)(2,1)S(1)}, u32[]{:S(2)}, u32[]{:S(2)}) collective-permute-start(bf16[160,768]{1,0:T(8,128)(2,1)S(1)} %get-tuple-element.70), channel_id=1, source_target_pairs={{0,6},{1,7},{2,4},{3,5},{4,2},{5,3},{6,0},{7,1},{8,14},{9,15},{10,... | collective-permute-start | bytes 737288 | tf_op jit(solution)/shard_map/ppermute | solution.py:18
  52.4 12.9 %collective-permute-start.15 = (bf16[160,768]{1,0:T(8,128)(2,1)S(1)}, bf16[160,768]{1,0:T(8,128)(2,1)S(1)}, u32[]{:S(2)}, u32[]{:S(2)}) collective-permute-start(bf16[160,768]{1,0:T(8,128)(2,1)S(1)} %get-tuple-element.71), channel_id=1, source_target_pairs={{0,2},{1,3},{2,0},{3,1},{4,6},{5,7},{6,4},{7,5},{8,10},{9,11},{10,... | collective-permute-start | bytes 737288 | tf_op jit(solution)/shard_map/ppermute | solution.py:18
  53.7 14.3 %collective-permute-start.17 = (bf16[160,768]{1,0:T(8,128)(2,1)S(1)}, bf16[160,768]{1,0:T(8,128)(2,1)S(1)}, u32[]{:S(2)}, u32[]{:S(2)}) collective-permute-start(bf16[160,768]{1,0:T(8,128)(2,1)S(1)} %get-tuple-element.76), channel_id=1, source_target_pairs={{0,4},{1,5},{2,6},{3,7},{4,0},{5,1},{6,2},{7,3},{8,12},{9,13},{10,... | collective-permute-start | bytes 737288 | tf_op jit(solution)/shard_map/ppermute | solution.py:18
  55.2 12.8 %collective-permute-start.18 = (bf16[160,768]{1,0:T(8,128)(2,1)S(1)}, bf16[160,768]{1,0:T(8,128)(2,1)S(1)}, u32[]{:S(2)}, u32[]{:S(2)}) collective-permute-start(bf16[160,768]{1,0:T(8,128)(2,1)S(1)} %get-tuple-element.77), channel_id=1, source_target_pairs={{0,6},{1,7},{2,4},{3,5},{4,2},{5,3},{6,0},{7,1},{8,14},{9,15},{10,... | collective-permute-start | bytes 737288 | tf_op jit(solution)/shard_map/ppermute | solution.py:18
  62.3 21.1 %collective-permute-start.14 = (bf16[320,768]{1,0:T(8,128)(2,1)S(1)}, bf16[320,768]{1,0:T(8,128)(2,1)S(1)}, u32[]{:S(2)}, u32[]{:S(2)}) collective-permute-start(bf16[320,768]{1,0:T(8,128)(2,1)S(1)} %shard_map.102.refs_0_), channel_id=1, source_target_pairs={{0,16},{8,24},{16,0},{24,8},{1,17},{9,25},{17,1},{25,9},{2,18},{10... | collective-permute-start | bytes 1474568 | tf_op jit(solution)/shard_map/ppermute | solution.py:18
  66.6 8.9 %collective-permute-start.16 = (bf16[160,768]{1,0:T(8,128)(2,1)S(1)}, bf16[160,768]{1,0:T(8,128)(2,1)S(1)}, u32[]{:S(2)}, u32[]{:S(2)}) collective-permute-start(bf16[160,768]{1,0:T(8,128)(2,1)S(1)} %get-tuple-element.75), channel_id=1, source_target_pairs={{0,2},{1,3},{2,0},{3,1},{4,6},{5,7},{6,4},{7,5},{8,10},{9,11},{10,... | collective-permute-start | bytes 737288 | tf_op jit(solution)/shard_map/ppermute | solution.py:18
  69.3 12.9 %collective-permute-start.19 = (bf16[160,768]{1,0:T(8,128)(2,1)S(1)}, bf16[160,768]{1,0:T(8,128)(2,1)S(1)}, u32[]{:S(2)}, u32[]{:S(2)}) collective-permute-start(bf16[160,768]{1,0:T(8,128)(2,1)S(1)} %get-tuple-element.80), channel_id=1, source_target_pairs={{0,4},{1,5},{2,6},{3,7},{4,0},{5,1},{6,2},{7,3},{8,12},{9,13},{10,... | collective-permute-start | bytes 737288 | tf_op jit(solution)/shard_map/ppermute | solution.py:18
  70.5 12.8 %collective-permute-start.20 = (bf16[160,768]{1,0:T(8,128)(2,1)S(1)}, bf16[160,768]{1,0:T(8,128)(2,1)S(1)}, u32[]{:S(2)}, u32[]{:S(2)}) collective-permute-start(bf16[160,768]{1,0:T(8,128)(2,1)S(1)} %get-tuple-element.81), channel_id=1, source_target_pairs={{0,6},{1,7},{2,4},{3,5},{4,2},{5,3},{6,0},{7,1},{8,14},{9,15},{10,... | collective-permute-start | bytes 737288 | tf_op jit(solution)/shard_map/ppermute | solution.py:18
  72.3 23.6 %collective-permute-start.22 = (bf16[320,768]{1,0:T(8,128)(2,1)S(1)}, bf16[320,768]{1,0:T(8,128)(2,1)S(1)}, u32[]{:S(2)}, u32[]{:S(2)}) collective-permute-start(bf16[320,768]{1,0:T(8,128)(2,1)S(1)} %get-tuple-element.94), channel_id=1, source_target_pairs={{0,2},{1,3},{2,0},{3,1},{4,6},{5,7},{6,4},{7,5},{8,10},{9,11},{10,... | collective-permute-start | bytes 1474568 | tf_op jit(solution)/shard_map/ppermute | solution.py:18
  75.5 24.2 %collective-permute-start.23 = (bf16[320,768]{1,0:T(8,128)(2,1)S(1)}, bf16[320,768]{1,0:T(8,128)(2,1)S(1)}, u32[]{:S(2)}, u32[]{:S(2)}) collective-permute-start(bf16[320,768]{1,0:T(8,128)(2,1)S(1)} %get-tuple-element.95), channel_id=1, source_target_pairs={{0,4},{1,5},{2,6},{3,7},{4,0},{5,1},{6,2},{7,3},{8,12},{9,13},{10,... | collective-permute-start | bytes 1474568 | tf_op jit(solution)/shard_map/ppermute | solution.py:18
  82.2 4.1 %copy-start.10 = (bf16[160,768]{1,0:T(8,128)(2,1)S(1)}, bf16[160,768]{1,0:T(8,128)(2,1)}, u32[]{:S(2)}) copy-start(bf16[160,768]{1,0:T(8,128)(2,1)} %copy-done.9) | copy-start | bytes 737284
  82.2 4.1 %copy-start.12 = (bf16[160,768]{1,0:T(8,128)(2,1)S(1)}, bf16[160,768]{1,0:T(8,128)(2,1)}, u32[]{:S(2)}) copy-start(bf16[160,768]{1,0:T(8,128)(2,1)} %copy-done.11) | copy-start | bytes 737284
  82.2 4.1 %copy-start.14 = (bf16[160,768]{1,0:T(8,128)(2,1)S(1)}, bf16[160,768]{1,0:T(8,128)(2,1)}, u32[]{:S(2)}) copy-start(bf16[160,768]{1,0:T(8,128)(2,1)} %copy-done.13) | copy-start | bytes 737284
  82.2 4.1 %copy-start.19 = (bf16[160,768]{1,0:T(8,128)(2,1)S(1)}, bf16[160,768]{1,0:T(8,128)(2,1)}, u32[]{:S(2)}) copy-start(bf16[160,768]{1,0:T(8,128)(2,1)} %copy-done.18) | copy-start | bytes 737284
  82.2 17.6 %collective-permute-start.24 = (bf16[320,768]{1,0:T(8,128)(2,1)S(1)}, bf16[320,768]{1,0:T(8,128)(2,1)S(1)}, u32[]{:S(2)}, u32[]{:S(2)}) collective-permute-start(bf16[320,768]{1,0:T(8,128)(2,1)S(1)} %get-tuple-element.96), channel_id=1, source_target_pairs={{0,6},{1,7},{2,4},{3,5},{4,2},{5,3},{6,0},{7,1},{8,14},{9,15},{10,... | collective-permute-start | bytes 1474568 | tf_op jit(solution)/shard_map/ppermute | solution.py:18
  84.0 17.4 %collective-permute-start.25 = (bf16[320,768]{1,0:T(8,128)(2,1)S(1)}, bf16[320,768]{1,0:T(8,128)(2,1)S(1)}, u32[]{:S(2)}, u32[]{:S(2)}) collective-permute-start(bf16[320,768]{1,0:T(8,128)(2,1)S(1)} %shard_map.105.refs_0_), channel_id=1, source_target_pairs={{0,16},{8,24},{16,0},{24,8},{1,17},{9,25},{17,1},{25,9},{2,18},{10... | collective-permute-start | bytes 1474568 | tf_op jit(solution)/shard_map/ppermute | solution.py:18
  86.3 2.8 %copy-start.21 = (bf16[160,512]{1,0:T(8,128)(2,1)S(1)}, bf16[160,512]{1,0:T(8,128)(2,1)}, u32[]{:S(2)}) copy-start(bf16[160,512]{1,0:T(8,128)(2,1)} %copy-done.20) | copy-start | bytes 491524
  89.1 3.6 %collective-permute-start.21 = (bf16[3072,256]{1,0:T(8,128)(2,1)}, bf16[3072,256]{1,0:T(8,128)(2,1)S(1)}, u32[]{:S(2)}, u32[]{:S(2)}) collective-permute-start(bf16[3072,256]{1,0:T(8,128)(2,1)} %shard_map.106.refs_0_), channel_id=1, source_target_pairs={{0,1},{1,0},{2,3},{3,2},{4,5},{5,4},{6,7},{7,6},{8,9},{9,8},{10,11... | collective-permute-start | bytes 4718600 | tf_op jit(solution)/shard_map/ppermute | solution.py:18
  92.2 7.6 %copy-start = (f32[320]{0:T(512)S(1)}, f32[320]{0:T(512)}, u32[]{:S(2)}) copy-start(f32[320]{0:T(512)} %refs_7_.1) | copy-start | bytes 3844
  92.2 7.6 %copy-start.2 = (s32[1,320]{1,0:T(1,128)S(1)}, s32[1,320]{1,0:T(1,128)}, u32[]{:S(2)}) copy-start(s32[1,320]{1,0:T(1,128)} %copy-done.1) | copy-start | bytes 3844
  92.7 1.9 %copy-start.15 = (f32[3072,256]{1,0:T(8,128)S(1)}, f32[3072,256]{1,0:T(8,128)}, u32[]{:S(2)}) copy-start(f32[3072,256]{1,0:T(8,128)} %shard_map.107.refs_0_) | copy-start | bytes 9437188
  94.6 5.1 %copy-start.17 = (bf16[320,768]{1,0:T(8,128)(2,1)S(1)}, bf16[320,768]{1,0:T(8,128)(2,1)}, u32[]{:S(2)}) copy-start(bf16[320,768]{1,0:T(8,128)(2,1)} %copy-done.16) | copy-start | bytes 1474564

commit v6 on v5

--- a/solution.py
+++ b/solution.py
@@ -157,19 +157,43 @@
     def body(slot_ref, *refs):
         parts, (other_ref, gate_ref, mixed_ref, back_ref) = refs[:blocks], refs[blocks:]
         out = picked(slot_ref[...], parts, 0, rows) + other_ref[...].astype(F32)
-        mixed_ref[...] = (column(gate_ref[...].reshape(1, local)) * out.astype(BF16).astype(F32)).astype(BF16)
+        factor = column(gate_ref[...].reshape(1, local))
+        mixed_ref[...] = (factor * out.astype(BF16).astype(F32)).astype(BF16)
         back_ref[...] = picked(slot_ref[...], parts, rows, rows).astype(BF16)
 
-    return call(
+    kept = [pltpu.VMEM((local, width), BF16)] * 2
+    return call(body, kept, slots, *parts, other_out, gate, after=after, space=pltpu.HBM)
+
+
+def finished(mixed, one, other):
+    local, width = mixed.shape
+    pieces = 4
+    piece = local // pieces
+    parts = [pl.ds(number * piece, piece) for number in range(pieces)]
+
+    def body(mixed_ref, one_ref, other_ref, mixed_out, sum_out, here, sems):
+        copies = [
+            pltpu.make_async_copy(source.at[part], target.at[part], sems.at[index, number])
+            for index, (source, target) in enumerate(((mixed_ref, mixed_out), (here, sum_out)))
+            for number, part in enumerate(parts)
+        ]
+        for copy in copies[:pieces]:
+            copy.start()
+        for part, copy in zip(parts, copies[pieces:]):
+            total = one_ref[part, :].astype(F32) + other_ref[part, :].astype(F32)
+            here[part, :] = total.astype(BF16)
+            copy.start()
+        for copy in copies:
+            copy.wait()
+
+    return pl.pallas_call(
         body,
-        [shape(local, width)] * 2,
-        slots,
-        *parts,
-        other_out,
-        gate,
-        after=after,
-        space=pltpu.HBM,
-    )
+        out_shape=[shape(local, width)] * 2,
+        out_specs=[pl.BlockSpec(memory_space=pl.ANY)] * 2,
+        scratch_shapes=[pltpu.VMEM((local, width), BF16), pltpu.SemaphoreType.DMA((2, pieces))],
+        cost_estimate=HEAVY,
+        compiler_params=pltpu.CompilerParams(vmem_limit_bytes=VMEM_LIMIT),
+    )(mixed, one, other)
 
 
 def rows_of(refs, which, capacity, base=0):
@@ -345,7 +369,7 @@
     pair_slots = across(own_slots)
     scaled = handed_on(scaled, (pair_tokens, pair_slots))
     pair_scaled = across(scaled)
-    sent = dispatch(pair_slots, (pair_tokens,), blocks, rows, after=(scaled,))
+    sent = dispatch(pair_slots, (pair_tokens,), blocks, rows, after=(scaled,), weight=LIGHT)
     pair_x = spread(sent)
     own_sent, own_hidden, own_hidden_grad = both_ways(own, ups, downs, capacity, after=(sent[0],))
     half = blocks // 2
@@ -391,7 +415,7 @@
     peer = exchange(give, "expert", 1)
     grad_up, grad_down = joined(keep, peer, *ups[0].shape)
     mixed, own_term = collect_own(slots, own_back, other_out, gate_prob, after=(pltpu.with_memory_space_constraint(grad_up, pltpu.HBM),))
-    token_grad = (own_term.astype(F32) + other_back.astype(F32)).astype(BF16)
+    mixed, token_grad = finished(mixed, own_term, other_back)
     return (mixed, token_grad, grad_up[None], grad_down[None])
 
 

time: 102 us -> 102 us (level)
    unnamed x44 -> x48, local copies, waits for them, and re-layouts: 3.07 us -> 3.08 us
  transfers between devices with their start and end apart: 26 -> 26, of which waited for: 11 -> 12; matrix products, arithmetic and copies ran while one was open for 0% -> 0% of each run, Pallas kernels for 23% -> 23%
where the time goes in v6:
time: 102 us
  waiting for transfers between devices  39.9 us (39%)
  starting transfers between devices  33.9 us (33%)
  Pallas kernels  24.1 us (24%)
  local copies, waits for them, and re-layouts  3.08 us (3%)
  between operations  1.15 us (1%)
    ppermute x26, waiting for transfers between devices, exchange(): lax.ppermute(array, axis, [(i, i ^ flip) for i in range(lax.axis_size(axi...  39.9 us
    ppermute x26, starting transfers between devices, exchange(): lax.ppermute(array, axis, [(i, i ^ flip) for i in range(lax.axis_size(axi...  33.9 us
    pallas_call x16, Pallas kernels, call(): pl.pallas_call(kernel, out_shape=out_shape, in_specs=[pl.BlockSpec(memory...  21.7 us
    unnamed x48, local copies, waits for them, and re-layouts  3.08 us
  transfers between devices with their start and end apart: 26, of which 12 were waited for; matrix products, arithmetic and copies ran while one was open for 0% of the time, Pallas kernels for 23%

profile of v6, /device:TPU:0, one launch (start us, length us, event | category | flops | bytes accessed | tf_op | source)
XLA Modules:
  0.0 102.2 jit_solution(12239975494337754531)
XLA Ops:
  0.6 0.5 collective-permute-start.1
  1.1 0.1 collective-permute-start.2
  1.2 4.0 %collective-permute-start = (bf16[320,768]{1,0:T(8,128)(2,1)}, bf16[320,768]{1,0:T(8,128)(2,1)S(1)}, u32[]{:S(2)}, u32[]{:S(2)}) collective-permute-start(bf16[320,768]{1,0:T(8,128)(2,1)} %token_ref.1), channel_id=1, source_target_pairs={{0,16},{8,24},{16,0},{24,8},{1,17},{9,25},{17,1},{25,9},{2,18},{10... | collective-permute-start | bytes 1474568 | tf_op jit(solution)/shard_map/ppermute | solution.py:18
  5.2 1.5 %shard_map.93 = (s32[1,320]{1,0:T(1,128)S(1)}, bf16[320,768]{1,0:T(8,128)(2,1)S(1)}, bf16[320,768]{1,0:T(8,128)(2,1)S(1)}) custom-call(s32[1]{0:T(128)} %bitcast.2.device_ref, s32[1,320]{1,0:T(1,128)} %bitcast.18, f32[320]{0:T(512)} %refs_7_.1, bf16[320,768]{1,0:T(8,128)(2,1)} %token_ref.1, bf16[320,768]{1,0:T(8,128)(2,1)} %cotangent_ref.1), custom_call_target="tpu_custom_call" | custom-call | flops 1 | bytes 1 | tf_op jit(solution)/shard_map/pallas_call | solution.py:89
  6.7 1.2 %shard_map.94 = (bf16[320,768]{1,0:T(8,128)(2,1)S(1)}, bf16[320,768]{1,0:T(8,128)(2,1)S(1)}, bf16[320,768]{1,0:T(8,128)(2,1)S(1)}, bf16[320,768]{1,0:T(8,128)(2,1)S(1)}, s32[1,320]{1,0:T(1,128)S(1)}) custom-call(s32[1,320]{1,0:T(1,128)S(1)} %get-tuple-element.54.refs_0_.refs_1_, bf16[320,768]{1,0:T(8,128)(2,1)S(1)} %get-tuple-element.55.refs_1_, ...), custom_call_target="tpu_custom_call" | custom-call | flops 1 | bytes 1 | tf_op jit(solution)/shard_map/pallas_call | solution.py:31
  7.9 0.0 copy-start.5
  8.0 0.0 collective-permute-done.2.refs_1_.refs_8_.refs_6_
  8.0 0.0 copy-start.7
  8.0 0.8 copy-done.5
  8.8 0.3 copy-done.7
  9.1 0.2 collective-permute-start.3
  9.2 1.7 %collective-permute-start.4 = (bf16[320,768]{1,0:T(8,128)(2,1)S(1)}, bf16[320,768]{1,0:T(8,128)(2,1)S(1)}, u32[]{:S(2)}, u32[]{:S(2)}) collective-permute-start(bf16[320,768]{1,0:T(8,128)(2,1)S(1)} %get-tuple-element.60), channel_id=1, source_target_pairs={{0,2},{1,3},{2,0},{3,1},{4,6},{5,7},{6,4},{7,5},{8,10},{9,11},{10,... | collective-permute-start | bytes 1474568 | tf_op jit(solution)/shard_map/ppermute | solution.py:18
  10.9 1.5 %collective-permute-start.5 = (bf16[320,768]{1,0:T(8,128)(2,1)S(1)}, bf16[320,768]{1,0:T(8,128)(2,1)S(1)}, u32[]{:S(2)}, u32[]{:S(2)}) collective-permute-start(bf16[320,768]{1,0:T(8,128)(2,1)S(1)} %get-tuple-element.61), channel_id=1, source_target_pairs={{0,4},{1,5},{2,6},{3,7},{4,0},{5,1},{6,2},{7,3},{8,12},{9,13},{10,... | collective-permute-start | bytes 1474568 | tf_op jit(solution)/shard_map/ppermute | solution.py:18
  12.4 0.3 collective-permute-start.6
  12.7 14.8 %collective-permute-done.refs_0_.refs_2_ = bf16[320,768]{1,0:T(8,128)(2,1)S(1)} collective-permute-done((bf16[320,768]{1,0:T(8,128)(2,1)}, bf16[320,768]{1,0:T(8,128)(2,1)S(1)}, u32[]{:S(2)}, u32[]{:S(2)}) %collective-permute-start) | collective-permute-done | bytes 491552 | tf_op jit(solution)/shard_map/ppermute | solution.py:18
  27.5 0.0 collective-permute-done.3.refs_1_
  27.6 0.1 collective-permute-start.10
  27.7 0.7 shard_map.97
  28.3 1.6 %collective-permute-start.7 = (bf16[160,768]{1,0:T(8,128)(2,1)S(1)}, bf16[160,768]{1,0:T(8,128)(2,1)S(1)}, u32[]{:S(2)}, u32[]{:S(2)}) collective-permute-start(bf16[160,768]{1,0:T(8,128)(2,1)S(1)} %get-tuple-element.64), channel_id=1, source_target_pairs={{0,2},{1,3},{2,0},{3,1},{4,6},{5,7},{6,4},{7,5},{8,10},{9,11},{10,... | collective-permute-start | bytes 737288 | tf_op jit(solution)/shard_map/ppermute | solution.py:18
  30.0 0.0 collective-permute-done.4.refs_2_
  30.0 1.5 %collective-permute-start.8 = (bf16[160,768]{1,0:T(8,128)(2,1)S(1)}, bf16[160,768]{1,0:T(8,128)(2,1)S(1)}, u32[]{:S(2)}, u32[]{:S(2)}) collective-permute-start(bf16[160,768]{1,0:T(8,128)(2,1)S(1)} %get-tuple-element.66), channel_id=1, source_target_pairs={{0,4},{1,5},{2,6},{3,7},{4,0},{5,1},{6,2},{7,3},{8,12},{9,13},{10,... | collective-permute-start | bytes 737288 | tf_op jit(solution)/shard_map/ppermute | solution.py:18
  31.5 2.6 %collective-permute-done.5.refs_3_ = bf16[320,768]{1,0:T(8,128)(2,1)S(1)} collective-permute-done((bf16[320,768]{1,0:T(8,128)(2,1)S(1)}, bf16[320,768]{1,0:T(8,128)(2,1)S(1)}, u32[]{:S(2)}, u32[]{:S(2)}) %collective-permute-start.5) | collective-permute-done | bytes 491552 | tf_op jit(solution)/shard_map/ppermute | solution.py:18
  34.1 0.6 collective-permute-start.9
  34.7 0.4 collective-permute-done.6.refs_4_
  35.1 4.7 %shard_map.98 = (bf16[320,768]{1,0:T(8,128)(2,1)S(1)}, bf16[320,768]{1,0:T(8,128)(2,1)S(1)}, bf16[320,768]{1,0:T(8,128)(2,1)S(1)}, bf16[320,768]{1,0:T(8,128)(2,...) custom-call(bf16[160,768]{1,0:T(8,128)(2,1)S(1)} %get-tuple-element., ...), custom_call_target="tpu_custom_call" | custom-call | flops 30000001024 | bytes 1 | tf_op jit(solution)/shard_map/pallas_call | solution.py:31
  39.8 0.0 copy-start.20
  39.8 0.0 collective-permute-done.7.refs_2_.refs_6_
  39.9 1.2 %shard_map.99 = (bf16[160,768]{1,0:T(8,128)(2,1)S(1)}, bf16[160,768]{1,0:T(8,128)(2,1)S(1)}, bf16[160,512]{1,0:T(8,128)(2,1)S(1)}, bf16[160,512]{1,0:T(8,128)(2,...) custom-call(bf16[320,768]{1,0:T(8,128)(2,1)S(1)} %get-tuple-element.63.refs_0_.refs_2_, ...), custom_call_target="tpu_custom_call" | custom-call | flops 30000001024 | bytes 1 | tf_op jit(solution)/shard_map/pallas_call | solution.py:31
  41.1 3.0 %collective-permute-start.11 = (bf16[160,768]{1,0:T(8,128)(2,1)S(1)}, bf16[160,768]{1,0:T(8,128)(2,1)S(1)}, u32[]{:S(2)}, u32[]{:S(2)}) collective-permute-start(bf16[160,768]{1,0:T(8,128)(2,1)S(1)} %get-tuple-element.70), channel_id=1, source_target_pairs={{0,2},{1,3},{2,0},{3,1},{4,6},{5,7},{6,4},{7,5},{8,10},{9,11},{10,... | collective-permute-start | bytes 737288 | tf_op jit(solution)/shard_map/ppermute | solution.py:18
  44.1 1.5 %collective-permute-done.9.refs_2_.refs_8_ = bf16[160,768]{1,0:T(8,128)(2,1)S(1)} collective-permute-done((bf16[160,768]{1,0:T(8,128)(2,1)S(1)}, bf16[160,768]{1,0:T(8,128)(2,1)S(1)}, u32[]{:S(2)}, u32[]{:S(2)}) %collective-permute-start.9) | collective-permute-done | bytes 245792 | tf_op jit(solution)/shard_map/ppermute | solution.py:18
  45.7 1.2 %shard_map.100 = (bf16[160,768]{1,0:T(8,128)(2,1)S(1)}, bf16[160,768]{1,0:T(8,128)(2,1)S(1)}, bf16[160,512]{1,0:T(8,128)(2,1)S(1)}, bf16[160,512]{1,0:T(8,128)(2...) custom-call(bf16[160,768]{1,0:T(8,128)(2,1)S(1)} %get-tuple-element.65.refs_0_.refs_2_, ...), custom_call_target="tpu_custom_call" | custom-call | flops 30000001024 | bytes 1 | tf_op jit(solution)/shard_map/pallas_call | solution.py:31
  46.9 0.8 collective-permute-start.12
  47.7 2.1 %collective-permute-start.13 = (bf16[160,768]{1,0:T(8,128)(2,1)S(1)}, bf16[160,768]{1,0:T(8,128)(2,1)S(1)}, u32[]{:S(2)}, u32[]{:S(2)}) collective-permute-start(bf16[160,768]{1,0:T(8,128)(2,1)S(1)} %get-tuple-element.72), channel_id=1, source_target_pairs={{0,6},{1,7},{2,4},{3,5},{4,2},{5,3},{6,0},{7,1},{8,14},{9,15},{10,... | collective-permute-start | bytes 737288 | tf_op jit(solution)/shard_map/ppermute | solution.py:18
  49.8 1.9 %collective-permute-done.10.refs_2_ = bf16[320,768]{1,0:T(8,128)(2,1)S(1)} collective-permute-done((bf16[320,768]{1,0:T(8,128)(2,1)S(1)}, bf16[320,768]{1,0:T(8,128)(2,1)S(1)}, u32[]{:S(2)}, u32[]{:S(2)}) %collective-permute-start.10) | collective-permute-done | bytes 491552 | tf_op jit(solution)/shard_map/ppermute | solution.py:18
  51.7 0.7 shard_map.101
  52.4 1.3 %collective-permute-start.15 = (bf16[160,768]{1,0:T(8,128)(2,1)S(1)}, bf16[160,768]{1,0:T(8,128)(2,1)S(1)}, u32[]{:S(2)}, u32[]{:S(2)}) collective-permute-start(bf16[160,768]{1,0:T(8,128)(2,1)S(1)} %get-tuple-element.73), channel_id=1, source_target_pairs={{0,2},{1,3},{2,0},{3,1},{4,6},{5,7},{6,4},{7,5},{8,10},{9,11},{10,... | collective-permute-start | bytes 737288 | tf_op jit(solution)/shard_map/ppermute | solution.py:18
  53.7 1.5 %collective-permute-start.17 = (bf16[160,768]{1,0:T(8,128)(2,1)S(1)}, bf16[160,768]{1,0:T(8,128)(2,1)S(1)}, u32[]{:S(2)}, u32[]{:S(2)}) collective-permute-start(bf16[160,768]{1,0:T(8,128)(2,1)S(1)} %get-tuple-element.78), channel_id=1, source_target_pairs={{0,4},{1,5},{2,6},{3,7},{4,0},{5,1},{6,2},{7,3},{8,12},{9,13},{10,... | collective-permute-start | bytes 737288 | tf_op jit(solution)/shard_map/ppermute | solution.py:18
  55.2 0.7 collective-permute-start.18
  56.0 5.6 %collective-permute-done.12.refs_4_ = bf16[160,768]{1,0:T(8,128)(2,1)S(1)} collective-permute-done((bf16[160,768]{1,0:T(8,128)(2,1)S(1)}, bf16[160,768]{1,0:T(8,128)(2,1)S(1)}, u32[]{:S(2)}, u32[]{:S(2)}) %collective-permute-start.12) | collective-permute-done | bytes 245792 | tf_op jit(solution)/shard_map/ppermute | solution.py:18
  61.6 0.6 shard_map.102.refs_0_
  62.2 3.2 %collective-permute-start.14 = (bf16[320,768]{1,0:T(8,128)(2,1)S(1)}, bf16[320,768]{1,0:T(8,128)(2,1)S(1)}, u32[]{:S(2)}, u32[]{:S(2)}) collective-permute-start(bf16[320,768]{1,0:T(8,128)(2,1)S(1)} %shard_map.102.refs_0_), channel_id=1, source_target_pairs={{0,16},{8,24},{16,0},{24,8},{1,17},{9,25},{17,1},{25,9},{2,18},{10... | collective-permute-start | bytes 1474568 | tf_op jit(solution)/shard_map/ppermute | solution.py:18
  65.4 1.3 %shard_map.103 = (bf16[160,768]{1,0:T(8,128)(2,1)S(1)}, bf16[160,768]{1,0:T(8,128)(2,1)S(1)}, bf16[160,512]{1,0:T(8,128)(2,1)S(1)}, bf16[160,512]{1,0:T(8,128)(2,1)S(1)}) custom-call(bf16[320,768]{1,0:T(8,128)(2,1)S(1)} %shard_map.102.refs_0_, bf16[160,768]{1,0:T(8,128)(2,1)S(1)} %get-tuple-element.69.refs_0_.refs_1_.refs_9_, ...), custom_call_target="tpu_custom_call" | custom-call | flops 30000001024 | bytes 1 | tf_op jit(solution)/shard_map/pallas_call | solution.py:31
  66.7 1.1 %collective-permute-start.16 = (bf16[160,768]{1,0:T(8,128)(2,1)S(1)}, bf16[160,768]{1,0:T(8,128)(2,1)S(1)}, u32[]{:S(2)}, u32[]{:S(2)}) collective-permute-start(bf16[160,768]{1,0:T(8,128)(2,1)S(1)} %get-tuple-element.77), channel_id=1, source_target_pairs={{0,2},{1,3},{2,0},{3,1},{4,6},{5,7},{6,4},{7,5},{8,10},{9,11},{10,... | collective-permute-start | bytes 737288 | tf_op jit(solution)/shard_map/ppermute | solution.py:18
  67.8 0.3 collective-permute-done.17.refs_1_.refs_11_
  68.0 1.3 %shard_map.104 = (bf16[160,768]{1,0:T(8,128)(2,1)S(1)}, bf16[160,768]{1,0:T(8,128)(2,1)S(1)}, bf16[160,512]{1,0:T(8,128)(2,1)S(1)}, bf16[160,512]{1,0:T(8,128)(2,1)S(1)}) custom-call(bf16[160,768]{1,0:T(8,128)(2,1)S(1)} %get-tuple-element.76.refs_0_.refs_2_, bf16[160,768]{1,0:T(8,128)(2,1)S(1)} %collective-permute-done.17.refs_1_.refs_11_, ...), custom_call_target="tpu_custom_call" | custom-call | flops 30000001024 | bytes 1 | tf_op jit(solution)/shard_map/pallas_call | solution.py:31
  69.3 1.2 %collective-permute-start.19 = (bf16[160,768]{1,0:T(8,128)(2,1)S(1)}, bf16[160,768]{1,0:T(8,128)(2,1)S(1)}, u32[]{:S(2)}, u32[]{:S(2)}) collective-permute-start(bf16[160,768]{1,0:T(8,128)(2,1)S(1)} %get-tuple-element.82), channel_id=1, source_target_pairs={{0,4},{1,5},{2,6},{3,7},{4,0},{5,1},{6,2},{7,3},{8,12},{9,13},{10,... | collective-permute-start | bytes 737288 | tf_op jit(solution)/shard_map/ppermute | solution.py:18
  70.5 1.8 %collective-permute-start.20 = (bf16[160,768]{1,0:T(8,128)(2,1)S(1)}, bf16[160,768]{1,0:T(8,128)(2,1)S(1)}, u32[]{:S(2)}, u32[]{:S(2)}) collective-permute-start(bf16[160,768]{1,0:T(8,128)(2,1)S(1)} %get-tuple-element.83), channel_id=1, source_target_pairs={{0,6},{1,7},{2,4},{3,5},{4,2},{5,3},{6,0},{7,1},{8,14},{9,15},{10,... | collective-permute-start | bytes 737288 | tf_op jit(solution)/shard_map/ppermute | solution.py:18
  72.3 0.5 collective-permute-start.22
  72.9 2.7 %collective-permute-done.16.refs_3_ = bf16[160,768]{1,0:T(8,128)(2,1)S(1)} collective-permute-done((bf16[160,768]{1,0:T(8,128)(2,1)S(1)}, bf16[160,768]{1,0:T(8,128)(2,1)S(1)}, u32[]{:S(2)}, u32[]{:S(2)}) %collective-permute-start.16) | collective-permute-done | bytes 245792 | tf_op jit(solution)/shard_map/ppermute | solution.py:18
  75.6 1.1 %collective-permute-start.23 = (bf16[320,768]{1,0:T(8,128)(2,1)S(1)}, bf16[320,768]{1,0:T(8,128)(2,1)S(1)}, u32[]{:S(2)}, u32[]{:S(2)}) collective-permute-start(bf16[320,768]{1,0:T(8,128)(2,1)S(1)} %get-tuple-element.97), channel_id=1, source_target_pairs={{0,4},{1,5},{2,6},{3,7},{4,0},{5,1},{6,2},{7,3},{8,12},{9,13},{10,... | collective-permute-start | bytes 1474568 | tf_op jit(solution)/shard_map/ppermute | solution.py:18
  76.7 5.6 %collective-permute-done.19.refs_4_ = bf16[160,768]{1,0:T(8,128)(2,1)S(1)} collective-permute-done((bf16[160,768]{1,0:T(8,128)(2,1)S(1)}, bf16[160,768]{1,0:T(8,128)(2,1)S(1)}, u32[]{:S(2)}, u32[]{:S(2)}) %collective-permute-start.19) | collective-permute-done | bytes 245792 | tf_op jit(solution)/shard_map/ppermute | solution.py:18
  82.2 0.0 copy-start.18
  82.2 1.1 %collective-permute-start.24 = (bf16[320,768]{1,0:T(8,128)(2,1)S(1)}, bf16[320,768]{1,0:T(8,128)(2,1)S(1)}, u32[]{:S(2)}, u32[]{:S(2)}) collective-permute-start(bf16[320,768]{1,0:T(8,128)(2,1)S(1)} %get-tuple-element.98), channel_id=1, source_target_pairs={{0,6},{1,7},{2,4},{3,5},{4,2},{5,3},{6,0},{7,1},{8,14},{9,15},{10,... | collective-permute-start | bytes 1474568 | tf_op jit(solution)/shard_map/ppermute | solution.py:18
  83.3 0.6 shard_map.105.refs_0_
  84.0 2.3 %collective-permute-start.25 = (bf16[320,768]{1,0:T(8,128)(2,1)S(1)}, bf16[320,768]{1,0:T(8,128)(2,1)S(1)}, u32[]{:S(2)}, u32[]{:S(2)}) collective-permute-start(bf16[320,768]{1,0:T(8,128)(2,1)S(1)} %shard_map.105.refs_0_), channel_id=1, source_target_pairs={{0,16},{8,24},{16,0},{24,8},{1,17},{9,25},{17,1},{25,9},{2,18},{10... | collective-permute-start | bytes 1474568 | tf_op jit(solution)/shard_map/ppermute | solution.py:18
  86.3 2.8 %shard_map.106.refs_0_ = bf16[3072,256]{1,0:T(8,128)(2,1)} custom-call(bf16[320,768]{1,0:T(8,128)(2,1)S(1)} %shard_map.105.refs_0_, bf16[320,768]{1,0:T(8,128)(2,1)S(1)} %get-tuple-element.59.refs_1_, bf16[320,768]{1,0:T(8,128)(2,1)S(1)} %copy-done.10, bf16[320,768]{1,0:T(8,128)(2,1)S(1)} %collective-permute-done.5.refs_3_, ...), custom_call_target="tpu_custom_call" | custom-call | flops 30000001024 | bytes 1 | tf_op jit(solution)/shard_map/pallas_call | solution.py:31
  89.1 3.1 %shard_map.107.refs_0_ = f32[3072,256]{1,0:T(8,128)} custom-call(bf16[3072,256]{1,0:T(8,128)(2,1)} %shard_map.106.refs_0_, bf16[320,768]{1,0:T(8,128)(2,1)S(1)} %get-tuple-element.59.refs_1_, bf16[320,768]{1,0:T(8,128)(2,1)S(1)} %copy-done.10, bf16[320,768]{1,0:T(8,128)(2,1)S(1)} %collective-permute-done.5.refs_3_, ...), custom_call_target="tpu_custom_call" | custom-call | flops 30000001024 | bytes 1 | tf_op jit(solution)/shard_map/pallas_call | solution.py:31
  92.2 0.5 collective-permute-done.21.refs_1_
  92.8 1.9 %copy-done.19 = f32[3072,256]{1,0:T(8,128)S(1)} copy-done((f32[3072,256]{1,0:T(8,128)S(1)}, f32[3072,256]{1,0:T(8,128)}, u32[]{:S(2)}) %copy-start.19) | copy-done | bytes 3145752
  94.6 1.3 %shard_map.108 = (bf16[768,512]{1,0:T(8,128)(2,1)}, bf16[512,768]{1,0:T(8,128)(2,1)}) custom-call(f32[3072,256]{1,0:T(8,128)S(1)} %copy-done.19, bf16[3072,256]{1,0:T(8,128)(2,1)S(1)} %collective-permute-done.21.refs_1_), custom_call_target="tpu_custom_call" | custom-call | flops 30000001024 | bytes 1 | tf_op jit(solution)/shard_map/pallas_call | solution.py:31
  96.0 3.8 %collective-permute-done.23.refs_4_ = bf16[320,768]{1,0:T(8,128)(2,1)S(1)} collective-permute-done((bf16[320,768]{1,0:T(8,128)(2,1)S(1)}, bf16[320,768]{1,0:T(8,128)(2,1)S(1)}, u32[]{:S(2)}, u32[]{:S(2)}) %collective-permute-start.23) | collective-permute-done | bytes 491552 | tf_op jit(solution)/shard_map/ppermute | solution.py:18
  99.8 1.1 %shard_map.109 = (bf16[320,768]{1,0:T(8,128)(2,1)S(1)}, bf16[320,768]{1,0:T(8,128)(2,1)S(1)}) custom-call(bf16[768,512]{1,0:T(8,128)(2,1)} %get-tuple-element.95.refs_0_, s32[1,320]{1,0:T(1,128)S(1)} %copy-done.2, bf16[320,768]{1,0:T(8,128)(2,1)S(1)} %copy-done.21, bf16[320,768]{1,0:T(8,128)(2,1)S(1)} %collective-permute-done.22.refs_3_, ...), custom_call_target="tpu_custom_call" | custom-call | flops 30000001024 | bytes 1 | tf_op jit(solution)/shard_map/pallas_call | solution.py:31
  100.9 0.1 collective-permute-done.25.other_ref
  101.0 1.0 shard_map.110
  (54 shorter events, 0.1 us)
Async XLA Ops:
  0.6 7.3 %collective-permute-start.1 = (bf16[768,512]{1,0:T(8,128)(2,1)}, bf16[768,512]{1,0:T(8,128)(2,1)S(1)}, u32[]{:S(2)}, u32[]{:S(2)}) collective-permute-start(bf16[768,512]{1,0:T(8,128)(2,1)} %bitcast.6), channel_id=1, source_target_pairs={{0,1},{1,0},{2,3},{3,2},{4,5},{5,4},{6,7},{7,6},{8,9},{9,8},{10,11... | collective-permute-start | bytes 2359304 | tf_op jit(solution)/shard_map/ppermute | solution.py:18
  1.1 6.8 %collective-permute-start.2 = (bf16[512,768]{1,0:T(8,128)(2,1)}, bf16[512,768]{1,0:T(8,128)(2,1)S(1)}, u32[]{:S(2)}, u32[]{:S(2)}) collective-permute-start(bf16[512,768]{1,0:T(8,128)(2,1)} %bitcast.12), channel_id=1, source_target_pairs={{0,1},{1,0},{2,3},{3,2},{4,5},{5,4},{6,7},{7,6},{8,9},{9,8},{10,11... | collective-permute-start | bytes 2359304 | tf_op jit(solution)/shard_map/ppermute | solution.py:18
  1.2 26.3 %collective-permute-start = (bf16[320,768]{1,0:T(8,128)(2,1)}, bf16[320,768]{1,0:T(8,128)(2,1)S(1)}, u32[]{:S(2)}, u32[]{:S(2)}) collective-permute-start(bf16[320,768]{1,0:T(8,128)(2,1)} %token_ref.1), channel_id=1, source_target_pairs={{0,16},{8,24},{16,0},{24,8},{1,17},{9,25},{17,1},{25,9},{2,18},{10... | collective-permute-start | bytes 1474568 | tf_op jit(solution)/shard_map/ppermute | solution.py:18
  6.7 1.2 %copy-start.1 = (s32[1,320]{1,0:T(1,128)}, s32[1,320]{1,0:T(1,128)S(1)}, u32[]{:S(2)}) copy-start(s32[1,320]{1,0:T(1,128)S(1)} %get-tuple-element.54.refs_0_.refs_1_) | copy-start | bytes 3844
  7.9 0.9 copy-start.5
  8.0 1.1 %copy-start.7 = (bf16[512,768]{1,0:T(8,128)(2,1)}, bf16[512,768]{1,0:T(8,128)(2,1)S(1)}, u32[]{:S(2)}) copy-start(bf16[512,768]{1,0:T(8,128)(2,1)S(1)} %collective-permute-done.2.refs_1_.refs_8_.refs_6_) | copy-start | bytes 2359300
  9.1 18.5 %collective-permute-start.3 = (s32[1,320]{1,0:T(1,128)S(1)}, s32[1,320]{1,0:T(1,128)S(1)}, u32[]{:S(2)}, u32[]{:S(2)}) collective-permute-start(s32[1,320]{1,0:T(1,128)S(1)} %shard_map.95), channel_id=1, source_target_pairs={{0,16},{8,24},{16,0},{24,8},{1,17},{9,25},{17,1},{25,9},{2,18},{10... | collective-permute-start | bytes 3848 | tf_op jit(solution)/shard_map/ppermute | solution.py:18
  9.2 20.7 %collective-permute-start.4 = (bf16[320,768]{1,0:T(8,128)(2,1)S(1)}, bf16[320,768]{1,0:T(8,128)(2,1)S(1)}, u32[]{:S(2)}, u32[]{:S(2)}) collective-permute-start(bf16[320,768]{1,0:T(8,128)(2,1)S(1)} %get-tuple-element.60), channel_id=1, source_target_pairs={{0,2},{1,3},{2,0},{3,1},{4,6},{5,7},{6,4},{7,5},{8,10},{9,11},{10,... | collective-permute-start | bytes 1474568 | tf_op jit(solution)/shard_map/ppermute | solution.py:18
  10.9 23.2 %collective-permute-start.5 = (bf16[320,768]{1,0:T(8,128)(2,1)S(1)}, bf16[320,768]{1,0:T(8,128)(2,1)S(1)}, u32[]{:S(2)}, u32[]{:S(2)}) collective-permute-start(bf16[320,768]{1,0:T(8,128)(2,1)S(1)} %get-tuple-element.61), channel_id=1, source_target_pairs={{0,4},{1,5},{2,6},{3,7},{4,0},{5,1},{6,2},{7,3},{8,12},{9,13},{10,... | collective-permute-start | bytes 1474568 | tf_op jit(solution)/shard_map/ppermute | solution.py:18
  12.4 22.7 %collective-permute-start.6 = (bf16[320,768]{1,0:T(8,128)(2,1)S(1)}, bf16[320,768]{1,0:T(8,128)(2,1)S(1)}, u32[]{:S(2)}, u32[]{:S(2)}) collective-permute-start(bf16[320,768]{1,0:T(8,128)(2,1)S(1)} %get-tuple-element.62), channel_id=1, source_target_pairs={{0,6},{1,7},{2,4},{3,5},{4,2},{5,3},{6,0},{7,1},{8,14},{9,15},{10,... | collective-permute-start | bytes 1474568 | tf_op jit(solution)/shard_map/ppermute | solution.py:18
  27.6 24.2 %collective-permute-start.10 = (bf16[320,768]{1,0:T(8,128)(2,1)S(1)}, bf16[320,768]{1,0:T(8,128)(2,1)S(1)}, u32[]{:S(2)}, u32[]{:S(2)}) collective-permute-start(bf16[320,768]{1,0:T(8,128)(2,1)S(1)} %shard_map.96.refs_0_), channel_id=1, source_target_pairs={{0,16},{8,24},{16,0},{24,8},{1,17},{9,25},{17,1},{25,9},{2,18},{10... | collective-permute-start | bytes 1474568 | tf_op jit(solution)/shard_map/ppermute | solution.py:18
  28.3 11.5 %copy-start.11 = (bf16[160,768]{1,0:T(8,128)(2,1)}, bf16[160,768]{1,0:T(8,128)(2,1)S(1)}, u32[]{:S(2)}) copy-start(bf16[160,768]{1,0:T(8,128)(2,1)S(1)} %get-tuple-element.58.refs_0_.refs_1_.refs_5_) | copy-start | bytes 737284
  28.3 11.5 %collective-permute-start.7 = (bf16[160,768]{1,0:T(8,128)(2,1)S(1)}, bf16[160,768]{1,0:T(8,128)(2,1)S(1)}, u32[]{:S(2)}, u32[]{:S(2)}) collective-permute-start(bf16[160,768]{1,0:T(8,128)(2,1)S(1)} %get-tuple-element.64), channel_id=1, source_target_pairs={{0,2},{1,3},{2,0},{3,1},{4,6},{5,7},{6,4},{7,5},{8,10},{9,11},{10,... | collective-permute-start | bytes 737288 | tf_op jit(solution)/shard_map/ppermute | solution.py:18
  30.0 9.8 %copy-start.9 = (bf16[320,768]{1,0:T(8,128)(2,1)}, bf16[320,768]{1,0:T(8,128)(2,1)S(1)}, u32[]{:S(2)}) copy-start(bf16[320,768]{1,0:T(8,128)(2,1)S(1)} %collective-permute-done.4.refs_2_) | copy-start | bytes 1474564
  30.0 14.2 %collective-permute-start.8 = (bf16[160,768]{1,0:T(8,128)(2,1)S(1)}, bf16[160,768]{1,0:T(8,128)(2,1)S(1)}, u32[]{:S(2)}, u32[]{:S(2)}) collective-permute-start(bf16[160,768]{1,0:T(8,128)(2,1)S(1)} %get-tuple-element.66), channel_id=1, source_target_pairs={{0,4},{1,5},{2,6},{3,7},{4,0},{5,1},{6,2},{7,3},{8,12},{9,13},{10,... | collective-permute-start | bytes 737288 | tf_op jit(solution)/shard_map/ppermute | solution.py:18
  34.1 11.6 %collective-permute-start.9 = (bf16[160,768]{1,0:T(8,128)(2,1)S(1)}, bf16[160,768]{1,0:T(8,128)(2,1)S(1)}, u32[]{:S(2)}, u32[]{:S(2)}) collective-permute-start(bf16[160,768]{1,0:T(8,128)(2,1)S(1)} %get-tuple-element.67), channel_id=1, source_target_pairs={{0,6},{1,7},{2,4},{3,5},{4,2},{5,3},{6,0},{7,1},{8,14},{9,15},{10,... | collective-permute-start | bytes 737288 | tf_op jit(solution)/shard_map/ppermute | solution.py:18
  35.1 4.8 %copy-start.3 = (bf16[1,768,512]{2,1,0:T(8,128)(2,1)S(1)}, bf16[1,768,512]{2,1,0:T(8,128)(2,1)}, u32[]{:S(2)}) copy-start(bf16[1,768,512]{2,1,0:T(8,128)(2,1)} %param.9) | copy-start | bytes 2359300
  35.1 4.8 %copy-start.4 = (bf16[1,512,768]{2,1,0:T(8,128)(2,1)S(1)}, bf16[1,512,768]{2,1,0:T(8,128)(2,1)}, u32[]{:S(2)}) copy-start(bf16[1,512,768]{2,1,0:T(8,128)(2,1)} %param.10) | copy-start | bytes 2359300
  35.1 4.8 %copy-start.6 = (bf16[768,512]{1,0:T(8,128)(2,1)S(1)}, bf16[768,512]{1,0:T(8,128)(2,1)}, u32[]{:S(2)}) copy-start(bf16[768,512]{1,0:T(8,128)(2,1)} %copy-done.5) | copy-start | bytes 2359300
  35.1 4.8 %copy-start.8 = (bf16[512,768]{1,0:T(8,128)(2,1)S(1)}, bf16[512,768]{1,0:T(8,128)(2,1)}, u32[]{:S(2)}) copy-start(bf16[512,768]{1,0:T(8,128)(2,1)} %copy-done.7) | copy-start | bytes 2359300
  39.8 1.3 %copy-start.20 = (bf16[320,768]{1,0:T(8,128)(2,1)}, bf16[320,768]{1,0:T(8,128)(2,1)S(1)}, u32[]{:S(2)}) copy-start(bf16[320,768]{1,0:T(8,128)(2,1)S(1)} %get-tuple-element.63.refs_0_.refs_2_) | copy-start | bytes 1474564
  39.8 1.2 %copy-start.13 = (bf16[160,768]{1,0:T(8,128)(2,1)}, bf16[160,768]{1,0:T(8,128)(2,1)S(1)}, u32[]{:S(2)}) copy-start(bf16[160,768]{1,0:T(8,128)(2,1)S(1)} %collective-permute-done.7.refs_2_.refs_6_) | copy-start | bytes 737284
  41.1 14.1 %collective-permute-start.11 = (bf16[160,768]{1,0:T(8,128)(2,1)S(1)}, bf16[160,768]{1,0:T(8,128)(2,1)S(1)}, u32[]{:S(2)}, u32[]{:S(2)}) collective-permute-start(bf16[160,768]{1,0:T(8,128)(2,1)S(1)} %get-tuple-element.70), channel_id=1, source_target_pairs={{0,2},{1,3},{2,0},{3,1},{4,6},{5,7},{6,4},{7,5},{8,10},{9,11},{10,... | collective-permute-start | bytes 737288 | tf_op jit(solution)/shard_map/ppermute | solution.py:18
  44.1 2.7 %copy-start.15 = (bf16[160,768]{1,0:T(8,128)(2,1)}, bf16[160,768]{1,0:T(8,128)(2,1)S(1)}, u32[]{:S(2)}) copy-start(bf16[160,768]{1,0:T(8,128)(2,1)S(1)} %collective-permute-done.8.refs_1_.refs_7_) | copy-start | bytes 737284
  45.7 1.2 %copy-start.17 = (bf16[160,768]{1,0:T(8,128)(2,1)}, bf16[160,768]{1,0:T(8,128)(2,1)S(1)}, u32[]{:S(2)}) copy-start(bf16[160,768]{1,0:T(8,128)(2,1)S(1)} %collective-permute-done.9.refs_2_.refs_8_) | copy-start | bytes 737284
  46.9 5.5 %copy-start.22 = (bf16[160,512]{1,0:T(8,128)(2,1)}, bf16[160,512]{1,0:T(8,128)(2,1)S(1)}, u32[]{:S(2)}) copy-start(bf16[160,512]{1,0:T(8,128)(2,1)S(1)} %get-tuple-element.68.refs_0_.refs_15_) | copy-start | bytes 491524
  46.9 14.7 %collective-permute-start.12 = (bf16[160,768]{1,0:T(8,128)(2,1)S(1)}, bf16[160,768]{1,0:T(8,128)(2,1)S(1)}, u32[]{:S(2)}, u32[]{:S(2)}) collective-permute-start(bf16[160,768]{1,0:T(8,128)(2,1)S(1)} %get-tuple-element.71), channel_id=1, source_target_pairs={{0,4},{1,5},{2,6},{3,7},{4,0},{5,1},{6,2},{7,3},{8,12},{9,13},{10,... | collective-permute-start | bytes 737288 | tf_op jit(solution)/shard_map/ppermute | solution.py:18
  47.7 13.9 %collective-permute-start.13 = (bf16[160,768]{1,0:T(8,128)(2,1)S(1)}, bf16[160,768]{1,0:T(8,128)(2,1)S(1)}, u32[]{:S(2)}, u32[]{:S(2)}) collective-permute-start(bf16[160,768]{1,0:T(8,128)(2,1)S(1)} %get-tuple-element.72), channel_id=1, source_target_pairs={{0,6},{1,7},{2,4},{3,5},{4,2},{5,3},{6,0},{7,1},{8,14},{9,15},{10,... | collective-permute-start | bytes 737288 | tf_op jit(solution)/shard_map/ppermute | solution.py:18
  52.4 13.0 %collective-permute-start.15 = (bf16[160,768]{1,0:T(8,128)(2,1)S(1)}, bf16[160,768]{1,0:T(8,128)(2,1)S(1)}, u32[]{:S(2)}, u32[]{:S(2)}) collective-permute-start(bf16[160,768]{1,0:T(8,128)(2,1)S(1)} %get-tuple-element.73), channel_id=1, source_target_pairs={{0,2},{1,3},{2,0},{3,1},{4,6},{5,7},{6,4},{7,5},{8,10},{9,11},{10,... | collective-permute-start | bytes 737288 | tf_op jit(solution)/shard_map/ppermute | solution.py:18
  53.7 14.3 %collective-permute-start.17 = (bf16[160,768]{1,0:T(8,128)(2,1)S(1)}, bf16[160,768]{1,0:T(8,128)(2,1)S(1)}, u32[]{:S(2)}, u32[]{:S(2)}) collective-permute-start(bf16[160,768]{1,0:T(8,128)(2,1)S(1)} %get-tuple-element.78), channel_id=1, source_target_pairs={{0,4},{1,5},{2,6},{3,7},{4,0},{5,1},{6,2},{7,3},{8,12},{9,13},{10,... | collective-permute-start | bytes 737288 | tf_op jit(solution)/shard_map/ppermute | solution.py:18
  55.2 12.8 %collective-permute-start.18 = (bf16[160,768]{1,0:T(8,128)(2,1)S(1)}, bf16[160,768]{1,0:T(8,128)(2,1)S(1)}, u32[]{:S(2)}, u32[]{:S(2)}) collective-permute-start(bf16[160,768]{1,0:T(8,128)(2,1)S(1)} %get-tuple-element.79), channel_id=1, source_target_pairs={{0,6},{1,7},{2,4},{3,5},{4,2},{5,3},{6,0},{7,1},{8,14},{9,15},{10,... | collective-permute-start | bytes 737288 | tf_op jit(solution)/shard_map/ppermute | solution.py:18
  62.2 21.1 %collective-permute-start.14 = (bf16[320,768]{1,0:T(8,128)(2,1)S(1)}, bf16[320,768]{1,0:T(8,128)(2,1)S(1)}, u32[]{:S(2)}, u32[]{:S(2)}) collective-permute-start(bf16[320,768]{1,0:T(8,128)(2,1)S(1)} %shard_map.102.refs_0_), channel_id=1, source_target_pairs={{0,16},{8,24},{16,0},{24,8},{1,17},{9,25},{17,1},{25,9},{2,18},{10... | collective-permute-start | bytes 1474568 | tf_op jit(solution)/shard_map/ppermute | solution.py:18
  66.7 8.9 %collective-permute-start.16 = (bf16[160,768]{1,0:T(8,128)(2,1)S(1)}, bf16[160,768]{1,0:T(8,128)(2,1)S(1)}, u32[]{:S(2)}, u32[]{:S(2)}) collective-permute-start(bf16[160,768]{1,0:T(8,128)(2,1)S(1)} %get-tuple-element.77), channel_id=1, source_target_pairs={{0,2},{1,3},{2,0},{3,1},{4,6},{5,7},{6,4},{7,5},{8,10},{9,11},{10,... | collective-permute-start | bytes 737288 | tf_op jit(solution)/shard_map/ppermute | solution.py:18
  69.3 12.9 %collective-permute-start.19 = (bf16[160,768]{1,0:T(8,128)(2,1)S(1)}, bf16[160,768]{1,0:T(8,128)(2,1)S(1)}, u32[]{:S(2)}, u32[]{:S(2)}) collective-permute-start(bf16[160,768]{1,0:T(8,128)(2,1)S(1)} %get-tuple-element.82), channel_id=1, source_target_pairs={{0,4},{1,5},{2,6},{3,7},{4,0},{5,1},{6,2},{7,3},{8,12},{9,13},{10,... | collective-permute-start | bytes 737288 | tf_op jit(solution)/shard_map/ppermute | solution.py:18
  70.5 12.8 %collective-permute-start.20 = (bf16[160,768]{1,0:T(8,128)(2,1)S(1)}, bf16[160,768]{1,0:T(8,128)(2,1)S(1)}, u32[]{:S(2)}, u32[]{:S(2)}) collective-permute-start(bf16[160,768]{1,0:T(8,128)(2,1)S(1)} %get-tuple-element.83), channel_id=1, source_target_pairs={{0,6},{1,7},{2,4},{3,5},{4,2},{5,3},{6,0},{7,1},{8,14},{9,15},{10,... | collective-permute-start | bytes 737288 | tf_op jit(solution)/shard_map/ppermute | solution.py:18
  72.3 23.6 %collective-permute-start.22 = (bf16[320,768]{1,0:T(8,128)(2,1)S(1)}, bf16[320,768]{1,0:T(8,128)(2,1)S(1)}, u32[]{:S(2)}, u32[]{:S(2)}) collective-permute-start(bf16[320,768]{1,0:T(8,128)(2,1)S(1)} %get-tuple-element.96), channel_id=1, source_target_pairs={{0,2},{1,3},{2,0},{3,1},{4,6},{5,7},{6,4},{7,5},{8,10},{9,11},{10,... | collective-permute-start | bytes 1474568 | tf_op jit(solution)/shard_map/ppermute | solution.py:18
  75.6 24.2 %collective-permute-start.23 = (bf16[320,768]{1,0:T(8,128)(2,1)S(1)}, bf16[320,768]{1,0:T(8,128)(2,1)S(1)}, u32[]{:S(2)}, u32[]{:S(2)}) collective-permute-start(bf16[320,768]{1,0:T(8,128)(2,1)S(1)} %get-tuple-element.97), channel_id=1, source_target_pairs={{0,4},{1,5},{2,6},{3,7},{4,0},{5,1},{6,2},{7,3},{8,12},{9,13},{10,... | collective-permute-start | bytes 1474568 | tf_op jit(solution)/shard_map/ppermute | solution.py:18
  82.2 4.1 %copy-start.10 = (bf16[320,768]{1,0:T(8,128)(2,1)S(1)}, bf16[320,768]{1,0:T(8,128)(2,1)}, u32[]{:S(2)}) copy-start(bf16[320,768]{1,0:T(8,128)(2,1)} %copy-done.9) | copy-start | bytes 1474564
  82.2 4.1 %copy-start.12 = (bf16[160,768]{1,0:T(8,128)(2,1)S(1)}, bf16[160,768]{1,0:T(8,128)(2,1)}, u32[]{:S(2)}) copy-start(bf16[160,768]{1,0:T(8,128)(2,1)} %copy-done.11) | copy-start | bytes 737284
  82.2 4.1 %copy-start.14 = (bf16[160,768]{1,0:T(8,128)(2,1)S(1)}, bf16[160,768]{1,0:T(8,128)(2,1)}, u32[]{:S(2)}) copy-start(bf16[160,768]{1,0:T(8,128)(2,1)} %copy-done.13) | copy-start | bytes 737284
  82.2 4.1 %copy-start.16 = (bf16[160,768]{1,0:T(8,128)(2,1)S(1)}, bf16[160,768]{1,0:T(8,128)(2,1)}, u32[]{:S(2)}) copy-start(bf16[160,768]{1,0:T(8,128)(2,1)} %copy-done.15) | copy-start | bytes 737284
  82.2 4.1 %copy-start.18 = (bf16[160,768]{1,0:T(8,128)(2,1)S(1)}, bf16[160,768]{1,0:T(8,128)(2,1)}, u32[]{:S(2)}) copy-start(bf16[160,768]{1,0:T(8,128)(2,1)} %copy-done.17) | copy-start | bytes 737284
  82.2 17.6 %collective-permute-start.24 = (bf16[320,768]{1,0:T(8,128)(2,1)S(1)}, bf16[320,768]{1,0:T(8,128)(2,1)S(1)}, u32[]{:S(2)}, u32[]{:S(2)}) collective-permute-start(bf16[320,768]{1,0:T(8,128)(2,1)S(1)} %get-tuple-element.98), channel_id=1, source_target_pairs={{0,6},{1,7},{2,4},{3,5},{4,2},{5,3},{6,0},{7,1},{8,14},{9,15},{10,... | collective-permute-start | bytes 1474568 | tf_op jit(solution)/shard_map/ppermute | solution.py:18
  84.0 17.0 %collective-permute-start.25 = (bf16[320,768]{1,0:T(8,128)(2,1)S(1)}, bf16[320,768]{1,0:T(8,128)(2,1)S(1)}, u32[]{:S(2)}, u32[]{:S(2)}) collective-permute-start(bf16[320,768]{1,0:T(8,128)(2,1)S(1)} %shard_map.105.refs_0_), channel_id=1, source_target_pairs={{0,16},{8,24},{16,0},{24,8},{1,17},{9,25},{17,1},{25,9},{2,18},{10... | collective-permute-start | bytes 1474568 | tf_op jit(solution)/shard_map/ppermute | solution.py:18
  86.3 2.8 %copy-start.23 = (bf16[160,512]{1,0:T(8,128)(2,1)S(1)}, bf16[160,512]{1,0:T(8,128)(2,1)}, u32[]{:S(2)}) copy-start(bf16[160,512]{1,0:T(8,128)(2,1)} %copy-done.22) | copy-start | bytes 491524
  89.1 3.6 %collective-permute-start.21 = (bf16[3072,256]{1,0:T(8,128)(2,1)}, bf16[3072,256]{1,0:T(8,128)(2,1)S(1)}, u32[]{:S(2)}, u32[]{:S(2)}) collective-permute-start(bf16[3072,256]{1,0:T(8,128)(2,1)} %shard_map.106.refs_0_), channel_id=1, source_target_pairs={{0,1},{1,0},{2,3},{3,2},{4,5},{5,4},{6,7},{7,6},{8,9},{9,8},{10,11... | collective-permute-start | bytes 4718600 | tf_op jit(solution)/shard_map/ppermute | solution.py:18
  92.2 7.6 %copy-start = (f32[320]{0:T(512)S(1)}, f32[320]{0:T(512)}, u32[]{:S(2)}) copy-start(f32[320]{0:T(512)} %refs_7_.1) | copy-start | bytes 3844
  92.2 7.6 %copy-start.2 = (s32[1,320]{1,0:T(1,128)S(1)}, s32[1,320]{1,0:T(1,128)}, u32[]{:S(2)}) copy-start(s32[1,320]{1,0:T(1,128)} %copy-done.1) | copy-start | bytes 3844
  92.8 1.9 %copy-start.19 = (f32[3072,256]{1,0:T(8,128)S(1)}, f32[3072,256]{1,0:T(8,128)}, u32[]{:S(2)}) copy-start(f32[3072,256]{1,0:T(8,128)} %shard_map.107.refs_0_) | copy-start | bytes 9437188
  94.6 5.2 %copy-start.21 = (bf16[320,768]{1,0:T(8,128)(2,1)S(1)}, bf16[320,768]{1,0:T(8,128)(2,1)}, u32[]{:S(2)}) copy-start(bf16[320,768]{1,0:T(8,128)(2,1)} %copy-done.20) | copy-start | bytes 1474564
